TPU v7x, 512 devices: a whole 4x8x8 slice. The times are simulated.
512 devices in a mesh: seq: 8 (over y_hi, x), expert: 64 (over z, y_lo, core).
Axes of the slice: x: 4, y: 8 (y_hi: 2, y_lo: 4; y = y_hi * 4 + y_lo), z: 8, core: 2. Of those that a mesh axis runs over, the one named last changes fastest.
Arguments:
- hidden_in: bfloat16 [3072, 4096], P('seq', 'expert'), may hold values from -6 to 6
- queries: bfloat16 [3072, 8192], P('seq', 'expert'), may hold values from -150 to 150
- frame_keys: bfloat16 [24, 201, 1024], P('seq'), may hold values from -6 to 6
- frame_values: bfloat16 [24, 201, 1024], P('seq'), may hold values from -6 to 6
- cited_frame: int32 [3072], P('seq'), may hold values from 0 to 23, as said below
- frame_slot: int32 [24], replicated, may hold values from 0 to 23, as said below
- attn_gate: float32 [4096], P('expert'), may hold values from 0.3 to 2
- out_weight: bfloat16 [8192, 4096], P(None, 'expert'), may hold values from -0.0625 to 0.0625
- mlp_gain: float32 [4096], replicated, may hold values from 0.1 to 1.9
- expert_ids: int32 [3072, 2], P('seq'), may hold values from 0 to 63, all different within a row; in each aligned block of 384 rows (0 to 383, 384 to 767, ...) at most 36 rows name the same one
- gate_fixed: int32 [3072, 2], P('seq'), may hold values from 6554 to 65535
- w_in: bfloat16 [64, 4096, 2, 1024], P('expert', None, None, 'seq'), may hold values from -0.09375 to 0.09375
- w_down: bfloat16 [64, 1024, 4096], P('expert', 'seq'), may hold values from -0.1875 to 0.1875
Outputs:
- hidden_out: bfloat16 [3072, 4096], P('seq', 'expert')
Inputs may be any that keep to these rules, and one draw needn't show every extreme that they name: `cited_frame`: any token may cite any frame. `frame_slot`: A permutation of the frame ids. `expert_ids`: the two experts of a token differ; among the 384 tokens of one seq shard no expert is named more than 36 times.
All inputs are finite; a program needn't handle non-finite values.
Results may differ from a plain program's by a relative error of at most 0.015.
Values may be sent and summed in bfloat16 or wider, within the bound.
No kernel may reach another device: no remote copies, remote signals or barrier semaphores. Data moves between devices by JAX's collectives and lax.ppermute only.
A program may use at most 64 MiB of HBM per device.

v0:
```python
import math

import jax
import jax.numpy as jnp
from jax import lax
from jax.sharding import PartitionSpec as P

KVH = 8


FIXED_SCALE = 1.0 / 65536.0
NORM_EPSILON = 1e-05
MASKED_SCORE = -1e30


def rms_normed(rows, gain):
    wide = rows.astype(jnp.float32)
    mean_square = jnp.mean(wide * wide, axis=1, keepdims=True)
    return (wide * lax.rsqrt(mean_square + NORM_EPSILON) * gain).astype(jnp.bfloat16)


def route_tables(expert_ids, gate_fixed, experts, capacity):
    token_count, top_count = expert_ids.shape
    flat_ids = expert_ids.reshape(-1)
    assigned = flat_ids.shape[0]
    expert_cols = lax.broadcasted_iota(jnp.int32, (assigned, experts), 1)
    matches = (flat_ids[:, None] == expert_cols).astype(jnp.int32)
    rank_of = jnp.sum(jnp.cumsum(matches, axis=0) * matches, axis=1) - 1
    slot_of = flat_ids * capacity + rank_of
    slot_cols = lax.broadcasted_iota(jnp.int32, (assigned, experts * capacity), 1)
    selectors = (
        (slot_of[:, None] == slot_cols)
        .astype(jnp.bfloat16)
        .reshape(token_count, top_count, experts * capacity)
    )
    select_rows = jnp.sum(selectors.astype(jnp.float32), axis=1).astype(jnp.bfloat16)
    weights = gate_fixed.astype(jnp.float32) * FIXED_SCALE
    return (select_rows, selectors, weights)


def per_device(
    hidden_in,
    queries,
    frame_keys,
    frame_values,
    cited_frame,
    frame_slot,
    attn_gate,
    out_weight,
    mlp_gain,
    expert_ids,
    gate_fixed,
    w_in,
    w_down,
):
    head_count = lax.axis_size("expert")
    head_index = lax.axis_index("expert")
    group_size = head_count // KVH
    kv_head = head_index // group_size
    frame_rows = frame_keys.shape[1]
    head_size = queries.shape[1]
    token_count = queries.shape[0]
    key_slice = lax.dynamic_slice_in_dim(frame_keys, kv_head * head_size, head_size, 2)
    value_slice = lax.dynamic_slice_in_dim(frame_values, kv_head * head_size, head_size, 2)
    frame_cols = lax.broadcasted_iota(jnp.int32, (token_count, frame_slot.shape[0]), 1)
    token_slot = jnp.sum(
        jnp.where(cited_frame[:, None] == frame_cols, frame_slot[None, :], 0), axis=1
    )
    score_scale = 1.0 / math.sqrt(head_size)
    key_block = lax.all_gather(key_slice, "seq", axis=0, tiled=True)
    value_block = lax.all_gather(value_slice, "seq", axis=0, tiled=True)
    width = key_block.shape[0] * frame_rows
    flat_keys = key_block.reshape(width, head_size)
    flat_values = value_block.reshape(width, head_size)
    scores = (
        lax.dot_general(
            queries, flat_keys, (((1,), (1,)), ((), ())), preferred_element_type=jnp.float32
        )
        * score_scale
    )
    column_frame = lax.broadcasted_iota(jnp.int32, (1, width), 1) // frame_rows
    inside = column_frame == token_slot[:, None]
    scores = jnp.where(inside, scores, MASKED_SCORE)
    row_max = jnp.max(scores, axis=1, keepdims=True)
    expon = jnp.exp(scores - row_max)
    row_total = jnp.sum(expon, axis=1, keepdims=True)
    probability = (expon / row_total).astype(jnp.bfloat16)
    mixed = jnp.dot(probability, flat_values, preferred_element_type=jnp.float32)
    present = jnp.any(inside, axis=1, keepdims=True)
    attended = jnp.where(present, mixed, 0.0).astype(jnp.bfloat16)
    projected = jnp.dot(
        lax.all_gather(attended, "expert", axis=1, tiled=True),
        out_weight,
        preferred_element_type=jnp.float32,
    )
    mid = (hidden_in.astype(jnp.float32) + jnp.tanh(attn_gate)[None, :] * projected).astype(
        jnp.bfloat16
    )
    capacity = 6 * token_count // head_count
    select_rows, selectors, weights = route_tables(expert_ids, gate_fixed, head_count, capacity)
    gathered = lax.all_gather(mid, "expert", axis=1, tiled=True)
    normed = rms_normed(gathered, mlp_gain)
    own_cols = lax.dynamic_slice_in_dim(select_rows, head_index * capacity, capacity, 1)
    dispatched = lax.dot_general(
        own_cols, normed, (((0,), (0,)), ((), ())), preferred_element_type=jnp.float32
    ).astype(jnp.bfloat16)
    hidden_units = w_in.shape[3]
    expert_in = w_in[0].reshape(w_in.shape[1], 2 * hidden_units)
    gate_up = jnp.dot(
        lax.all_gather(dispatched, "seq", axis=0, tiled=True),
        expert_in,
        preferred_element_type=jnp.float32,
    )
    activated = (jax.nn.silu(gate_up[:, :hidden_units]) * gate_up[:, hidden_units:]).astype(
        jnp.bfloat16
    )
    summed = lax.psum_scatter(
        jnp.dot(activated, w_down[0], preferred_element_type=jnp.float32).astype(jnp.bfloat16),
        "seq",
        scatter_dimension=0,
        tiled=True,
    )
    came_back = lax.all_to_all(summed, "expert", split_axis=1, concat_axis=0, tiled=True)
    picked = jnp.einsum("tks,sf->tkf", selectors, came_back, preferred_element_type=jnp.float32)
    mixed_out = jnp.sum(picked * weights[:, :, None], axis=1)
    return (mid.astype(jnp.float32) + mixed_out).astype(jnp.bfloat16)


def solution(mesh):
    return jax.shard_map(
        per_device,
        mesh=mesh,
        in_specs=(
            P("seq", "expert"),
            P("seq", "expert"),
            P("seq", None, None),
            P("seq", None, None),
            P("seq"),
            P(),
            P("expert"),
            P(None, "expert"),
            P(),
            P("seq", None),
            P("seq", None),
            P("expert", None, None, "seq"),
            P("expert", "seq", None),
        ),
        out_specs=P("seq", "expert"),
        check_vma=False,
    )
```

profile of v0, /device:TPU:1, one launch (start us, length us, event | category | flops | bytes accessed | tf_op | source)
XLA Modules:
  0.0 619.4 jit_solution(13729635019712938098)
XLA Ops:
  6.5 1.3 copy-done
  7.8 0.7 constant_dynamic-slice_fusion.2
  8.6 1.6 constant_dynamic-slice_fusion.1
  10.3 0.8 select_reduce_fusion
  11.1 2.2 compare_reduce_fusion
  13.3 70.1 %all-gather.7.cloned.1.call-done = bf16[24,201,128]{2,1,0:T(8,128)(2,1)} async-done(((bf16[3,201,128]{2,1,0:T(8,128)(2,1)}), bf16[24,201,128]{2,1,0:T(8,128)(2,1)}) %all-gather.7.cloned.1.call-update) | async-done | bytes 1234960 | tf_op jit(solution)/shard_map/all_gather | solution.py:70
  83.4 1.6 reshape.104
  85.0 1.5 fusion.44
  86.5 3.0 copy-done.1
  89.5 1.1 fusion.6
  90.6 62.1 %all-gather.9.cloned.1.call-done = bf16[24,201,128]{2,1,0:T(8,128)(2,1)} async-done(((bf16[3,201,128]{2,1,0:T(8,128)(2,1)}), bf16[24,201,128]{2,1,0:T(8,128)(2,1)}) %all-gather.9.cloned.1.call-update) | async-done | bytes 1234960 | tf_op jit(solution)/shard_map/all_gather | solution.py:71
  152.7 1.6 reshape.105
  154.3 5.1 fusion.27
  159.5 127.8 %all-gather.11.cloned.1.call-done = bf16[384,8192]{1,0:T(8,128)(2,1)} async-done(((bf16[384,128]{1,0:T(8,128)(2,1)}), bf16[384,8192]{1,0:T(8,128)(2,1)}) %all-gather.11.cloned.1.call-update) | async-done | bytes 6291472 | tf_op jit(solution)/shard_map/all_gather | solution.py:92
  287.3 5.7 fusion.29
  293.1 0.2 all-gather.15.cloned.1.call-start
  293.3 0.1 copy.41
  293.4 0.1 eq.73
  293.6 0.1 eq.76
  293.8 1.8 reduce-window.6
  295.6 0.3 slice_reduce_fusion
  295.9 0.1 fusion.33
  296.0 0.2 sub.29
  296.2 0.1 copy.44
  296.3 0.8 fusion.12
  297.1 112.6 %all-gather.13.cloned.1.call-done = bf16[384,4096]{0,1:T(8,128)(2,1)} async-done(((bf16[384,64]{0,1:T(8,128)(2,1)}), bf16[384,4096]{0,1:T(8,128)(2,1)}) %all-gather.13.cloned.1.call-update) | async-done | bytes 3145744 | tf_op jit(solution)/shard_map/all_gather | solution.py:101
  409.8 2.8 fusion.7
  412.6 2.6 fusion.10
  415.3 81.5 %all-gather.15.cloned.1.call-done = bf16[8,36,4096]{2,1,0:T(8,128)(2,1)} async-done(((bf16[1,36,4096]{2,1,0:T(8,128)(2,1)}), bf16[8,36,4096]{2,1,0:T(8,128)(2,1)}) %all-gather.15.cloned.1.call-update) | async-done | bytes 2359312 | tf_op jit(solution)/shard_map/all_gather | solution.py:110
  496.8 4.1 reshape.108
  500.9 3.2 fusion.17
  504.1 2.2 convolution_convert_fusion
  506.3 43.9 %fusion = bf16[40,4096]{1,0:T(8,128)(2,1)S(1)} fusion(bf16[288,4096]{1,0:T(8,128)(2,1)} %convolution_convert_fusion), kind=kCustom, calls=%all-reduce-scatter | all-reduce-scatter fusion | flops 1310721 | bytes 2689024
  550.2 0.1 slice.19
  550.3 1.3 collective-permute-start
  551.6 1.3 dynamic-slice.4
  553.6 1.5 collective-permute-done
  555.2 0.5 concatenate
  555.7 0.1 constant_dynamic-slice_fusion
  555.8 0.6 all_to_all.14
  556.4 0.4 copy.57
  556.8 1.1 reshape.112
  557.9 37.6 %all-to-all-start = ((bf16[64,2,1152]{2,1,0:T(2,128)(2,1)}), bf16[64,2,1152]{2,1,0:T(2,128)(2,1)S(1)}, u32[]{:S(2)}, u32[]{:S(2)}) async-start(bf16[64,2,1152]{2,1,0:T(2,128)(2,1)} %reshape.112), calls=%async_computation | async-start | bytes 589824 | tf_op jit(solution)/shard_map/all_to_all | solution.py:123
  595.6 14.1 %all-to-all-done = bf16[64,2,1152]{2,1,0:T(2,128)(2,1)S(1)} async-done(((bf16[64,2,1152]{2,1,0:T(2,128)(2,1)}), bf16[64,2,1152]{2,1,0:T(2,128)(2,1)S(1)}, u32[]{:S(2)}, u32[]{:S(2)}) %all-to-all-start) | async-done | bytes 294944 | tf_op jit(solution)/shard_map/all_to_all | solution.py:123
  609.7 0.5 reshape.113
  610.4 0.2 all_to_all.17
  610.6 1.6 fusion.23
  612.2 0.6 add_convert_fusion
  (38 shorter events, 0.4 us)
Async XLA Ops:
  6.5 1.3 copy-start
  6.5 78.5 %copy-start.8 = (bf16[384,128]{1,0:T(8,128)(2,1)S(1)}, bf16[384,128]{1,0:T(8,128)(2,1)}, u32[]{:S(2)}) copy-start(bf16[384,128]{1,0:T(8,128)(2,1)} %param.14) | copy-start | bytes 294916
  6.5 76.9 %all-gather.7.cloned.1.call-start = ((), (), s32[]{:S(2)}) async-start(), calls=%async_computation.1 | async-start | bytes 1437696 | tf_op jit(solution)/shard_map/all_gather | solution.py:70
  8.6 144.1 %all-gather.9.cloned.1.call-start = ((), (), s32[]{:S(2)}) async-start(), calls=%async_computation.2 | async-start | bytes 1437696 | tf_op jit(solution)/shard_map/all_gather | solution.py:71
  10.2 277.1 %all-gather.11.cloned.1.call-start = ((), (), s32[]{:S(2)}) async-start(), calls=%async_computation.3 | async-start | bytes 6389760 | tf_op jit(solution)/shard_map/all_gather | solution.py:92
  86.5 3.0 copy-start.1
  154.3 5.2 copy-start.10
  154.3 133.0 %copy-start.5 = (bf16[384,64]{0,1:T(8,128)(2,1)S(1)}, bf16[384,64]{0,1:T(8,128)(2,1)}, u32[]{:S(2)}) copy-start(bf16[384,64]{0,1:T(8,128)(2,1)} %param.13) | copy-start | bytes 147460
  159.4 250.4 %all-gather.13.cloned.1.call-start = ((), (), s32[]{:S(2)}) async-start(), calls=%async_computation.4 | async-start | bytes 3194880 | tf_op jit(solution)/shard_map/all_gather | solution.py:101
  159.5 133.8 %copy-start.6 = (s32[384,2]{0,1:T(2,128)S(1)}, s32[384,2]{0,1:T(2,128)}, u32[]{:S(2)}) copy-start(s32[384,2]{0,1:T(2,128)} %param.22) | copy-start | bytes 9220
  293.1 203.7 %all-gather.15.cloned.1.call-start = ((), (), s32[]{:S(2)}) async-start(), calls=%async_computation.5 | async-start | bytes 2949120 | tf_op jit(solution)/shard_map/all_gather | solution.py:110
  293.7 118.9 %copy-start.9 = (f32[4096]{0:T(1024)S(1)}, f32[4096]{0:T(1024)}, u32[]{:S(2)}) copy-start(f32[4096]{0:T(1024)} %param.21) | copy-start | bytes 49156
  409.8 2.8 copy-start.2
  500.9 3.2 copy-start.3
  550.2 45.4 %copy-start.7 = (s32[384,2]{0,1:T(2,128)S(1)}, s32[384,2]{0,1:T(2,128)}, u32[]{:S(2)}) copy-start(s32[384,2]{0,1:T(2,128)} %param.23) | copy-start | bytes 9220
  550.3 4.9 collective-permute-start
  557.9 51.8 %all-to-all-start = ((bf16[64,2,1152]{2,1,0:T(2,128)(2,1)}), bf16[64,2,1152]{2,1,0:T(2,128)(2,1)S(1)}, u32[]{:S(2)}, u32[]{:S(2)}) async-start(bf16[64,2,1152]{2,1,0:T(2,128)(2,1)} %reshape.112), calls=%async_computation | async-start | bytes 589824 | tf_op jit(solution)/shard_map/all_to_all | solution.py:123
  595.6 16.6 %copy-start.4 = (bf16[384,64]{0,1:T(8,128)(2,1)S(1)}, bf16[384,64]{0,1:T(8,128)(2,1)}, u32[]{:S(2)}) copy-start(bf16[384,64]{0,1:T(8,128)(2,1)} %fusion.29) | copy-start | bytes 147460
Sparse Core Ops, SparseCore 0:
  10.6 72.7 all-gather.6
  86.6 66.0 all-gather.8
  159.5 127.7 all-gather.10
  293.2 116.5 all-gather.12
  415.4 81.3 all-gather.14
where the time goes:
time: 624 us; the launch traced here: 619 us
  waiting for transfers between devices  470 us (75%)
  blocking collectives  43.9 us (7%)
  starting transfers between devices  39.3 us (6%)
  matrix products  21.9 us (4%)
  local copies, waits for them, and re-layouts  19.8 us (3%)
  between operations  14.2 us (2%)
  other arithmetic  10.3 us (2%)
    all_gather x1, waiting for transfers between devices, per_device(): lax.all_gather(attended, 'expert', axis=1, tiled=True)  128 us
    all_gather x1, waiting for transfers between devices, per_device(): gathered = lax.all_gather(mid, 'expert', axis=1, tiled=True)  113 us
    all_gather x1, waiting for transfers between devices, per_device(): lax.all_gather(dispatched, 'seq', axis=0, tiled=True)  81.5 us
    all_gather x1, waiting for transfers between devices, per_device(): key_block = lax.all_gather(key_slice, 'seq', axis=0, tiled=True)  70.1 us
    all_gather x1, waiting for transfers between devices, per_device(): value_block = lax.all_gather(value_slice, 'seq', axis=0, tiled=True)  62.1 us
    unnamed x1, blocking collectives  43.9 us
    all_to_all x1, starting transfers between devices, per_device(): lax.all_to_all(summed, 'expert', split_axis=1, concat_axis=0, tiled=True)  37.6 us
    all_to_all x1, waiting for transfers between devices, per_device(): lax.all_to_all(summed, 'expert', split_axis=1, concat_axis=0, tiled=True)  14.1 us
  transfers between devices with their start and end apart: 7, of which 7 were waited for; matrix products, arithmetic and copies ran while one was open for 2% of the time, Pallas kernels for 0%

commit v1 on v0

v1 whole, which is shorter than its diff:
```python
import math

import jax
import jax.numpy as jnp
from jax import lax
from jax.sharding import Mesh
from jax.sharding import PartitionSpec as P

FIXED_SCALE = 1.0 / 65536.0
NORM_EPSILON = 1e-05
MASKED_SCORE = -1e30
SEQ = ("yh", "x")
EXP = ("z", "yl", "core")
NEAR = ("yl", "core")
f32, bf16 = jnp.float32, jnp.bfloat16


def swap(v, axis):
    return lax.ppermute(v, axis, [(0, 1), (1, 0)])


def spread(v, axis):
    n = lax.axis_size(axis)
    return lax.all_to_all(jnp.broadcast_to(v[None], (n,) + v.shape), axis, 0, 0, tiled=True)


def route_tables(expert_ids, gate_fixed, experts, capacity):
    token_count, top_count = expert_ids.shape
    flat_ids = expert_ids.reshape(-1)
    assigned = flat_ids.shape[0]
    expert_cols = lax.broadcasted_iota(jnp.int32, (assigned, experts), 1)
    matches = flat_ids[:, None] == expert_cols
    before = lax.broadcasted_iota(jnp.int32, (assigned, assigned), 1) < lax.broadcasted_iota(
        jnp.int32, (assigned, assigned), 0
    )
    counts = jnp.dot(before.astype(bf16), matches.astype(bf16), preferred_element_type=f32)
    rank_of = jnp.sum(jnp.where(matches, counts, 0.0), axis=1).astype(jnp.int32)
    slot_of = (flat_ids * capacity + rank_of).reshape(token_count, top_count)
    slot_cols = lax.broadcasted_iota(jnp.int32, (token_count, experts * capacity), 1)
    selectors = [(slot_of[:, k : k + 1] == slot_cols) for k in range(top_count)]
    weights = gate_fixed.astype(f32) * FIXED_SCALE
    return selectors, weights


def attention(queries, keys, values, slot, frame_ids, frame_rows):
    width = keys.shape[0]
    scale = 1.0 / math.sqrt(queries.shape[1])
    scores = lax.dot_general(queries, keys, (((1,), (1,)), ((), ())), preferred_element_type=f32) * scale
    column_frame = jnp.repeat(frame_ids, frame_rows, total_repeat_length=width)
    inside = column_frame[None, :] == slot[:, None]
    scores = jnp.where(inside, scores, MASKED_SCORE)
    row_max = jnp.max(scores, axis=1, keepdims=True)
    expon = jnp.exp(scores - row_max)
    row_total = jnp.sum(expon, axis=1, keepdims=True)
    probability = (expon / row_total).astype(bf16)
    mixed = jnp.dot(probability, values, preferred_element_type=f32)
    present = jnp.any(frame_ids[None, :] == slot[:, None], axis=1, keepdims=True)
    return jnp.where(present, mixed, 0.0).astype(bf16)


def per_device(
    hidden_in,
    queries,
    frame_keys,
    frame_values,
    cited_frame,
    frame_slot,
    attn_gate,
    out_weight,
    mlp_gain,
    expert_ids,
    gate_fixed,
    w_in,
    w_down,
):
    head = queries.shape[1]
    tokens = queries.shape[0]
    nx, nz, nh = lax.axis_size("x"), lax.axis_size("z"), lax.axis_size("yh")
    experts = lax.axis_size(EXP)
    near = lax.axis_size(NEAR)
    feats = hidden_in.shape[1]
    yh, x, z = lax.axis_index("yh"), lax.axis_index("x"), lax.axis_index("z")
    held, frame_rows = frame_keys.shape[0], frame_keys.shape[1]
    own = jnp.concatenate(
        [
            lax.dynamic_slice_in_dim(frame_keys, z * head, head, 2).reshape(held * frame_rows, head),
            lax.dynamic_slice_in_dim(frame_values, z * head, head, 2).reshape(held * frame_rows, head),
        ],
        axis=0,
    )
    other = swap(own, "yh")
    half = held * frame_rows
    keys = jnp.concatenate([own[:half], other[:half]], axis=0)
    values = jnp.concatenate([own[half:], other[half:]], axis=0)
    turned = out_weight.T.reshape(feats, nz, near * head).transpose(1, 0, 2)
    near_weight = lax.all_to_all(turned, "z", 0, 0, tiled=True).reshape(nz * feats, near * head)
    frame_cols = lax.broadcasted_iota(jnp.int32, (tokens, frame_slot.shape[0]), 1)
    token_slot = jnp.sum(jnp.where(cited_frame[:, None] == frame_cols, frame_slot[None, :], 0), axis=1)
    slot_rows = jnp.zeros((16, head), bf16).at[: tokens // head].set(
        token_slot.reshape(tokens // head, head).astype(bf16)
    )
    gathered = spread(jnp.concatenate([queries, slot_rows]), "x")
    all_queries = gathered[:, :tokens].reshape(nx * tokens, head)
    all_slots = gathered[:, tokens : tokens + tokens // head].reshape(nx * tokens).astype(jnp.int32)
    frame_ids = jnp.concatenate(
        [held * (h * nx + x) + jnp.arange(held, dtype=jnp.int32) for h in (yh, 1 - yh)]
    )
    mixed = attention(all_queries, keys, values, all_slots, frame_ids, frame_rows)
    back = lax.all_to_all(mixed.reshape(nx, tokens, head), "x", 0, 0, tiled=True)
    attended = jnp.sum(back.astype(f32), axis=0).astype(bf16)
    heads = lax.all_gather(attended, NEAR, axis=1, tiled=True)
    partial = lax.dot_general(
        near_weight, heads, (((1,), (1,)), ((), ())), preferred_element_type=f32
    ).astype(bf16)
    parts = lax.all_to_all(partial.reshape(nz, feats, tokens), "z", 0, 0, tiled=True)
    projected = jnp.sum(parts.astype(f32), axis=0)
    mid = (hidden_in.T.astype(f32) + jnp.tanh(attn_gate)[:, None] * projected).astype(bf16)
    capacity = 6 * tokens // experts
    selectors, weights = route_tables(expert_ids, gate_fixed, experts, capacity)
    select_rows = (selectors[0] | selectors[1]).astype(bf16)
    sent = lax.dot_general(
        select_rows, mid, (((0,), (1,)), ((), ())), preferred_element_type=f32
    ).astype(bf16)
    came = lax.all_to_all(sent.reshape(experts, capacity, feats), EXP, 0, 0, tiled=True)
    rows = came.transpose(1, 0, 2).reshape(capacity, experts * feats)
    wide = rows.astype(f32)
    mean_square = jnp.mean(wide * wide, axis=1, keepdims=True)
    normed = (wide * lax.rsqrt(mean_square + NORM_EPSILON) * mlp_gain).astype(bf16)
    far = swap(normed, "yh")
    pair = jnp.where(yh == 0, jnp.concatenate([normed, far]), jnp.concatenate([far, normed]))
    everyone = spread(pair, "x").reshape(nx * nh * capacity, experts * feats)
    hidden_units = w_in.shape[3]
    expert_in = w_in[0].reshape(w_in.shape[1], 2 * hidden_units)
    gate_up = jnp.dot(everyone, expert_in, preferred_element_type=f32)
    activated = (jax.nn.silu(gate_up[:, :hidden_units]) * gate_up[:, hidden_units:]).astype(bf16)
    down = jnp.dot(activated, w_down[0], preferred_element_type=f32).astype(bf16)
    over_x = lax.all_to_all(
        down.reshape(nx, nh * capacity, experts * feats), "x", 0, 0, tiled=True
    )
    halves = jnp.sum(over_x.astype(f32), axis=0)
    low, high = halves[:capacity], halves[capacity:]
    mine, theirs = jnp.where(yh == 0, low, high), jnp.where(yh == 0, high, low)
    summed = (mine + swap(theirs.astype(bf16), "yh").astype(f32)).astype(bf16)
    dealt = summed.reshape(capacity, experts, feats).transpose(1, 0, 2)
    came_back = lax.all_to_all(dealt, EXP, 0, 0, tiled=True).reshape(experts * capacity, feats)
    mixed_out = sum(
        jnp.dot(s.astype(bf16), came_back, preferred_element_type=f32) * weights[:, k : k + 1]
        for k, s in enumerate(selectors)
    )
    return (mid.T.astype(f32) + mixed_out).astype(bf16)


def solution(mesh):
    fine = Mesh(mesh.devices.reshape(2, 4, 8, 4, 2), SEQ + EXP)
    return jax.shard_map(
        per_device,
        mesh=fine,
        in_specs=(
            P(SEQ, EXP),
            P(SEQ, EXP),
            P(SEQ, None, None),
            P(SEQ, None, None),
            P(SEQ),
            P(),
            P(EXP),
            P(None, EXP),
            P(),
            P(SEQ, None),
            P(SEQ, None),
            P(EXP, None, None, SEQ),
            P(EXP, SEQ, None),
        ),
        out_specs=P(SEQ, EXP),
        check_vma=False,
    )
```

time: 624 us -> 249 us (0.40)
  waiting for transfers between devices: 470 us -> 57.4 us
  blocking collectives: 43.9 us -> 106 us
  starting transfers between devices: 39.3 us -> 53.3 us
  between operations: 14.2 us -> 0.49 us
  matrix products: 21.9 us -> 10.3 us
  local copies, waits for them, and re-layouts: 19.8 us -> 12.3 us
    all_gather x5 -> x0, waiting for transfers between devices: 454 us -> none  [the longest x1 128 us: per_device(): lax.all_gather(attended, 'expert', axis=1, tiled=True)]
    all_to_all x0 -> x3, blocking collectives: none -> 86.8 us  [the longest x1 30.6 us: spread(): lax.all_to_all(jnp.broadcast_to(v[None], (n,) + v.shape), axis, 0, 0, til...]
    unnamed x1 -> x0, blocking collectives: 43.9 us -> none
    all_to_all x1 -> x5, waiting for transfers between devices: 14.1 us -> 36.1 us  [the longest x1 14.1 us: per_device(): lax.all_to_all(dealt, EXP, 0, 0, tiled=True)]
    ppermute x0 -> x3, waiting for transfers between devices: none -> 21.2 us  [swap(): return lax.ppermute(v, axis, [(0, 1), (1, 0)])]
    ppermute x0 -> x3, starting transfers between devices: none -> 20.5 us  [swap(): return lax.ppermute(v, axis, [(0, 1), (1, 0)])]
    all_gather x0 -> x1, blocking collectives: none -> 19.1 us  [per_device(): heads = lax.all_gather(attended, NEAR, axis=1, tiled=True)]
    dot_general x7 -> x9, matrix products: 21.9 us -> 10.3 us  [the longest x1 2.89 us: attention(): mixed = jnp.dot(probability, values, preferred_element_type=f32)]
  transfers between devices with their start and end apart: 7 -> 8, of which waited for: 7 -> 7; matrix products, arithmetic and copies ran while one was open for 2% -> 4% of each run, Pallas kernels for 0% -> 0%
where the time goes in v1:
time: 249 us; the launch traced here: 248 us
  blocking collectives  106 us (43%)
  waiting for transfers between devices  57.4 us (23%)
  starting transfers between devices  53.3 us (21%)
  local copies, waits for them, and re-layouts  12.3 us (5%)
  matrix products  10.3 us (4%)
  other arithmetic  8.36 us (3%)
    all_to_all x1, blocking collectives, spread(): lax.all_to_all(jnp.broadcast_to(v[None], (n,) + v.shape), axis, 0, 0, til...  30.6 us
    all_to_all x1, blocking collectives, per_device(): lax.all_to_all(down.reshape(nx, nh * capacity, experts * feats), 'x', 0,...  29.2 us
    all_to_all x1, blocking collectives, per_device(): lax.all_to_all(sent.reshape(experts, capacity, feats), EXP, 0, 0, tiled=T...  27 us
    ppermute x3, waiting for transfers between devices, swap(): return lax.ppermute(v, axis, [(0, 1), (1, 0)])  21.2 us
    ppermute x3, starting transfers between devices, swap(): return lax.ppermute(v, axis, [(0, 1), (1, 0)])  20.5 us
    all_gather x1, blocking collectives, per_device(): heads = lax.all_gather(attended, NEAR, axis=1, tiled=True)  19.1 us
    all_to_all x1, waiting for transfers between devices, per_device(): lax.all_to_all(dealt, EXP, 0, 0, tiled=True)  14.1 us
    all_to_all x1, starting transfers between devices, per_device(): lax.all_to_all(dealt, EXP, 0, 0, tiled=True)  12.1 us
  transfers between devices with their start and end apart: 8, of which 7 were waited for; matrix products, arithmetic and copies ran while one was open for 4% of the time, Pallas kernels for 0%

profile of v1, /device:TPU:1, one launch (start us, length us, event | category | flops | bytes accessed | tf_op | source)
XLA Modules:
  0.0 248.0 jit_solution(15705859312829586642)
XLA Ops:
  0.1 1.1 constant_dynamic-slice_fusion
  1.3 8.3 %collective-permute-start = (bf16[1206,128]{1,0:T(8,128)(2,1)S(1)}, bf16[1206,128]{1,0:T(8,128)(2,1)S(1)}, u32[]{:S(2)}, u32[]{:S(2)}) collective-permute-start(bf16[1206,128]{1,0:T(8,128)(2,1)S(1)} %pad_maximum_fusion), channel_id=1, source_target_pairs={{0,256},{256,0},{1,257},{257,1},{2,258},{258,2},{3,259},{259,3},{4... | collective-permute-start | bytes 926216 | tf_op jit(solution)/shard_map/ppermute | solution.py:19
  9.6 0.8 select_reduce_fusion
  10.4 0.9 fusion.37
  11.3 0.8 broadcast_in_dim.42
  12.1 4.0 %all-to-all-start = ((bf16[4,400,128]{2,1,0:T(8,128)(2,1)}), bf16[4,400,128]{2,1,0:T(8,128)(2,1)S(1)}, u32[]{:S(2)}, u32[]{:S(2)}) async-start(bf16[4,400,128]{2,1,0:T(8,128)(2,1)} %broadcast_in_dim.42), calls=%async_computation | async-start | bytes 819200 | tf_op jit(solution)/shard_map/all_to_all | solution.py:24
  16.1 0.7 fusion.51
  16.8 0.7 fusion.50
  17.6 3.9 %select_select_fusion = s32[1206]{0:T(1024)S(1)} fusion(pred[1206]{0:T(1024)(128)(4,1)S(1)} %copy-done.5, pred[1206]{0:T(1024)(128)(4,1)S(1)} %copy-done.6, pred[1206]{0:T(1024)(128)(4,1)S(1)} %copy-done.7, pred[1206]{0:T(1024)(128)(4,1)S(1)} %copy-done.8, pred[1206]{0:T(1024)(128)(4,1)S(1)} %copy-done.9, s32[]{:T(128)} %bitcast.6, s32[]{:T(128)} %bitcast.1, ...), kind=kLoop, calls=%fused_computation.67 | loop fusion | flops 6030 | bytes 10878 | tf_op jit(solution)/shard_map/jit(_take)/gather | solution.py:49
  21.5 1.7 all-to-all-done
  23.4 1.3 fusion.52
  24.6 1.1 fusion.1
  25.7 2.9 %fusion.12 = bf16[1536,128]{1,0:T(8,128)(2,1)} fusion(f32[1536,1206]{0,1:T(8,128)S(1)} %get-tuple-element.42, f32[1536]{0:T(1024)S(1)} %fusion.1, f32[1536]{0:T(1024)S(1)} %get-tuple-element.41, pred[1536]{0:T(1024)(128)(4,1)S(1)} %compare_reduce_fusion, bf16[603,128]{1,0:T(8,128)(2,1)S(1)} %get-tuple-element.33, bf16[603,128]{1,0:T(8,128)(2,1)S(1)} %reshape.192), kind=kOutput, calls=%fused_computation.16 | convolution fusion | flops 480786432 | bytes 8125440 | tf_op jit(solution)/shard_map/dot_general | solution.py:56
  28.6 3.5 %all-to-all-start.1 = ((bf16[4,384,128]{2,1,0:T(8,128)(2,1)}), bf16[4,384,128]{2,1,0:T(8,128)(2,1)S(1)}, u32[]{:S(2)}, u32[]{:S(2)}) async-start(bf16[4,384,128]{2,1,0:T(8,128)(2,1)} %bitcast.8), calls=%async_computation.1 | async-start | bytes 786432 | tf_op jit(solution)/shard_map/all_to_all | solution.py:109
  32.1 0.6 copy.51
  32.7 1.6 copy.44
  34.3 4.0 %all-to-all-done.1 = bf16[4,384,128]{2,1,0:T(8,128)(2,1)S(1)} async-done(((bf16[4,384,128]{2,1,0:T(8,128)(2,1)}), bf16[4,384,128]{2,1,0:T(8,128)(2,1)S(1)}, u32[]{:S(2)}, u32[]{:S(2)}) %all-to-all-start.1) | async-done | bytes 393248 | tf_op jit(solution)/shard_map/all_to_all | solution.py:109
  38.3 9.7 %all-to-all-start.2 = ((bf16[8,64,1024]{2,1,0:T(8,128)(2,1)}), bf16[8,64,1024]{2,1,0:T(8,128)(2,1)S(1)}, u32[]{:S(2)}, u32[]{:S(2)}) async-start(bf16[8,64,1024]{2,1,0:T(8,128)(2,1)} %copy.44), calls=%async_computation.2 | async-start | bytes 2097152 | tf_op jit(solution)/shard_map/all_to_all | solution.py:96
  48.1 19.1 %all_gather.3 = bf16[384,1024]{1,0:T(8,128)(2,1)S(1)} all-gather(bf16[384,128]{1,0:T(8,128)(2,1)S(1)} %reduce_sum.68), channel_id=1, replica_groups=mesh['yh'=2,'x'=4,'z'=8,'yl'=4,'core'=2] {'yl','core'}, dimensions={1}, use_global_device_ids=true | all-gather | bytes 884736 | tf_op jit(solution)/shard_map/all_gather | solution.py:111
  67.2 6.6 %all-to-all-done.2 = bf16[8,64,1024]{2,1,0:T(8,128)(2,1)S(1)} async-done(((bf16[8,64,1024]{2,1,0:T(8,128)(2,1)}), bf16[8,64,1024]{2,1,0:T(8,128)(2,1)S(1)}, u32[]{:S(2)}, u32[]{:S(2)}) %all-to-all-start.2) | async-done | bytes 1048608 | tf_op jit(solution)/shard_map/all_to_all | solution.py:96
  73.8 0.6 fusion.22
  74.4 0.9 copy.45
  75.4 3.5 %all-to-all-start.3 = ((bf16[8,64,384]{2,1,0:T(8,128)(2,1)}), bf16[8,64,384]{2,1,0:T(8,128)(2,1)S(1)}, u32[]{:S(2)}, u32[]{:S(2)}) async-start(bf16[8,64,384]{2,1,0:T(8,128)(2,1)} %bitcast.13), calls=%async_computation.3 | async-start | bytes 786432 | tf_op jit(solution)/shard_map/all_to_all | solution.py:115
  79.1 0.4 fusion.24
  79.8 9.7 %all-to-all-done.3 = bf16[8,64,384]{2,1,0:T(8,128)(2,1)S(1)} async-done(((bf16[8,64,384]{2,1,0:T(8,128)(2,1)}), bf16[8,64,384]{2,1,0:T(8,128)(2,1)S(1)}, u32[]{:S(2)}, u32[]{:S(2)}) %all-to-all-start.3) | async-done | bytes 393248 | tf_op jit(solution)/shard_map/all_to_all | solution.py:115
  89.6 1.1 fusion.8
  90.7 0.3 copy.48
  91.2 0.4 reshape.221
  91.6 27.0 %all_to_all.40 = bf16[64,2,1152]{2,1,0:T(2,128)(2,1)S(1)} all-to-all(bf16[64,2,1152]{2,1,0:T(2,128)(2,1)S(1)} %reshape.221), channel_id=1, replica_groups=mesh['yh'=2,'x'=4,'z'=8,'yl'=4,'core'=2] {'z','yl','core'}, dimensions={0} | all-to-all | bytes 589824 | tf_op jit(solution)/shard_map/all_to_all | solution.py:124
  118.6 0.5 reshape.222
  119.8 0.4 reshape.203
  120.3 5.3 %collective-permute-start.1 = (bf16[36,4096]{1,0:T(8,128)(2,1)S(1)}, bf16[36,4096]{1,0:T(8,128)(2,1)S(1)}, u32[]{:S(2)}, u32[]{:S(2)}) collective-permute-start(bf16[36,4096]{1,0:T(8,128)(2,1)S(1)} %multiply_convert_fusion), channel_id=1, source_target_pairs={{0,256},{256,0},{1,257},{257,1},{2,258},{258,2},{3,259},{259,3},{4... | collective-permute-start | bytes 884744 | tf_op jit(solution)/shard_map/ppermute | solution.py:19
  125.6 16.4 %collective-permute-done.1 = bf16[36,4096]{1,0:T(8,128)(2,1)S(1)} collective-permute-done((bf16[36,4096]{1,0:T(8,128)(2,1)S(1)}, bf16[36,4096]{1,0:T(8,128)(2,1)S(1)}, u32[]{:S(2)}, u32[]{:S(2)}) %collective-permute-start.1) | collective-permute-done | bytes 294944 | tf_op jit(solution)/shard_map/ppermute | solution.py:19
  142.6 30.6 %all_to_all.41 = bf16[4,72,4096]{2,1,0:T(8,128)(2,1)S(1)} all-to-all(bf16[4,72,4096]{2,1,0:T(8,128)(2,1)S(1)} %broadcast_in_dim.70), channel_id=1, replica_groups=mesh['yh'=2,'x'=4,'z'=8,'yl'=4,'core'=2] {'x'}, dimensions={0} | all-to-all | bytes 4718592 | tf_op jit(solution)/shard_map/all_to_all | solution.py:24
  173.2 0.8 fusion.14
  174.0 0.8 convolution_convert_fusion
  174.8 29.2 %all_to_all.42 = bf16[4,72,4096]{2,1,0:T(8,128)(2,1)S(1)} all-to-all(bf16[4,72,4096]{2,1,0:T(8,128)(2,1)S(1)} %bitcast.49), channel_id=1, replica_groups=mesh['yh'=2,'x'=4,'z'=8,'yl'=4,'core'=2] {'x'}, dimensions={0} | all-to-all | bytes 4718592 | tf_op jit(solution)/shard_map/all_to_all | solution.py:137
  204.0 0.4 convert_reduce_fusion
  204.5 6.9 %collective-permute-start.2 = (bf16[36,4096]{1,0:T(8,128)(2,1)S(1)}, bf16[36,4096]{1,0:T(8,128)(2,1)S(1)}, u32[]{:S(2)}, u32[]{:S(2)}) collective-permute-start(bf16[36,4096]{1,0:T(8,128)(2,1)S(1)} %select_convert_fusion), channel_id=1, source_target_pairs={{0,256},{256,0},{1,257},{257,1},{2,258},{258,2},{3,259},{259,3},{4... | collective-permute-start | bytes 884744 | tf_op jit(solution)/shard_map/ppermute | solution.py:19
  211.4 4.8 %collective-permute-done.2 = bf16[36,4096]{1,0:T(8,128)(2,1)S(1)} collective-permute-done((bf16[36,4096]{1,0:T(8,128)(2,1)S(1)}, bf16[36,4096]{1,0:T(8,128)(2,1)S(1)}, u32[]{:S(2)}, u32[]{:S(2)}) %collective-permute-start.2) | collective-permute-done | bytes 294944 | tf_op jit(solution)/shard_map/ppermute | solution.py:19
  216.3 0.6 reshape.200
  217.0 0.4 copy.50
  217.4 1.1 reshape.223
  218.5 12.1 %all-to-all-start.7 = ((bf16[64,2,1152]{2,1,0:T(2,128)(2,1)}), bf16[64,2,1152]{2,1,0:T(2,128)(2,1)S(1)}, u32[]{:S(2)}, u32[]{:S(2)}) async-start(bf16[64,2,1152]{2,1,0:T(2,128)(2,1)} %reshape.223), calls=%async_computation.7 | async-start | bytes 589824 | tf_op jit(solution)/shard_map/all_to_all | solution.py:145
  230.7 14.1 %all-to-all-done.7 = bf16[64,2,1152]{2,1,0:T(2,128)(2,1)S(1)} async-done(((bf16[64,2,1152]{2,1,0:T(2,128)(2,1)}), bf16[64,2,1152]{2,1,0:T(2,128)(2,1)S(1)}, u32[]{:S(2)}, u32[]{:S(2)}) %all-to-all-start.7) | async-done | bytes 294944 | tf_op jit(solution)/shard_map/all_to_all | solution.py:145
  244.8 0.5 reshape.224
  245.6 0.9 fusion.28
  246.5 1.5 fusion.29
  (61 shorter events, 3.0 us)
Async XLA Ops:
  0.0 174.0 %copy-start = (bf16[1,128,4096]{2,1,0:T(8,128)(2,1)S(1)}, bf16[1,128,4096]{2,1,0:T(8,128)(2,1)}, u32[]{:S(2)}) copy-start(bf16[1,128,4096]{2,1,0:T(8,128)(2,1)} %param.29) | copy-start | bytes 3145732
  0.0 17.5 %copy-start.5 = (pred[1206]{0:T(1024)(128)(4,1)S(1)}, pred[1206]{0:T(1024)(128)(4,1)}, u32[]{:S(2)}) copy-start(pred[1206]{0:T(1024)(128)(4,1)} %constant.175) | copy-start | bytes 3622
  0.0 17.5 %copy-start.6 = (pred[1206]{0:T(1024)(128)(4,1)S(1)}, pred[1206]{0:T(1024)(128)(4,1)}, u32[]{:S(2)}) copy-start(pred[1206]{0:T(1024)(128)(4,1)} %constant.176) | copy-start | bytes 3622
  0.0 17.5 %copy-start.7 = (pred[1206]{0:T(1024)(128)(4,1)S(1)}, pred[1206]{0:T(1024)(128)(4,1)}, u32[]{:S(2)}) copy-start(pred[1206]{0:T(1024)(128)(4,1)} %constant.177) | copy-start | bytes 3622
  0.0 17.5 %copy-start.8 = (pred[1206]{0:T(1024)(128)(4,1)S(1)}, pred[1206]{0:T(1024)(128)(4,1)}, u32[]{:S(2)}) copy-start(pred[1206]{0:T(1024)(128)(4,1)} %constant.178) | copy-start | bytes 3622
  0.0 17.5 %copy-start.9 = (pred[1206]{0:T(1024)(128)(4,1)S(1)}, pred[1206]{0:T(1024)(128)(4,1)}, u32[]{:S(2)}) copy-start(pred[1206]{0:T(1024)(128)(4,1)} %constant.179) | copy-start | bytes 3622
  1.3 22.0 %collective-permute-start = (bf16[1206,128]{1,0:T(8,128)(2,1)S(1)}, bf16[1206,128]{1,0:T(8,128)(2,1)S(1)}, u32[]{:S(2)}, u32[]{:S(2)}) collective-permute-start(bf16[1206,128]{1,0:T(8,128)(2,1)S(1)} %pad_maximum_fusion), channel_id=1, source_target_pairs={{0,256},{256,0},{1,257},{257,1},{2,258},{258,2},{3,259},{259,3},{4... | collective-permute-start | bytes 926216 | tf_op jit(solution)/shard_map/ppermute | solution.py:19
  12.1 11.1 %all-to-all-start = ((bf16[4,400,128]{2,1,0:T(8,128)(2,1)}), bf16[4,400,128]{2,1,0:T(8,128)(2,1)S(1)}, u32[]{:S(2)}, u32[]{:S(2)}) async-start(bf16[4,400,128]{2,1,0:T(8,128)(2,1)} %broadcast_in_dim.42), calls=%async_computation | async-start | bytes 819200 | tf_op jit(solution)/shard_map/all_to_all | solution.py:24
  25.7 6.4 %copy-start.1 = (bf16[8192,64]{0,1:T(8,128)(2,1)S(1)}, bf16[8192,64]{0,1:T(8,128)(2,1)}, u32[]{:S(2)}) copy-start(bf16[8192,64]{0,1:T(8,128)(2,1)} %param.24) | copy-start | bytes 3145732
  28.6 9.7 %all-to-all-start.1 = ((bf16[4,384,128]{2,1,0:T(8,128)(2,1)}), bf16[4,384,128]{2,1,0:T(8,128)(2,1)S(1)}, u32[]{:S(2)}, u32[]{:S(2)}) async-start(bf16[4,384,128]{2,1,0:T(8,128)(2,1)} %bitcast.8), calls=%async_computation.1 | async-start | bytes 786432 | tf_op jit(solution)/shard_map/all_to_all | solution.py:109
  38.3 35.6 %all-to-all-start.2 = ((bf16[8,64,1024]{2,1,0:T(8,128)(2,1)}), bf16[8,64,1024]{2,1,0:T(8,128)(2,1)S(1)}, u32[]{:S(2)}, u32[]{:S(2)}) async-start(bf16[8,64,1024]{2,1,0:T(8,128)(2,1)} %copy.44), calls=%async_computation.2 | async-start | bytes 2097152 | tf_op jit(solution)/shard_map/all_to_all | solution.py:96
  48.1 30.7 %copy-start.3 = (s32[384,2]{0,1:T(2,128)S(1)}, s32[384,2]{0,1:T(2,128)}, u32[]{:S(2)}) copy-start(s32[384,2]{0,1:T(2,128)} %param.26) | copy-start | bytes 9220
  73.8 6.0 %copy-start.12 = (f32[64]{0:T(128)S(1)}, f32[64]{0:T(128)}, u32[]{:S(2)}) copy-start(f32[64]{0:T(128)} %param.23) | copy-start | bytes 772
  74.4 15.2 %copy-start.11 = (bf16[384,64]{0,1:T(8,128)(2,1)S(1)}, bf16[384,64]{0,1:T(8,128)(2,1)}, u32[]{:S(2)}) copy-start(bf16[384,64]{0,1:T(8,128)(2,1)} %param.17) | copy-start | bytes 147460
  75.4 14.2 %all-to-all-start.3 = ((bf16[8,64,384]{2,1,0:T(8,128)(2,1)}), bf16[8,64,384]{2,1,0:T(8,128)(2,1)S(1)}, u32[]{:S(2)}, u32[]{:S(2)}) async-start(bf16[8,64,384]{2,1,0:T(8,128)(2,1)} %bitcast.13), calls=%async_computation.3 | async-start | bytes 786432 | tf_op jit(solution)/shard_map/all_to_all | solution.py:115
  119.2 1.0 copy-start.2
  120.3 21.7 %collective-permute-start.1 = (bf16[36,4096]{1,0:T(8,128)(2,1)S(1)}, bf16[36,4096]{1,0:T(8,128)(2,1)S(1)}, u32[]{:S(2)}, u32[]{:S(2)}) collective-permute-start(bf16[36,4096]{1,0:T(8,128)(2,1)S(1)} %multiply_convert_fusion), channel_id=1, source_target_pairs={{0,256},{256,0},{1,257},{257,1},{2,258},{258,2},{3,259},{259,3},{4... | collective-permute-start | bytes 884744 | tf_op jit(solution)/shard_map/ppermute | solution.py:19
  142.6 30.6 %copy-start.10 = (bf16[1,4096,2,128]{3,2,1,0:T(2,128)(2,1)S(1)}, bf16[1,4096,2,128]{3,2,1,0:T(2,128)(2,1)}, u32[]{:S(2)}) copy-start(bf16[1,4096,2,128]{3,2,1,0:T(2,128)(2,1)} %param.28) | copy-start | bytes 6291460
  204.5 26.2 %copy-start.4 = (s32[384,2]{0,1:T(2,128)S(1)}, s32[384,2]{0,1:T(2,128)}, u32[]{:S(2)}) copy-start(s32[384,2]{0,1:T(2,128)} %param.27) | copy-start | bytes 9220
  204.5 11.7 %collective-permute-start.2 = (bf16[36,4096]{1,0:T(8,128)(2,1)S(1)}, bf16[36,4096]{1,0:T(8,128)(2,1)S(1)}, u32[]{:S(2)}, u32[]{:S(2)}) collective-permute-start(bf16[36,4096]{1,0:T(8,128)(2,1)S(1)} %select_convert_fusion), channel_id=1, source_target_pairs={{0,256},{256,0},{1,257},{257,1},{2,258},{258,2},{3,259},{259,3},{4... | collective-permute-start | bytes 884744 | tf_op jit(solution)/shard_map/ppermute | solution.py:19
  218.5 26.3 %all-to-all-start.7 = ((bf16[64,2,1152]{2,1,0:T(2,128)(2,1)}), bf16[64,2,1152]{2,1,0:T(2,128)(2,1)S(1)}, u32[]{:S(2)}, u32[]{:S(2)}) async-start(bf16[64,2,1152]{2,1,0:T(2,128)(2,1)} %reshape.223), calls=%async_computation.7 | async-start | bytes 589824 | tf_op jit(solution)/shard_map/all_to_all | solution.py:145

commit v2 on v1

--- a/solution.py
+++ b/solution.py
@@ -12,11 +12,21 @@
 SEQ = ("yh", "x")
 EXP = ("z", "yl", "core")
 NEAR = ("yl", "core")
+BOTH = ("yh",) + EXP
 f32, bf16 = jnp.float32, jnp.bfloat16
 
 
 def swap(v, axis):
     return lax.ppermute(v, axis, [(0, 1), (1, 0)])
+
+
+def shift(v, axis, by):
+    n = lax.axis_size(axis)
+    return lax.ppermute(v, axis, [(i, (i + by) % n) for i in range(n)])
+
+
+def tie(*values):
+    return lax.optimization_barrier(values)
 
 
 def spread(v, axis):
@@ -81,6 +91,8 @@
     feats = hidden_in.shape[1]
     yh, x, z = lax.axis_index("yh"), lax.axis_index("x"), lax.axis_index("z")
     held, frame_rows = frame_keys.shape[0], frame_keys.shape[1]
+    in_left, in_right = shift(w_in[0], "x", 1), shift(w_in[0], "x", -1)
+    down_left, down_right = shift(w_down[0], "x", 1), shift(w_down[0], "x", -1)
     own = jnp.concatenate(
         [
             lax.dynamic_slice_in_dim(frame_keys, z * head, head, 2).reshape(held * frame_rows, head),
@@ -92,26 +104,38 @@
     half = held * frame_rows
     keys = jnp.concatenate([own[:half], other[:half]], axis=0)
     values = jnp.concatenate([own[half:], other[half:]], axis=0)
-    turned = out_weight.T.reshape(feats, nz, near * head).transpose(1, 0, 2)
-    near_weight = lax.all_to_all(turned, "z", 0, 0, tiled=True).reshape(nz * feats, near * head)
     frame_cols = lax.broadcasted_iota(jnp.int32, (tokens, frame_slot.shape[0]), 1)
     token_slot = jnp.sum(jnp.where(cited_frame[:, None] == frame_cols, frame_slot[None, :], 0), axis=1)
     slot_rows = jnp.zeros((16, head), bf16).at[: tokens // head].set(
         token_slot.reshape(tokens // head, head).astype(bf16)
     )
-    gathered = spread(jnp.concatenate([queries, slot_rows]), "x")
+    packed = jnp.concatenate([queries, slot_rows])
+    gathered = spread(packed, "x")
+    gathered, turned = tie(gathered, out_weight.T)
+    turned = turned.reshape(feats, nz, near * head).transpose(1, 0, 2)
+    near_weight = lax.all_to_all(turned, "z", 0, 0, tiled=True).reshape(nz * feats, near * head)
     all_queries = gathered[:, :tokens].reshape(nx * tokens, head)
     all_slots = gathered[:, tokens : tokens + tokens // head].reshape(nx * tokens).astype(jnp.int32)
     frame_ids = jnp.concatenate(
         [held * (h * nx + x) + jnp.arange(held, dtype=jnp.int32) for h in (yh, 1 - yh)]
     )
     mixed = attention(all_queries, keys, values, all_slots, frame_ids, frame_rows)
-    back = lax.all_to_all(mixed.reshape(nx, tokens, head), "x", 0, 0, tiled=True)
-    attended = jnp.sum(back.astype(f32), axis=0).astype(bf16)
+    back = mixed.reshape(nx, tokens, head)
+    attended = lax.dynamic_index_in_dim(back, x, 0, keepdims=False).astype(f32)
+    for k in range(1, nx):
+        piece = lax.dynamic_index_in_dim(back, (x + k) % nx, 0, keepdims=False)
+        attended = attended + shift(piece, "x", k).astype(f32)
+    attended, near_weight = tie(attended.astype(bf16), near_weight)
     heads = lax.all_gather(attended, NEAR, axis=1, tiled=True)
     partial = lax.dot_general(
         near_weight, heads, (((1,), (1,)), ((), ())), preferred_element_type=f32
     ).astype(bf16)
+    partial, in_left, in_right, down_left, down_right = tie(
+        partial, in_left, in_right, down_left, down_right
+    )
+    half_in, half_down = w_in.shape[1] // 2, w_down.shape[1] // 2
+    in_far = shift(in_left[:half_in], "x", 1), shift(in_right[half_in:], "x", -1)
+    down_far = shift(down_left[:half_down], "x", 1), shift(down_right[half_down:], "x", -1)
     parts = lax.all_to_all(partial.reshape(nz, feats, tokens), "z", 0, 0, tiled=True)
     projected = jnp.sum(parts.astype(f32), axis=0)
     mid = (hidden_in.T.astype(f32) + jnp.tanh(attn_gate)[:, None] * projected).astype(bf16)
@@ -121,28 +145,32 @@
     sent = lax.dot_general(
         select_rows, mid, (((0,), (1,)), ((), ())), preferred_element_type=f32
     ).astype(bf16)
-    came = lax.all_to_all(sent.reshape(experts, capacity, feats), EXP, 0, 0, tiled=True)
-    rows = came.transpose(1, 0, 2).reshape(capacity, experts * feats)
+    sent = jnp.broadcast_to(sent.reshape(1, experts, capacity, feats), (nh, experts, capacity, feats))
+    came = lax.all_to_all(sent.reshape(-1, capacity, feats), BOTH, 0, 0, tiled=True)
+    rows = came.reshape(nh, experts, capacity, feats).transpose(0, 2, 1, 3)
+    (rows,) = tie(rows.reshape(nh * capacity, experts * feats))
     wide = rows.astype(f32)
     mean_square = jnp.mean(wide * wide, axis=1, keepdims=True)
     normed = (wide * lax.rsqrt(mean_square + NORM_EPSILON) * mlp_gain).astype(bf16)
-    far = swap(normed, "yh")
-    pair = jnp.where(yh == 0, jnp.concatenate([normed, far]), jnp.concatenate([far, normed]))
-    everyone = spread(pair, "x").reshape(nx * nh * capacity, experts * feats)
     hidden_units = w_in.shape[3]
-    expert_in = w_in[0].reshape(w_in.shape[1], 2 * hidden_units)
-    gate_up = jnp.dot(everyone, expert_in, preferred_element_type=f32)
-    activated = (jax.nn.silu(gate_up[:, :hidden_units]) * gate_up[:, hidden_units:]).astype(bf16)
-    down = jnp.dot(activated, w_down[0], preferred_element_type=f32).astype(bf16)
-    over_x = lax.all_to_all(
-        down.reshape(nx, nh * capacity, experts * feats), "x", 0, 0, tiled=True
-    )
-    halves = jnp.sum(over_x.astype(f32), axis=0)
-    low, high = halves[:capacity], halves[capacity:]
-    mine, theirs = jnp.where(yh == 0, low, high), jnp.where(yh == 0, high, low)
-    summed = (mine + swap(theirs.astype(bf16), "yh").astype(f32)).astype(bf16)
-    dealt = summed.reshape(capacity, experts, feats).transpose(1, 0, 2)
-    came_back = lax.all_to_all(dealt, EXP, 0, 0, tiled=True).reshape(experts * capacity, feats)
+
+    def up(part, weight):
+        weight = weight.reshape(weight.shape[0], 2 * hidden_units)
+        return jnp.dot(part, weight, preferred_element_type=f32)
+
+    def gated(gate_up):
+        return (jax.nn.silu(gate_up[:, :hidden_units]) * gate_up[:, hidden_units:]).astype(bf16)
+
+    ups = [up(normed, weight) for weight in (w_in[0], in_left, in_right)]
+    ups.append(up(normed[:, :half_in], in_far[0]) + up(normed[:, half_in:], in_far[1]))
+    act = [gated(u) for u in ups]
+    weights_down = [w_down[0], down_left, down_right, jnp.concatenate(down_far)]
+    down = sum(jnp.dot(p, w, preferred_element_type=f32) for p, w in zip(act, weights_down))
+    (down,) = tie(down.astype(bf16))
+    dealt = down.reshape(nh, capacity, experts, feats).transpose(0, 2, 1, 3).reshape(-1, capacity, feats)
+    back_sums = lax.all_to_all(dealt, BOTH, 0, 0, tiled=True)
+    back_sums = back_sums.reshape(nh, experts * capacity, feats).astype(f32)
+    came_back = jnp.sum(back_sums, axis=0).astype(bf16)
     mixed_out = sum(
         jnp.dot(s.astype(bf16), came_back, preferred_element_type=f32) * weights[:, k : k + 1]
         for k, s in enumerate(selectors)

time: 249 us -> 264 us (1.060)
  blocking collectives: 106 us -> 20 us
  starting transfers between devices: 53.3 us -> 89.2 us
  waiting for transfers between devices: 57.4 us -> 92.9 us
  local copies, waits for them, and re-layouts: 12.3 us -> 29.4 us
  matrix products: 10.3 us -> 21.4 us
    all_to_all x3 -> x0, blocking collectives: 86.8 us -> none  [the longest x1 30.6 us: spread(): lax.all_to_all(jnp.broadcast_to(v[None], (n,) + v.shape), axis, 0, 0, til...]
    ppermute x0 -> x11, starting transfers between devices: none -> 37.4 us  [shift(): return lax.ppermute(v, axis, [(i, (i + by) % n) for i in range(n)])]
    ppermute x0 -> x11, waiting for transfers between devices: none -> 28.9 us  [shift(): return lax.ppermute(v, axis, [(i, (i + by) % n) for i in range(n)])]
    all_to_all x1, waiting for transfers between devices: 1.7 us -> 28.4 us  [spread(): lax.all_to_all(jnp.broadcast_to(v[None], (n,) + v.shape), axis, 0, 0, til...]
    ppermute x3 -> x1, waiting for transfers between devices: 21.2 us -> 0.01 us  [swap(): return lax.ppermute(v, axis, [(0, 1), (1, 0)])]
    ppermute x3 -> x1, starting transfers between devices: 20.5 us -> 7.64 us  [swap(): return lax.ppermute(v, axis, [(0, 1), (1, 0)])]
    dot_general x2 -> x9, matrix products: 1.58 us -> 11.9 us  [the longest x5 9.46 us: up(): return jnp.dot(part, weight, preferred_element_type=f32)]
    all_to_all x2, starting transfers between devices: 15.6 us -> 24 us  [the longest x1 15.6 us: per_device(): back_sums = lax.all_to_all(dealt, BOTH, 0, 0, tiled=True)]
  transfers between devices with their start and end apart: 8 -> 17, of which waited for: 7 -> 7; matrix products, arithmetic and copies ran while one was open for 4% -> 17% of each run, Pallas kernels for 0% -> 0%
where the time goes in v2:
time: 264 us; the launch traced here: 263 us
  waiting for transfers between devices  92.9 us (35%)
  starting transfers between devices  89.2 us (34%)
  local copies, waits for them, and re-layouts  29.4 us (11%)
  matrix products  21.4 us (8%)
  blocking collectives  20 us (8%)
  other arithmetic  8.9 us (3%)
    ppermute x11, starting transfers between devices, shift(): return lax.ppermute(v, axis, [(i, (i + by) % n) for i in range(n)])  37.4 us
    ppermute x11, waiting for transfers between devices, shift(): return lax.ppermute(v, axis, [(i, (i + by) % n) for i in range(n)])  28.9 us
    all_to_all x1, waiting for transfers between devices, spread(): lax.all_to_all(jnp.broadcast_to(v[None], (n,) + v.shape), axis, 0, 0, til...  28.4 us
    all_to_all x1, waiting for transfers between devices, per_device(): back_sums = lax.all_to_all(dealt, BOTH, 0, 0, tiled=True)  21 us
    all_gather x1, blocking collectives, per_device(): heads = lax.all_gather(attended, NEAR, axis=1, tiled=True)  20 us
    all_to_all x1, starting transfers between devices, per_device(): back_sums = lax.all_to_all(dealt, BOTH, 0, 0, tiled=True)  15.6 us
    all_to_all x1, waiting for transfers between devices, per_device(): lax.all_to_all(partial.reshape(nz, feats, tokens), 'z', 0, 0, tiled=True)  14.1 us
    all_to_all x1, starting transfers between devices, per_device(): lax.all_to_all(turned, 'z', 0, 0, tiled=True)  10 us
  transfers between devices with their start and end apart: 17, of which 7 were waited for; matrix products, arithmetic and copies ran while one was open for 17% of the time, Pallas kernels for 0%

profile of v2, /device:TPU:1, one launch (start us, length us, event | category | flops | bytes accessed | tf_op | source)
XLA Modules:
  0.0 262.6 jit_solution(12100170697682443626)
XLA Ops:
  0.0 4.1 %collective-permute-start.4 = (bf16[4096,2,128]{2,1,0:T(2,128)(2,1)}, bf16[4096,2,128]{2,1,0:T(2,128)(2,1)}, u32[]{:S(2)}, u32[]{:S(2)}) collective-permute-start(bf16[4096,2,128]{2,1,0:T(2,128)(2,1)} %bitcast.91), channel_id=1, source_target_pairs={{0,64},{64,128},{128,192},{192,0},{1,65},{65,129},{129,193},{193,1... | collective-permute-start | bytes 6291464 | tf_op jit(solution)/shard_map/ppermute | solution.py:25
  4.1 3.2 %collective-permute-start.5 = (bf16[4096,2,128]{2,1,0:T(2,128)(2,1)}, bf16[4096,2,128]{2,1,0:T(2,128)(2,1)}, u32[]{:S(2)}, u32[]{:S(2)}) collective-permute-start(bf16[4096,2,128]{2,1,0:T(2,128)(2,1)} %bitcast.92), channel_id=1, source_target_pairs={{0,192},{64,0},{128,64},{192,128},{1,193},{65,1},{129,65},{193,129... | collective-permute-start | bytes 6291464 | tf_op jit(solution)/shard_map/ppermute | solution.py:25
  7.3 1.1 constant_dynamic-slice_fusion
  8.6 7.6 %collective-permute-start = (bf16[1206,128]{1,0:T(8,128)(2,1)S(1)}, bf16[1206,128]{1,0:T(8,128)(2,1)S(1)}, u32[]{:S(2)}, u32[]{:S(2)}) collective-permute-start(bf16[1206,128]{1,0:T(8,128)(2,1)S(1)} %pad_maximum_fusion), channel_id=1, source_target_pairs={{0,256},{256,0},{1,257},{257,1},{2,258},{258,2},{3,259},{259,3},{4... | collective-permute-start | bytes 926216 | tf_op jit(solution)/shard_map/ppermute | solution.py:20
  18.8 3.5 %all-to-all-start = ((bf16[4,400,128]{2,1,0:T(8,128)(2,1)}), bf16[4,400,128]{2,1,0:T(8,128)(2,1)S(1)}, u32[]{:S(2)}, u32[]{:S(2)}) async-start(bf16[4,400,128]{2,1,0:T(8,128)(2,1)} %broadcast_in_dim.44), calls=%async_computation | async-start | bytes 819200 | tf_op jit(solution)/shard_map/all_to_all | solution.py:34
  23.7 3.8 %select_select_fusion = s32[1206]{0:T(1024)S(1)} fusion(pred[1206]{0:T(1024)(128)(4,1)S(1)} %copy-done.12, pred[1206]{0:T(1024)(128)(4,1)S(1)} %copy-done.13, pred[1206]{0:T(1024)(128)(4,1)S(1)} %copy-done.14, pred[1206]{0:T(1024)(128)(4,1)S(1)} %copy-done.15, pred[1206]{0:T(1024)(128)(4,1)S(1)} %copy-done.16, s32[]{:T(128)} %bitcast.7, s32[]{:T(128)} %bitcast.2, ...), kind=kLoop, calls=%fused_computation.100 | loop fusion | flops 6030 | bytes 10878 | tf_op jit(solution)/shard_map/jit(_take)/gather | solution.py:59
  27.5 28.4 %all-to-all-done = bf16[4,400,128]{2,1,0:T(8,128)(2,1)S(1)} async-done(((bf16[4,400,128]{2,1,0:T(8,128)(2,1)}), bf16[4,400,128]{2,1,0:T(8,128)(2,1)S(1)}, u32[]{:S(2)}, u32[]{:S(2)}) %all-to-all-start) | async-done | bytes 409632 | tf_op jit(solution)/shard_map/all_to_all | solution.py:34
  56.6 1.6 copy.48
  58.1 10.0 %all-to-all-start.1 = ((bf16[8,64,1024]{2,1,0:T(8,128)(2,1)}), bf16[8,64,1024]{2,1,0:T(8,128)(2,1)}, u32[]{:S(2)}, u32[]{:S(2)}) async-start(bf16[8,64,1024]{2,1,0:T(8,128)(2,1)} %copy.48), calls=%async_computation.1 | async-start | bytes 2097152 | tf_op jit(solution)/shard_map/all_to_all | solution.py:116
  68.3 1.3 fusion.89
  70.7 1.5 fusion.14
  72.3 4.4 %collective-permute-start.1 = (bf16[384,128]{1,0:T(8,128)(2,1)S(1)}, bf16[384,128]{1,0:T(8,128)(2,1)S(1)}, u32[]{:S(2)}, u32[]{:S(2)}) collective-permute-start(bf16[384,128]{1,0:T(8,128)(2,1)S(1)} %get-tuple-element.51), channel_id=1, source_target_pairs={{0,64},{64,128},{128,192},{192,0},{1,65},{65,129},{129,193},{193,1... | collective-permute-start | bytes 294920 | tf_op jit(solution)/shard_map/ppermute | solution.py:25
  76.7 3.6 %collective-permute-start.2 = (bf16[384,128]{1,0:T(8,128)(2,1)S(1)}, bf16[384,128]{1,0:T(8,128)(2,1)S(1)}, u32[]{:S(2)}, u32[]{:S(2)}) collective-permute-start(bf16[384,128]{1,0:T(8,128)(2,1)S(1)} %get-tuple-element.53), channel_id=1, source_target_pairs={{0,128},{64,192},{128,0},{192,64},{1,129},{65,193},{129,1},{193,65... | collective-permute-start | bytes 294920 | tf_op jit(solution)/shard_map/ppermute | solution.py:25
  80.3 1.9 collective-permute-start.6
  82.2 4.6 %collective-permute-start.7 = (bf16[128,4096]{1,0:T(8,128)(2,1)S(1)}, bf16[128,4096]{1,0:T(8,128)(2,1)S(1)}, u32[]{:S(2)}, u32[]{:S(2)}) collective-permute-start(bf16[128,4096]{1,0:T(8,128)(2,1)S(1)} %bitcast.87), channel_id=1, source_target_pairs={{0,192},{64,0},{128,64},{192,128},{1,193},{65,1},{129,65},{193,129... | collective-permute-start | bytes 3145736 | tf_op jit(solution)/shard_map/ppermute | solution.py:25
  86.9 1.9 collective-permute-start.3
  88.8 19.0 %collective-permute-done.3 = bf16[384,128]{1,0:T(8,128)(2,1)S(1)} collective-permute-done((bf16[384,128]{1,0:T(8,128)(2,1)S(1)}, bf16[384,128]{1,0:T(8,128)(2,1)S(1)}, u32[]{:S(2)}, u32[]{:S(2)}) %collective-permute-start.3) | collective-permute-done | bytes 98336 | tf_op jit(solution)/shard_map/ppermute | solution.py:25
  108.8 20.0 %all_gather.3 = bf16[384,1024]{1,0:T(8,128)(2,1)S(1)} all-gather(bf16[384,128]{1,0:T(8,128)(2,1)S(1)} %fusion.57), channel_id=1, replica_groups=mesh['yh'=2,'x'=4,'z'=8,'yl'=4,'core'=2] {'yl','core'}, dimensions={1}, use_global_device_ids=true | all-gather | bytes 884736 | tf_op jit(solution)/shard_map/all_gather | solution.py:129
  128.8 2.7 %convolution_convert_fusion = bf16[512,384]{1,0:T(8,128)(2,1)} fusion(bf16[512,1024]{1,0:T(8,128)(2,1)} %bitcast.15, bf16[384,1024]{1,0:T(8,128)(2,1)S(1)} %all_gather.3), kind=kOutput, calls=%fused_computation.36 | convolution fusion | flops 402849792 | bytes 2228224 | tf_op jit(solution)/shard_map/dot_general | solution.py:130
  131.5 6.7 %all-to-all-start.2 = ((bf16[8,64,384]{2,1,0:T(8,128)(2,1)}), bf16[8,64,384]{2,1,0:T(8,128)(2,1)S(1)}, u32[]{:S(2)}, u32[]{:S(2)}) async-start(bf16[8,64,384]{2,1,0:T(8,128)(2,1)} %bitcast.18), calls=%async_computation.2 | async-start | bytes 786432 | tf_op jit(solution)/shard_map/all_to_all | solution.py:139
  139.2 14.1 %all-to-all-done.2 = bf16[8,64,384]{2,1,0:T(8,128)(2,1)S(1)} async-done(((bf16[8,64,384]{2,1,0:T(8,128)(2,1)}), bf16[8,64,384]{2,1,0:T(8,128)(2,1)S(1)}, u32[]{:S(2)}, u32[]{:S(2)}) %all-to-all-start.2) | async-done | bytes 393248 | tf_op jit(solution)/shard_map/all_to_all | solution.py:139
  153.4 1.1 fusion.10
  155.2 1.6 reshape.195
  156.8 8.4 %all-to-all-start.3 = ((bf16[128,2,1152]{2,1,0:T(2,128)(2,1)}), bf16[128,2,1152]{2,1,0:T(2,128)(2,1)S(1)}, u32[]{:S(2)}, u32[]{:S(2)}) async-start(bf16[128,2,1152]{2,1,0:T(2,128)(2,1)} %reshape.195), calls=%async_computation.3 | async-start | bytes 1179648 | tf_op jit(solution)/shard_map/all_to_all | solution.py:149
  165.2 2.7 %slice.114 = bf16[2048,2,128]{2,1,0:T(2,128)(2,1)} slice(bf16[4096,2,128]{2,1,0:T(2,128)(2,1)} %collective-permute-done.5), slice={[2048:4096], [0:2], [0:128]} | slice | bytes 2097152 | tf_op jit(solution)/shard_map/slice | solution.py:137
  167.9 5.3 %collective-permute-start.9 = (bf16[2048,2,128]{2,1,0:T(2,128)(2,1)}, bf16[2048,2,128]{2,1,0:T(2,128)(2,1)}, u32[]{:S(2)}, u32[]{:S(2)}) collective-permute-start(bf16[2048,2,128]{2,1,0:T(2,128)(2,1)} %slice.114), channel_id=1, source_target_pairs={{0,192},{64,0},{128,64},{192,128},{1,193},{65,1},{129,65},{193,129... | collective-permute-start | bytes 3145736 | tf_op jit(solution)/shard_map/ppermute | solution.py:25
  173.2 2.6 slice.112
  175.8 1.9 collective-permute-start.8
  178.5 1.9 collective-permute-start.10
  181.3 4.6 %collective-permute-start.11 = (bf16[64,4096]{1,0:T(8,128)(2,1)}, bf16[64,4096]{1,0:T(8,128)(2,1)}, u32[]{:S(2)}, u32[]{:S(2)}) collective-permute-start(bf16[64,4096]{1,0:T(8,128)(2,1)} %slice.118), channel_id=1, source_target_pairs={{0,192},{64,0},{128,64},{192,128},{1,193},{65,1},{129,65},{193,129... | collective-permute-start | bytes 1572872 | tf_op jit(solution)/shard_map/ppermute | solution.py:25
  186.3 1.1 reshape.196
  187.4 1.7 copy.56
  189.1 2.1 copy.53
  191.2 2.2 reshape.168
  193.9 2.2 fusion.22
  196.1 1.5 fusion.39
  197.9 2.1 fusion.16
  200.0 2.2 fusion.19
  202.7 1.5 convolution_add_fusion.2
  204.5 9.4 %collective-permute-done.10 = bf16[64,4096]{1,0:T(8,128)(2,1)} collective-permute-done((bf16[64,4096]{1,0:T(8,128)(2,1)}, bf16[64,4096]{1,0:T(8,128)(2,1)}, u32[]{:S(2)}, u32[]{:S(2)}) %collective-permute-start.10) | collective-permute-done | bytes 524320 | tf_op jit(solution)/shard_map/ppermute | solution.py:25
  213.9 1.5 fusion.44
  215.8 1.3 reshape.173
  217.9 1.6 copy.57
  219.6 1.6 reshape.197
  221.2 15.6 %all-to-all-start.4 = ((bf16[128,2,1152]{2,1,0:T(2,128)(2,1)}), bf16[128,2,1152]{2,1,0:T(2,128)(2,1)S(1)}, u32[]{:S(2)}, u32[]{:S(2)}) async-start(bf16[128,2,1152]{2,1,0:T(2,128)(2,1)} %reshape.197), calls=%async_computation.4 | async-start | bytes 1179648 | tf_op jit(solution)/shard_map/all_to_all | solution.py:171
  236.9 21.0 %all-to-all-done.4 = bf16[128,2,1152]{2,1,0:T(2,128)(2,1)S(1)} async-done(((bf16[128,2,1152]{2,1,0:T(2,128)(2,1)}), bf16[128,2,1152]{2,1,0:T(2,128)(2,1)S(1)}, u32[]{:S(2)}, u32[]{:S(2)}) %all-to-all-start.4) | async-done | bytes 589856 | tf_op jit(solution)/shard_map/all_to_all | solution.py:171
  257.9 1.1 reshape.198
  261.1 1.5 fusion.38
  (99 shorter events, 15.6 us)
Async XLA Ops:
  0.0 23.6 %copy-start.12 = (pred[1206]{0:T(1024)(128)(4,1)S(1)}, pred[1206]{0:T(1024)(128)(4,1)}, u32[]{:S(2)}) copy-start(pred[1206]{0:T(1024)(128)(4,1)} %constant.207) | copy-start | bytes 3622
  0.0 23.6 %copy-start.13 = (pred[1206]{0:T(1024)(128)(4,1)S(1)}, pred[1206]{0:T(1024)(128)(4,1)}, u32[]{:S(2)}) copy-start(pred[1206]{0:T(1024)(128)(4,1)} %constant.208) | copy-start | bytes 3622
  0.0 23.6 %copy-start.14 = (pred[1206]{0:T(1024)(128)(4,1)S(1)}, pred[1206]{0:T(1024)(128)(4,1)}, u32[]{:S(2)}) copy-start(pred[1206]{0:T(1024)(128)(4,1)} %constant.209) | copy-start | bytes 3622
  0.0 23.6 %copy-start.15 = (pred[1206]{0:T(1024)(128)(4,1)S(1)}, pred[1206]{0:T(1024)(128)(4,1)}, u32[]{:S(2)}) copy-start(pred[1206]{0:T(1024)(128)(4,1)} %constant.210) | copy-start | bytes 3622
  0.0 23.6 %copy-start.16 = (pred[1206]{0:T(1024)(128)(4,1)S(1)}, pred[1206]{0:T(1024)(128)(4,1)}, u32[]{:S(2)}) copy-start(pred[1206]{0:T(1024)(128)(4,1)} %constant.211) | copy-start | bytes 3622
  0.0 131.5 %collective-permute-start.4 = (bf16[4096,2,128]{2,1,0:T(2,128)(2,1)}, bf16[4096,2,128]{2,1,0:T(2,128)(2,1)}, u32[]{:S(2)}, u32[]{:S(2)}) collective-permute-start(bf16[4096,2,128]{2,1,0:T(2,128)(2,1)} %bitcast.91), channel_id=1, source_target_pairs={{0,64},{64,128},{128,192},{192,0},{1,65},{65,129},{129,193},{193,1... | collective-permute-start | bytes 6291464 | tf_op jit(solution)/shard_map/ppermute | solution.py:25
  4.1 127.4 %collective-permute-start.5 = (bf16[4096,2,128]{2,1,0:T(2,128)(2,1)}, bf16[4096,2,128]{2,1,0:T(2,128)(2,1)}, u32[]{:S(2)}, u32[]{:S(2)}) collective-permute-start(bf16[4096,2,128]{2,1,0:T(2,128)(2,1)} %bitcast.92), channel_id=1, source_target_pairs={{0,192},{64,0},{128,64},{192,128},{1,193},{65,1},{129,65},{193,129... | collective-permute-start | bytes 6291464 | tf_op jit(solution)/shard_map/ppermute | solution.py:25
  7.3 48.6 %copy-start.3 = (bf16[8192,64]{0,1:T(8,128)(2,1)S(1)}, bf16[8192,64]{0,1:T(8,128)(2,1)}, u32[]{:S(2)}) copy-start(bf16[8192,64]{0,1:T(8,128)(2,1)} %param.24) | copy-start | bytes 3145732
  8.6 59.7 %collective-permute-start = (bf16[1206,128]{1,0:T(8,128)(2,1)S(1)}, bf16[1206,128]{1,0:T(8,128)(2,1)S(1)}, u32[]{:S(2)}, u32[]{:S(2)}) collective-permute-start(bf16[1206,128]{1,0:T(8,128)(2,1)S(1)} %pad_maximum_fusion), channel_id=1, source_target_pairs={{0,256},{256,0},{1,257},{257,1},{2,258},{258,2},{3,259},{259,3},{4... | collective-permute-start | bytes 926216 | tf_op jit(solution)/shard_map/ppermute | solution.py:20
  18.8 37.1 %all-to-all-start = ((bf16[4,400,128]{2,1,0:T(8,128)(2,1)}), bf16[4,400,128]{2,1,0:T(8,128)(2,1)S(1)}, u32[]{:S(2)}, u32[]{:S(2)}) async-start(bf16[4,400,128]{2,1,0:T(8,128)(2,1)} %broadcast_in_dim.44), calls=%async_computation | async-start | bytes 819200 | tf_op jit(solution)/shard_map/all_to_all | solution.py:34
  58.1 50.6 %all-to-all-start.1 = ((bf16[8,64,1024]{2,1,0:T(8,128)(2,1)}), bf16[8,64,1024]{2,1,0:T(8,128)(2,1)}, u32[]{:S(2)}, u32[]{:S(2)}) async-start(bf16[8,64,1024]{2,1,0:T(8,128)(2,1)} %copy.48), calls=%async_computation.1 | async-start | bytes 2097152 | tf_op jit(solution)/shard_map/all_to_all | solution.py:116
  70.7 9.6 %copy-start.4 = (bf16[1,128,4096]{2,1,0:T(8,128)(2,1)S(1)}, bf16[1,128,4096]{2,1,0:T(8,128)(2,1)}, u32[]{:S(2)}) copy-start(bf16[1,128,4096]{2,1,0:T(8,128)(2,1)} %param.29) | copy-start | bytes 3145732
  72.2 14.6 %copy-start.6 = (bf16[1536,128]{1,0:T(8,128)(2,1)}, bf16[1536,128]{1,0:T(8,128)(2,1)S(1)}, u32[]{:S(2)}) copy-start(bf16[1536,128]{1,0:T(8,128)(2,1)S(1)} %fusion.14) | copy-start | bytes 1179652
  72.3 10.0 %collective-permute-start.1 = (bf16[384,128]{1,0:T(8,128)(2,1)S(1)}, bf16[384,128]{1,0:T(8,128)(2,1)S(1)}, u32[]{:S(2)}, u32[]{:S(2)}) collective-permute-start(bf16[384,128]{1,0:T(8,128)(2,1)S(1)} %get-tuple-element.51), channel_id=1, source_target_pairs={{0,64},{64,128},{128,192},{192,0},{1,65},{65,129},{129,193},{193,1... | collective-permute-start | bytes 294920 | tf_op jit(solution)/shard_map/ppermute | solution.py:25
  76.7 10.2 %collective-permute-start.2 = (bf16[384,128]{1,0:T(8,128)(2,1)S(1)}, bf16[384,128]{1,0:T(8,128)(2,1)S(1)}, u32[]{:S(2)}, u32[]{:S(2)}) collective-permute-start(bf16[384,128]{1,0:T(8,128)(2,1)S(1)} %get-tuple-element.53), channel_id=1, source_target_pairs={{0,128},{64,192},{128,0},{192,64},{1,129},{65,193},{129,1},{193,65... | collective-permute-start | bytes 294920 | tf_op jit(solution)/shard_map/ppermute | solution.py:25
  80.3 51.2 %collective-permute-start.6 = (bf16[128,4096]{1,0:T(8,128)(2,1)S(1)}, bf16[128,4096]{1,0:T(8,128)(2,1)S(1)}, u32[]{:S(2)}, u32[]{:S(2)}) collective-permute-start(bf16[128,4096]{1,0:T(8,128)(2,1)S(1)} %bitcast.86), channel_id=1, source_target_pairs={{0,64},{64,128},{128,192},{192,0},{1,65},{65,129},{129,193},{193,1... | collective-permute-start | bytes 3145736 | tf_op jit(solution)/shard_map/ppermute | solution.py:25
  82.2 49.3 %collective-permute-start.7 = (bf16[128,4096]{1,0:T(8,128)(2,1)S(1)}, bf16[128,4096]{1,0:T(8,128)(2,1)S(1)}, u32[]{:S(2)}, u32[]{:S(2)}) collective-permute-start(bf16[128,4096]{1,0:T(8,128)(2,1)S(1)} %bitcast.87), channel_id=1, source_target_pairs={{0,192},{64,0},{128,64},{192,128},{1,193},{65,1},{129,65},{193,129... | collective-permute-start | bytes 3145736 | tf_op jit(solution)/shard_map/ppermute | solution.py:25
  86.9 21.0 %collective-permute-start.3 = (bf16[384,128]{1,0:T(8,128)(2,1)S(1)}, bf16[384,128]{1,0:T(8,128)(2,1)S(1)}, u32[]{:S(2)}, u32[]{:S(2)}) collective-permute-start(bf16[384,128]{1,0:T(8,128)(2,1)S(1)} %get-tuple-element.52), channel_id=1, source_target_pairs={{0,192},{64,0},{128,64},{192,128},{1,193},{65,1},{129,65},{193,129... | collective-permute-start | bytes 294920 | tf_op jit(solution)/shard_map/ppermute | solution.py:25
  108.8 29.4 %copy-start.10 = (s32[384,2]{0,1:T(2,128)S(1)}, s32[384,2]{0,1:T(2,128)}, u32[]{:S(2)}) copy-start(s32[384,2]{0,1:T(2,128)} %param.26) | copy-start | bytes 9220
  128.8 10.4 %copy-start.19 = (f32[64]{0:T(128)S(1)}, f32[64]{0:T(128)}, u32[]{:S(2)}) copy-start(f32[64]{0:T(128)} %param.23) | copy-start | bytes 772
  131.5 21.9 %copy-start.17 = (bf16[384,64]{0,1:T(8,128)(2,1)S(1)}, bf16[384,64]{0,1:T(8,128)(2,1)}, u32[]{:S(2)}) copy-start(bf16[384,64]{0,1:T(8,128)(2,1)} %param.17) | copy-start | bytes 147460
  131.5 21.9 %copy-start = (bf16[128,4096]{1,0:T(8,128)(2,1)}, bf16[128,4096]{1,0:T(8,128)(2,1)S(1)}, u32[]{:S(2)}) copy-start(bf16[128,4096]{1,0:T(8,128)(2,1)S(1)} %collective-permute-done.6) | copy-start | bytes 3145732
  131.5 21.8 %all-to-all-start.2 = ((bf16[8,64,384]{2,1,0:T(8,128)(2,1)}), bf16[8,64,384]{2,1,0:T(8,128)(2,1)S(1)}, u32[]{:S(2)}, u32[]{:S(2)}) async-start(bf16[8,64,384]{2,1,0:T(8,128)(2,1)} %bitcast.18), calls=%async_computation.2 | async-start | bytes 786432 | tf_op jit(solution)/shard_map/all_to_all | solution.py:139
  153.4 1.2 copy-start.7
  156.8 29.5 %all-to-all-start.3 = ((bf16[128,2,1152]{2,1,0:T(2,128)(2,1)}), bf16[128,2,1152]{2,1,0:T(2,128)(2,1)S(1)}, u32[]{:S(2)}, u32[]{:S(2)}) async-start(bf16[128,2,1152]{2,1,0:T(2,128)(2,1)} %reshape.195), calls=%async_computation.3 | async-start | bytes 1179648 | tf_op jit(solution)/shard_map/all_to_all | solution.py:149
  165.2 12.5 %copy-start.1 = (bf16[128,4096]{1,0:T(8,128)(2,1)S(1)}, bf16[128,4096]{1,0:T(8,128)(2,1)}, u32[]{:S(2)}) copy-start(bf16[128,4096]{1,0:T(8,128)(2,1)} %copy-done) | copy-start | bytes 3145732
  167.9 28.2 %collective-permute-start.9 = (bf16[2048,2,128]{2,1,0:T(2,128)(2,1)}, bf16[2048,2,128]{2,1,0:T(2,128)(2,1)}, u32[]{:S(2)}, u32[]{:S(2)}) collective-permute-start(bf16[2048,2,128]{2,1,0:T(2,128)(2,1)} %slice.114), channel_id=1, source_target_pairs={{0,192},{64,0},{128,64},{192,128},{1,193},{65,1},{129,65},{193,129... | collective-permute-start | bytes 3145736 | tf_op jit(solution)/shard_map/ppermute | solution.py:25
  175.8 26.9 %collective-permute-start.8 = (bf16[2048,2,128]{2,1,0:T(2,128)(2,1)}, bf16[2048,2,128]{2,1,0:T(2,128)(2,1)}, u32[]{:S(2)}, u32[]{:S(2)}) collective-permute-start(bf16[2048,2,128]{2,1,0:T(2,128)(2,1)} %slice.112), channel_id=1, source_target_pairs={{0,64},{64,128},{128,192},{192,0},{1,65},{65,129},{129,193},{193,1... | collective-permute-start | bytes 3145736 | tf_op jit(solution)/shard_map/ppermute | solution.py:25
  178.5 35.4 %collective-permute-start.10 = (bf16[64,4096]{1,0:T(8,128)(2,1)}, bf16[64,4096]{1,0:T(8,128)(2,1)}, u32[]{:S(2)}, u32[]{:S(2)}) collective-permute-start(bf16[64,4096]{1,0:T(8,128)(2,1)} %slice.117), channel_id=1, source_target_pairs={{0,64},{64,128},{128,192},{192,0},{1,65},{65,129},{129,193},{193,1... | collective-permute-start | bytes 1572872 | tf_op jit(solution)/shard_map/ppermute | solution.py:25
  181.3 32.6 %collective-permute-start.11 = (bf16[64,4096]{1,0:T(8,128)(2,1)}, bf16[64,4096]{1,0:T(8,128)(2,1)}, u32[]{:S(2)}, u32[]{:S(2)}) collective-permute-start(bf16[64,4096]{1,0:T(8,128)(2,1)} %slice.118), channel_id=1, source_target_pairs={{0,192},{64,0},{128,64},{192,128},{1,193},{65,1},{129,65},{193,129... | collective-permute-start | bytes 1572872 | tf_op jit(solution)/shard_map/ppermute | solution.py:25
  189.1 4.5 %copy-start.9 = (f32[4096]{0:T(1024)S(1)}, f32[4096]{0:T(1024)}, u32[]{:S(2)}) copy-start(f32[4096]{0:T(1024)} %param.25) | copy-start | bytes 49156
  193.9 3.7 %copy-start.5 = (bf16[1,128,4096]{2,1,0:T(8,128)(2,1)S(1)}, bf16[1,128,4096]{2,1,0:T(8,128)(2,1)}, u32[]{:S(2)}) copy-start(bf16[1,128,4096]{2,1,0:T(8,128)(2,1)} %param.29) | copy-start | bytes 3145732
  200.0 4.2 %copy-start.2 = (bf16[128,4096]{1,0:T(8,128)(2,1)S(1)}, bf16[128,4096]{1,0:T(8,128)(2,1)}, u32[]{:S(2)}) copy-start(bf16[128,4096]{1,0:T(8,128)(2,1)} %copy-done) | copy-start | bytes 3145732
  219.6 17.2 %copy-start.11 = (s32[384,2]{0,1:T(2,128)S(1)}, s32[384,2]{0,1:T(2,128)}, u32[]{:S(2)}) copy-start(s32[384,2]{0,1:T(2,128)} %param.27) | copy-start | bytes 9220
  221.2 36.7 %all-to-all-start.4 = ((bf16[128,2,1152]{2,1,0:T(2,128)(2,1)}), bf16[128,2,1152]{2,1,0:T(2,128)(2,1)S(1)}, u32[]{:S(2)}, u32[]{:S(2)}) async-start(bf16[128,2,1152]{2,1,0:T(2,128)(2,1)} %reshape.197), calls=%async_computation.4 | async-start | bytes 1179648 | tf_op jit(solution)/shard_map/all_to_all | solution.py:171
  259.5 1.6 copy-start.8
  259.5 1.6 copy-start.18

commit v3 on v2

--- a/solution.py
+++ b/solution.py
@@ -52,20 +52,19 @@
     return selectors, weights
 
 
-def attention(queries, keys, values, slot, frame_ids, frame_rows):
+def attention(queries, keys, values, local_frame, frame_rows):
     width = keys.shape[0]
     scale = 1.0 / math.sqrt(queries.shape[1])
     scores = lax.dot_general(queries, keys, (((1,), (1,)), ((), ())), preferred_element_type=f32) * scale
-    column_frame = jnp.repeat(frame_ids, frame_rows, total_repeat_length=width)
-    inside = column_frame[None, :] == slot[:, None]
+    column_frame = lax.broadcasted_iota(jnp.int32, (1, width), 1) // frame_rows
+    inside = column_frame == local_frame[:, None]
     scores = jnp.where(inside, scores, MASKED_SCORE)
     row_max = jnp.max(scores, axis=1, keepdims=True)
     expon = jnp.exp(scores - row_max)
     row_total = jnp.sum(expon, axis=1, keepdims=True)
     probability = (expon / row_total).astype(bf16)
     mixed = jnp.dot(probability, values, preferred_element_type=f32)
-    present = jnp.any(frame_ids[None, :] == slot[:, None], axis=1, keepdims=True)
-    return jnp.where(present, mixed, 0.0).astype(bf16)
+    return jnp.where(local_frame[:, None] >= 0, mixed, 0.0).astype(bf16)
 
 
 def per_device(
@@ -91,8 +90,6 @@
     feats = hidden_in.shape[1]
     yh, x, z = lax.axis_index("yh"), lax.axis_index("x"), lax.axis_index("z")
     held, frame_rows = frame_keys.shape[0], frame_keys.shape[1]
-    in_left, in_right = shift(w_in[0], "x", 1), shift(w_in[0], "x", -1)
-    down_left, down_right = shift(w_down[0], "x", 1), shift(w_down[0], "x", -1)
     own = jnp.concatenate(
         [
             lax.dynamic_slice_in_dim(frame_keys, z * head, head, 2).reshape(held * frame_rows, head),
@@ -111,34 +108,63 @@
     )
     packed = jnp.concatenate([queries, slot_rows])
     gathered = spread(packed, "x")
-    gathered, turned = tie(gathered, out_weight.T)
+    half_in, half_down = w_in.shape[1] // 2, w_down.shape[1] // 2
+    gathered, turned, down_0, down_1 = tie(
+        gathered, out_weight.T, w_down[0, :half_down], w_down[0, half_down:]
+    )
+    left_down_0, right_down_1 = shift(down_0, "x", 1), shift(down_1, "x", -1)
     turned = turned.reshape(feats, nz, near * head).transpose(1, 0, 2)
     near_weight = lax.all_to_all(turned, "z", 0, 0, tiled=True).reshape(nz * feats, near * head)
     all_queries = gathered[:, :tokens].reshape(nx * tokens, head)
     all_slots = gathered[:, tokens : tokens + tokens // head].reshape(nx * tokens).astype(jnp.int32)
-    frame_ids = jnp.concatenate(
-        [held * (h * nx + x) + jnp.arange(held, dtype=jnp.int32) for h in (yh, 1 - yh)]
-    )
-    mixed = attention(all_queries, keys, values, all_slots, frame_ids, frame_rows)
+    own_frame = all_slots - held * (yh * nx + x)
+    other_frame = all_slots - held * ((1 - yh) * nx + x)
+    local_frame = jnp.where(
+        (own_frame >= 0) & (own_frame < held),
+        own_frame,
+        jnp.where((other_frame >= 0) & (other_frame < held), other_frame + held, -1),
+    )
+    mixed = attention(all_queries, keys, values, local_frame, frame_rows)
     back = mixed.reshape(nx, tokens, head)
     attended = lax.dynamic_index_in_dim(back, x, 0, keepdims=False).astype(f32)
     for k in range(1, nx):
         piece = lax.dynamic_index_in_dim(back, (x + k) % nx, 0, keepdims=False)
         attended = attended + shift(piece, "x", k).astype(f32)
-    attended, near_weight = tie(attended.astype(bf16), near_weight)
+    attended, near_weight, left_down_0, right_down_1 = tie(
+        attended.astype(bf16), near_weight, left_down_0, right_down_1
+    )
+    quarter = half_in // 2
+    attended, in_0, in_1, in_q1, in_q2 = tie(
+        attended,
+        w_in[0, :half_in],
+        w_in[0, half_in:],
+        w_in[0, quarter:half_in],
+        w_in[0, half_in : half_in + quarter],
+    )
+    left_in_0, right_in_1 = shift(in_0, "x", 1), shift(in_1, "x", -1)
+    left_in_q2, right_in_q1 = shift(in_q2, "x", 1), shift(in_q1, "x", -1)
     heads = lax.all_gather(attended, NEAR, axis=1, tiled=True)
     partial = lax.dot_general(
         near_weight, heads, (((1,), (1,)), ((), ())), preferred_element_type=f32
     ).astype(bf16)
-    partial, in_left, in_right, down_left, down_right = tie(
-        partial, in_left, in_right, down_left, down_right
-    )
-    half_in, half_down = w_in.shape[1] // 2, w_down.shape[1] // 2
-    in_far = shift(in_left[:half_in], "x", 1), shift(in_right[half_in:], "x", -1)
-    down_far = shift(down_left[:half_down], "x", 1), shift(down_right[half_down:], "x", -1)
+    partial, left_in_0, right_in_1 = tie(partial, left_in_0, right_in_1)
     parts = lax.all_to_all(partial.reshape(nz, feats, tokens), "z", 0, 0, tiled=True)
     projected = jnp.sum(parts.astype(f32), axis=0)
     mid = (hidden_in.T.astype(f32) + jnp.tanh(attn_gate)[:, None] * projected).astype(bf16)
+    mid, left_in_0, right_in_1, left_in_q2, right_in_q1, down_0, down_1, in_q0, in_q3 = tie(
+        mid,
+        left_in_0,
+        right_in_1,
+        left_in_q2,
+        right_in_q1,
+        down_0,
+        down_1,
+        w_in[0, :quarter],
+        w_in[0, half_in + quarter :],
+    )
+    left_in_q3, right_in_q0 = shift(in_q3, "x", 1), shift(in_q0, "x", -1)
+    far_in_0, far_in_1 = shift(left_in_0, "x", 1), shift(right_in_1, "x", -1)
+    left_down_1, right_down_0 = shift(down_1, "x", 1), shift(down_0, "x", -1)
     capacity = 6 * tokens // experts
     selectors, weights = route_tables(expert_ids, gate_fixed, experts, capacity)
     select_rows = (selectors[0] | selectors[1]).astype(bf16)
@@ -148,7 +174,10 @@
     sent = jnp.broadcast_to(sent.reshape(1, experts, capacity, feats), (nh, experts, capacity, feats))
     came = lax.all_to_all(sent.reshape(-1, capacity, feats), BOTH, 0, 0, tiled=True)
     rows = came.reshape(nh, experts, capacity, feats).transpose(0, 2, 1, 3)
-    (rows,) = tie(rows.reshape(nh * capacity, experts * feats))
+    rows, left_down_0, right_down_1 = tie(
+        rows.reshape(nh * capacity, experts * feats), left_down_0, right_down_1
+    )
+    far_down_0, far_down_1 = shift(left_down_0, "x", 1), shift(right_down_1, "x", -1)
     wide = rows.astype(f32)
     mean_square = jnp.mean(wide * wide, axis=1, keepdims=True)
     normed = (wide * lax.rsqrt(mean_square + NORM_EPSILON) * mlp_gain).astype(bf16)
@@ -161,10 +190,31 @@
     def gated(gate_up):
         return (jax.nn.silu(gate_up[:, :hidden_units]) * gate_up[:, hidden_units:]).astype(bf16)
 
-    ups = [up(normed, weight) for weight in (w_in[0], in_left, in_right)]
-    ups.append(up(normed[:, :half_in], in_far[0]) + up(normed[:, half_in:], in_far[1]))
+    def up_of(pieces):
+        at, total = 0, 0.0
+        for piece in pieces:
+            total = total + up(normed[:, at : at + piece.shape[0]], piece)
+            at += piece.shape[0]
+        return total
+
+    ups = [
+        up_of(pieces)
+        for pieces in (
+            (w_in[0],),
+            (left_in_0, left_in_q2, left_in_q3),
+            (right_in_q0, right_in_q1, right_in_1),
+            (far_in_0, far_in_1),
+        )
+    ]
     act = [gated(u) for u in ups]
-    weights_down = [w_down[0], down_left, down_right, jnp.concatenate(down_far)]
+    weights_down = [w_down[0]] + [
+        jnp.concatenate(pieces)
+        for pieces in (
+            (left_down_0, left_down_1),
+            (right_down_0, right_down_1),
+            (far_down_0, far_down_1),
+        )
+    ]
     down = sum(jnp.dot(p, w, preferred_element_type=f32) for p, w in zip(act, weights_down))
     (down,) = tie(down.astype(bf16))
     dealt = down.reshape(nh, capacity, experts, feats).transpose(0, 2, 1, 3).reshape(-1, capacity, feats)

time: 264 us -> 260 us (0.985)
  waiting for transfers between devices: 92.9 us -> 56 us
  starting transfers between devices: 89.2 us -> 111 us
  local copies, waits for them, and re-layouts: 29.4 us -> 41.9 us
  blocking collectives: 20 us -> 15.9 us
  matrix products: 21.4 us -> 24.5 us
    all_to_all x1, waiting for transfers between devices: 28.4 us -> 0.01 us  [spread(): lax.all_to_all(jnp.broadcast_to(v[None], (n,) + v.shape), axis, 0, 0, til...]
    ppermute x11 -> x17, starting transfers between devices: 37.4 us -> 57.9 us  [shift(): return lax.ppermute(v, axis, [(i, (i + by) % n) for i in range(n)])]
    ppermute x11 -> x17, waiting for transfers between devices: 28.9 us -> 18.2 us  [shift(): return lax.ppermute(v, axis, [(i, (i + by) % n) for i in range(n)])]
    all_to_all x1, waiting for transfers between devices: 14.1 us -> 3.87 us  [per_device(): lax.all_to_all(partial.reshape(nz, feats, tokens), 'z', 0, 0, tiled=True)]
    all_to_all x1, waiting for transfers between devices: 0.01 us -> 7.91 us  [per_device(): lax.all_to_all(turned, 'z', 0, 0, tiled=True)]
    slice x4 -> x0, local copies, waits for them, and re-layouts: 6.9 us -> none  [the longest x1 2.67 us: per_device(): in_right[half_in:]]
    squeeze x0 -> x3, local copies, waits for them, and re-layouts: none -> 5.88 us  [the longest x1 2.44 us: per_device(): w_in[0, half_in:]]
    all_to_all x1, waiting for transfers between devices: 0.44 us -> 4.99 us  [per_device(): lax.all_to_all(sent.reshape(-1, capacity, feats), BOTH, 0, 0, tiled=True)]
  transfers between devices with their start and end apart: 17 -> 23, of which waited for: 7 -> 11; matrix products, arithmetic and copies ran while one was open for 17% -> 21% of each run, Pallas kernels for 0% -> 0%
where the time goes in v3:
time: 260 us; the launch traced here: 258 us
  starting transfers between devices  111 us (43%)
  waiting for transfers between devices  56 us (22%)
  local copies, waits for them, and re-layouts  41.9 us (16%)
  matrix products  24.5 us (9%)
  blocking collectives  15.9 us (6%)
  other arithmetic  8.02 us (3%)
    ppermute x17, starting transfers between devices, shift(): return lax.ppermute(v, axis, [(i, (i + by) % n) for i in range(n)])  57.9 us
    all_to_all x1, waiting for transfers between devices, per_device(): back_sums = lax.all_to_all(dealt, BOTH, 0, 0, tiled=True)  21 us
    ppermute x17, waiting for transfers between devices, shift(): return lax.ppermute(v, axis, [(i, (i + by) % n) for i in range(n)])  18.2 us
    all_gather x1, blocking collectives, per_device(): heads = lax.all_gather(attended, NEAR, axis=1, tiled=True)  15.9 us
    all_to_all x1, starting transfers between devices, per_device(): back_sums = lax.all_to_all(dealt, BOTH, 0, 0, tiled=True)  15.7 us
    dot_general x9, matrix products, up(): return jnp.dot(part, weight, preferred_element_type=f32)  11.7 us
    all_to_all x1, starting transfers between devices, per_device(): lax.all_to_all(sent.reshape(-1, capacity, feats), BOTH, 0, 0, tiled=True)  11.5 us
    all_to_all x1, starting transfers between devices, per_device(): lax.all_to_all(turned, 'z', 0, 0, tiled=True)  10 us
  transfers between devices with their start and end apart: 23, of which 11 were waited for; matrix products, arithmetic and copies ran while one was open for 21% of the time, Pallas kernels for 0%

profile of v3, /device:TPU:1, one launch (start us, length us, event | category | flops | bytes accessed | tf_op | source)
XLA Modules:
  0.0 257.8 jit_solution(5826240553110278009)
XLA Ops:
  2.6 4.8 %all-to-all-start = ((bf16[4,400,128]{2,1,0:T(8,128)(2,1)}), bf16[4,400,128]{2,1,0:T(8,128)(2,1)S(1)}, u32[]{:S(2)}, u32[]{:S(2)}) async-start(bf16[4,400,128]{2,1,0:T(8,128)(2,1)} %broadcast_in_dim.61), calls=%async_computation | async-start | bytes 819200 | tf_op jit(solution)/shard_map/all_to_all | solution.py:34
  7.4 1.9 constant_dynamic-slice_fusion
  9.3 1.6 reshape.173
  11.0 1.6 reshape.174
  12.6 1.8 pad_maximum_fusion
  14.3 7.4 %collective-permute-start = (bf16[1206,128]{1,0:T(8,128)(2,1)}, bf16[1206,128]{1,0:T(8,128)(2,1)}, u32[]{:S(2)}, u32[]{:S(2)}) collective-permute-start(bf16[1206,128]{1,0:T(8,128)(2,1)} %pad_maximum_fusion), channel_id=1, source_target_pairs={{0,256},{256,0},{1,257},{257,1},{2,258},{258,2},{3,259},{259,3},{4... | collective-permute-start | bytes 926216 | tf_op jit(solution)/shard_map/ppermute | solution.py:20
  23.5 2.4 slice_bitcast_fusion
  28.7 3.4 %collective-permute-start.4 = (bf16[64,4096]{1,0:T(8,128)(2,1)}, bf16[64,4096]{1,0:T(8,128)(2,1)}, u32[]{:S(2)}, u32[]{:S(2)}) collective-permute-start(bf16[64,4096]{1,0:T(8,128)(2,1)} %get-tuple-element.71), channel_id=1, source_target_pairs={{0,64},{64,128},{128,192},{192,0},{1,65},{65,129},{129,193},{193,1... | collective-permute-start | bytes 1572872 | tf_op jit(solution)/shard_map/ppermute | solution.py:25
  32.1 3.1 %collective-permute-start.5 = (bf16[64,4096]{1,0:T(8,128)(2,1)}, bf16[64,4096]{1,0:T(8,128)(2,1)}, u32[]{:S(2)}, u32[]{:S(2)}) collective-permute-start(bf16[64,4096]{1,0:T(8,128)(2,1)} %get-tuple-element.67), channel_id=1, source_target_pairs={{0,192},{64,0},{128,64},{192,128},{1,193},{65,1},{129,65},{193,129... | collective-permute-start | bytes 1572872 | tf_op jit(solution)/shard_map/ppermute | solution.py:25
  35.9 1.6 copy.48
  37.4 10.0 %all-to-all-start.1 = ((bf16[8,64,1024]{2,1,0:T(8,128)(2,1)}), bf16[8,64,1024]{2,1,0:T(8,128)(2,1)S(1)}, u32[]{:S(2)}, u32[]{:S(2)}) async-start(bf16[8,64,1024]{2,1,0:T(8,128)(2,1)} %copy.48), calls=%async_computation.1 | async-start | bytes 2097152 | tf_op jit(solution)/shard_map/all_to_all | solution.py:117
  48.5 2.3 fusion.114
  54.9 2.1 collective-permute-start.1
  57.0 4.3 %collective-permute-start.2 = (bf16[384,128]{1,0:T(8,128)(2,1)}, bf16[384,128]{1,0:T(8,128)(2,1)S(1)}, u32[]{:S(2)}, u32[]{:S(2)}) collective-permute-start(bf16[384,128]{1,0:T(8,128)(2,1)} %get-tuple-element.91), channel_id=1, source_target_pairs={{0,128},{64,192},{128,0},{192,64},{1,129},{65,193},{129,1},{193,65... | collective-permute-start | bytes 294920 | tf_op jit(solution)/shard_map/ppermute | solution.py:25
  61.3 3.1 %collective-permute-start.3 = (bf16[384,128]{1,0:T(8,128)(2,1)S(1)}, bf16[384,128]{1,0:T(8,128)(2,1)S(1)}, u32[]{:S(2)}, u32[]{:S(2)}) collective-permute-start(bf16[384,128]{1,0:T(8,128)(2,1)S(1)} %get-tuple-element.90), channel_id=1, source_target_pairs={{0,192},{64,0},{128,64},{192,128},{1,193},{65,1},{129,65},{193,129... | collective-permute-start | bytes 294920 | tf_op jit(solution)/shard_map/ppermute | solution.py:25
  64.4 2.4 slice_bitcast_fusion.2
  68.7 7.9 %all-to-all-done.1 = bf16[8,64,1024]{2,1,0:T(8,128)(2,1)S(1)} async-done(((bf16[8,64,1024]{2,1,0:T(8,128)(2,1)}), bf16[8,64,1024]{2,1,0:T(8,128)(2,1)S(1)}, u32[]{:S(2)}, u32[]{:S(2)}) %all-to-all-start.1) | async-done | bytes 1048608 | tf_op jit(solution)/shard_map/all_to_all | solution.py:117
  76.7 2.0 collective-permute-start.6
  78.7 4.6 %collective-permute-start.7 = (bf16[2048,2,128]{2,1,0:T(2,128)(2,1)}, bf16[2048,2,128]{2,1,0:T(2,128)(2,1)}, u32[]{:S(2)}, u32[]{:S(2)}) collective-permute-start(bf16[2048,2,128]{2,1,0:T(2,128)(2,1)} %get-tuple-element.53), channel_id=1, source_target_pairs={{0,192},{64,0},{128,64},{192,128},{1,193},{65,1},{129,65},{193,129... | collective-permute-start | bytes 3145736 | tf_op jit(solution)/shard_map/ppermute | solution.py:25
  83.3 15.9 %all_gather.3 = bf16[384,1024]{1,0:T(8,128)(2,1)S(1)} all-gather(bf16[384,128]{1,0:T(8,128)(2,1)S(1)} %fusion.75), channel_id=1, replica_groups=mesh['yh'=2,'x'=4,'z'=8,'yl'=4,'core'=2] {'yl','core'}, dimensions={1}, use_global_device_ids=true | all-gather | bytes 884736 | tf_op jit(solution)/shard_map/all_gather | solution.py:146
  100.7 3.8 %collective-permute-done.6 = bf16[2048,2,128]{2,1,0:T(2,128)(2,1)} collective-permute-done((bf16[2048,2,128]{2,1,0:T(2,128)(2,1)}, bf16[2048,2,128]{2,1,0:T(2,128)(2,1)}, u32[]{:S(2)}, u32[]{:S(2)}) %collective-permute-start.6) | collective-permute-done | bytes 1048608 | tf_op jit(solution)/shard_map/ppermute | solution.py:25
  105.3 3.5 %all-to-all-start.2 = ((bf16[8,64,384]{2,1,0:T(8,128)(2,1)}), bf16[8,64,384]{2,1,0:T(8,128)(2,1)S(1)}, u32[]{:S(2)}, u32[]{:S(2)}) async-start(bf16[8,64,384]{2,1,0:T(8,128)(2,1)} %bitcast.107), calls=%async_computation.2 | async-start | bytes 786432 | tf_op jit(solution)/shard_map/all_to_all | solution.py:151
  109.7 1.9 collective-permute-start.8
  111.7 5.5 %collective-permute-start.9 = (bf16[1024,2,128]{2,1,0:T(2,128)(2,1)S(1)}, bf16[1024,2,128]{2,1,0:T(2,128)(2,1)}, u32[]{:S(2)}, u32[]{:S(2)}) collective-permute-start(bf16[1024,2,128]{2,1,0:T(2,128)(2,1)S(1)} %copy-done.7), channel_id=1, source_target_pairs={{0,192},{64,0},{128,64},{192,128},{1,193},{65,1},{129,65},{193,129... | collective-permute-start | bytes 1572872 | tf_op jit(solution)/shard_map/ppermute | solution.py:25
  117.2 3.9 %all-to-all-done.2 = bf16[8,64,384]{2,1,0:T(8,128)(2,1)S(1)} async-done(((bf16[8,64,384]{2,1,0:T(8,128)(2,1)}), bf16[8,64,384]{2,1,0:T(8,128)(2,1)S(1)}, u32[]{:S(2)}, u32[]{:S(2)}) %all-to-all-start.2) | async-done | bytes 393248 | tf_op jit(solution)/shard_map/all_to_all | solution.py:151
  121.3 4.7 %collective-permute-done.8 = bf16[1024,2,128]{2,1,0:T(2,128)(2,1)} collective-permute-done((bf16[1024,2,128]{2,1,0:T(2,128)(2,1)}, bf16[1024,2,128]{2,1,0:T(2,128)(2,1)}, u32[]{:S(2)}, u32[]{:S(2)}) %collective-permute-start.8) | collective-permute-done | bytes 524320 | tf_op jit(solution)/shard_map/ppermute | solution.py:25
  130.2 1.6 reshape.200
  131.8 11.5 %all-to-all-start.3 = ((bf16[128,2,1152]{2,1,0:T(2,128)(2,1)}), bf16[128,2,1152]{2,1,0:T(2,128)(2,1)}, u32[]{:S(2)}, u32[]{:S(2)}) async-start(bf16[128,2,1152]{2,1,0:T(2,128)(2,1)} %reshape.200), calls=%async_computation.3 | async-start | bytes 1179648 | tf_op jit(solution)/shard_map/all_to_all | solution.py:175
  143.3 5.4 %collective-permute-start.12 = (bf16[1024,2,128]{2,1,0:T(2,128)(2,1)}, bf16[1024,2,128]{2,1,0:T(2,128)(2,1)}, u32[]{:S(2)}, u32[]{:S(2)}) collective-permute-start(bf16[1024,2,128]{2,1,0:T(2,128)(2,1)} %get-tuple-element.68), channel_id=1, source_target_pairs={{0,192},{64,0},{128,64},{192,128},{1,193},{65,1},{129,65},{193,129... | collective-permute-start | bytes 1572872 | tf_op jit(solution)/shard_map/ppermute | solution.py:25
  148.8 1.9 collective-permute-start.10
  150.7 1.9 collective-permute-start.11
  152.6 4.6 %collective-permute-start.15 = (bf16[2048,2,128]{2,1,0:T(2,128)(2,1)}, bf16[2048,2,128]{2,1,0:T(2,128)(2,1)}, u32[]{:S(2)}, u32[]{:S(2)}) collective-permute-start(bf16[2048,2,128]{2,1,0:T(2,128)(2,1)} %collective-permute-done.7), channel_id=1, source_target_pairs={{0,192},{64,0},{128,64},{192,128},{1,193},{65,1},{129,65},{193,129... | collective-permute-start | bytes 3145736 | tf_op jit(solution)/shard_map/ppermute | solution.py:25
  157.2 1.9 collective-permute-start.14
  159.1 5.0 %all-to-all-done.3 = bf16[128,2,1152]{2,1,0:T(2,128)(2,1)} async-done(((bf16[128,2,1152]{2,1,0:T(2,128)(2,1)}), bf16[128,2,1152]{2,1,0:T(2,128)(2,1)}, u32[]{:S(2)}, u32[]{:S(2)}) %all-to-all-start.3) | async-done | bytes 589856 | tf_op jit(solution)/shard_map/all_to_all | solution.py:175
  164.1 2.7 %reshape.201 = bf16[128,36,64]{2,1,0:T(8,128)(2,1)S(1)} reshape(bf16[128,2,1152]{2,1,0:T(2,128)(2,1)} %all-to-all-done.3) | data formatting | bytes 1179648
  166.8 2.9 %copy.56 = bf16[2,64,36,64]{1,0,3,2:T(2,128)(2,1)} copy(bf16[2,64,36,64]{3,2,1,0:T(8,128)(2,1)S(1)} %bitcast.99) | data formatting | bytes 1179648 | tf_op jit(solution)/shard_map/reshape | solution.py:176
  169.7 3.8 %copy.53 = bf16[2,36,64,64]{3,2,1,0:T(8,128)(2,1)} copy(bf16[2,36,64,64]{2,0,3,1:T(2,128)(2,1)} %bitcast.102) | data formatting | bytes 1179648 | tf_op jit(solution)/shard_map/transpose | solution.py:176
  173.5 2.2 reshape.181
  179.0 1.5 convolution_add_fusion.3
  181.8 5.3 %collective-permute-start.13 = (bf16[64,4096]{1,0:T(8,128)(2,1)S(1)}, bf16[64,4096]{1,0:T(8,128)(2,1)S(1)}, u32[]{:S(2)}, u32[]{:S(2)}) collective-permute-start(bf16[64,4096]{1,0:T(8,128)(2,1)S(1)} %copy-done.6), channel_id=1, source_target_pairs={{0,192},{64,0},{128,64},{192,128},{1,193},{65,1},{129,65},{193,129... | collective-permute-start | bytes 1572872 | tf_op jit(solution)/shard_map/ppermute | solution.py:25
  189.2 1.9 collective-permute-start.16
  192.7 4.8 %collective-permute-start.17 = (bf16[64,4096]{1,0:T(8,128)(2,1)}, bf16[64,4096]{1,0:T(8,128)(2,1)S(1)}, u32[]{:S(2)}, u32[]{:S(2)}) collective-permute-start(bf16[64,4096]{1,0:T(8,128)(2,1)} %collective-permute-done.5), channel_id=1, source_target_pairs={{0,192},{64,0},{128,64},{192,128},{1,193},{65,1},{129,65},{193,129... | collective-permute-start | bytes 1572872 | tf_op jit(solution)/shard_map/ppermute | solution.py:25
  201.6 1.5 convolution_add_fusion.2
  203.2 6.0 %collective-permute-done.16 = bf16[64,4096]{1,0:T(8,128)(2,1)S(1)} collective-permute-done((bf16[64,4096]{1,0:T(8,128)(2,1)}, bf16[64,4096]{1,0:T(8,128)(2,1)S(1)}, u32[]{:S(2)}, u32[]{:S(2)}) %collective-permute-start.16) | collective-permute-done | bytes 524320 | tf_op jit(solution)/shard_map/ppermute | solution.py:25
  213.1 1.6 copy.57
  214.8 1.6 reshape.202
  216.3 15.7 %all-to-all-start.4 = ((bf16[128,2,1152]{2,1,0:T(2,128)(2,1)}), bf16[128,2,1152]{2,1,0:T(2,128)(2,1)S(1)}, u32[]{:S(2)}, u32[]{:S(2)}) async-start(bf16[128,2,1152]{2,1,0:T(2,128)(2,1)} %reshape.202), calls=%async_computation.4 | async-start | bytes 1179648 | tf_op jit(solution)/shard_map/all_to_all | solution.py:221
  232.1 21.0 %all-to-all-done.4 = bf16[128,2,1152]{2,1,0:T(2,128)(2,1)S(1)} async-done(((bf16[128,2,1152]{2,1,0:T(2,128)(2,1)}), bf16[128,2,1152]{2,1,0:T(2,128)(2,1)S(1)}, u32[]{:S(2)}, u32[]{:S(2)}) %all-to-all-start.4) | async-done | bytes 589856 | tf_op jit(solution)/shard_map/all_to_all | solution.py:221
  (102 shorter events, 43.2 us)
Async XLA Ops:
  0.0 22.4 %copy-start.1 = (bf16[1,128,4096]{2,1,0:T(8,128)(2,1)S(1)}, bf16[1,128,4096]{2,1,0:T(8,128)(2,1)}, u32[]{:S(2)}) copy-start(bf16[1,128,4096]{2,1,0:T(8,128)(2,1)} %param.27) | copy-start | bytes 3145732
  2.6 23.3 %all-to-all-start = ((bf16[4,400,128]{2,1,0:T(8,128)(2,1)}), bf16[4,400,128]{2,1,0:T(8,128)(2,1)S(1)}, u32[]{:S(2)}, u32[]{:S(2)}) async-start(bf16[4,400,128]{2,1,0:T(8,128)(2,1)} %broadcast_in_dim.61), calls=%async_computation | async-start | bytes 819200 | tf_op jit(solution)/shard_map/all_to_all | solution.py:34
  7.4 16.0 %copy-start = (bf16[1,4096,2,128]{3,2,1,0:T(2,128)(2,1)S(1)}, bf16[1,4096,2,128]{3,2,1,0:T(2,128)(2,1)}, u32[]{:S(2)}) copy-start(bf16[1,4096,2,128]{3,2,1,0:T(2,128)(2,1)} %param.26) | copy-start | bytes 6291460
  14.3 33.1 %collective-permute-start = (bf16[1206,128]{1,0:T(8,128)(2,1)}, bf16[1206,128]{1,0:T(8,128)(2,1)}, u32[]{:S(2)}, u32[]{:S(2)}) collective-permute-start(bf16[1206,128]{1,0:T(8,128)(2,1)} %pad_maximum_fusion), channel_id=1, source_target_pairs={{0,256},{256,0},{1,257},{257,1},{2,258},{258,2},{3,259},{259,3},{4... | collective-permute-start | bytes 926216 | tf_op jit(solution)/shard_map/ppermute | solution.py:20
  23.5 11.8 %copy-start.3 = (bf16[8192,64]{0,1:T(8,128)(2,1)S(1)}, bf16[8192,64]{0,1:T(8,128)(2,1)}, u32[]{:S(2)}) copy-start(bf16[8192,64]{0,1:T(8,128)(2,1)} %param.22) | copy-start | bytes 3145732
  28.7 40.0 %collective-permute-start.4 = (bf16[64,4096]{1,0:T(8,128)(2,1)}, bf16[64,4096]{1,0:T(8,128)(2,1)}, u32[]{:S(2)}, u32[]{:S(2)}) collective-permute-start(bf16[64,4096]{1,0:T(8,128)(2,1)} %get-tuple-element.71), channel_id=1, source_target_pairs={{0,64},{64,128},{128,192},{192,0},{1,65},{65,129},{129,193},{193,1... | collective-permute-start | bytes 1572872 | tf_op jit(solution)/shard_map/ppermute | solution.py:25
  32.1 36.6 %collective-permute-start.5 = (bf16[64,4096]{1,0:T(8,128)(2,1)}, bf16[64,4096]{1,0:T(8,128)(2,1)}, u32[]{:S(2)}, u32[]{:S(2)}) collective-permute-start(bf16[64,4096]{1,0:T(8,128)(2,1)} %get-tuple-element.67), channel_id=1, source_target_pairs={{0,192},{64,0},{128,64},{192,128},{1,193},{65,1},{129,65},{193,129... | collective-permute-start | bytes 1572872 | tf_op jit(solution)/shard_map/ppermute | solution.py:25
  35.8 12.7 %copy-start.5 = (bf16[603,128]{1,0:T(8,128)(2,1)S(1)}, bf16[603,128]{1,0:T(8,128)(2,1)}, u32[]{:S(2)}) copy-start(bf16[603,128]{1,0:T(8,128)(2,1)} %reshape.173) | copy-start | bytes 463108
  35.9 12.7 %copy-start.12 = (s32[1206]{0:T(1024)S(1)}, s32[1206]{0:T(1024)}, u32[]{:S(2)}) copy-start(s32[1206]{0:T(1024)} %add_select_fusion) | copy-start | bytes 14476
  37.4 39.2 %all-to-all-start.1 = ((bf16[8,64,1024]{2,1,0:T(8,128)(2,1)}), bf16[8,64,1024]{2,1,0:T(8,128)(2,1)S(1)}, u32[]{:S(2)}, u32[]{:S(2)}) async-start(bf16[8,64,1024]{2,1,0:T(8,128)(2,1)} %copy.48), calls=%async_computation.1 | async-start | bytes 2097152 | tf_op jit(solution)/shard_map/all_to_all | solution.py:117
  50.8 1.1 copy-start.4
  53.4 0.8 copy-start.8
  54.9 11.9 %collective-permute-start.1 = (bf16[384,128]{1,0:T(8,128)(2,1)}, bf16[384,128]{1,0:T(8,128)(2,1)S(1)}, u32[]{:S(2)}, u32[]{:S(2)}) collective-permute-start(bf16[384,128]{1,0:T(8,128)(2,1)} %get-tuple-element.89), channel_id=1, source_target_pairs={{0,64},{64,128},{128,192},{192,0},{1,65},{65,129},{129,193},{193,1... | collective-permute-start | bytes 294920 | tf_op jit(solution)/shard_map/ppermute | solution.py:25
  57.0 9.8 %collective-permute-start.2 = (bf16[384,128]{1,0:T(8,128)(2,1)}, bf16[384,128]{1,0:T(8,128)(2,1)S(1)}, u32[]{:S(2)}, u32[]{:S(2)}) collective-permute-start(bf16[384,128]{1,0:T(8,128)(2,1)} %get-tuple-element.91), channel_id=1, source_target_pairs={{0,128},{64,192},{128,0},{192,64},{1,129},{65,193},{129,1},{193,65... | collective-permute-start | bytes 294920 | tf_op jit(solution)/shard_map/ppermute | solution.py:25
  61.3 6.4 %collective-permute-start.3 = (bf16[384,128]{1,0:T(8,128)(2,1)S(1)}, bf16[384,128]{1,0:T(8,128)(2,1)S(1)}, u32[]{:S(2)}, u32[]{:S(2)}) collective-permute-start(bf16[384,128]{1,0:T(8,128)(2,1)S(1)} %get-tuple-element.90), channel_id=1, source_target_pairs={{0,192},{64,0},{128,64},{192,128},{1,193},{65,1},{129,65},{193,129... | collective-permute-start | bytes 294920 | tf_op jit(solution)/shard_map/ppermute | solution.py:25
  76.6 32.1 %copy-start.11 = (s32[384,2]{0,1:T(2,128)S(1)}, s32[384,2]{0,1:T(2,128)}, u32[]{:S(2)}) copy-start(s32[384,2]{0,1:T(2,128)} %param.24) | copy-start | bytes 9220
  76.7 27.8 %collective-permute-start.6 = (bf16[2048,2,128]{2,1,0:T(2,128)(2,1)}, bf16[2048,2,128]{2,1,0:T(2,128)(2,1)}, u32[]{:S(2)}, u32[]{:S(2)}) collective-permute-start(bf16[2048,2,128]{2,1,0:T(2,128)(2,1)} %get-tuple-element.52), channel_id=1, source_target_pairs={{0,64},{64,128},{128,192},{192,0},{1,65},{65,129},{129,193},{193,1... | collective-permute-start | bytes 3145736 | tf_op jit(solution)/shard_map/ppermute | solution.py:25
  78.7 26.6 %collective-permute-start.7 = (bf16[2048,2,128]{2,1,0:T(2,128)(2,1)}, bf16[2048,2,128]{2,1,0:T(2,128)(2,1)}, u32[]{:S(2)}, u32[]{:S(2)}) collective-permute-start(bf16[2048,2,128]{2,1,0:T(2,128)(2,1)} %get-tuple-element.53), channel_id=1, source_target_pairs={{0,192},{64,0},{128,64},{192,128},{1,193},{65,1},{129,65},{193,129... | collective-permute-start | bytes 3145736 | tf_op jit(solution)/shard_map/ppermute | solution.py:25
  99.1 18.0 %copy-start.14 = (f32[64]{0:T(128)S(1)}, f32[64]{0:T(128)}, u32[]{:S(2)}) copy-start(f32[64]{0:T(128)} %param.21) | copy-start | bytes 772
  100.7 11.0 %copy-start.7 = (bf16[1024,2,128]{2,1,0:T(2,128)(2,1)S(1)}, bf16[1024,2,128]{2,1,0:T(2,128)(2,1)}, u32[]{:S(2)}) copy-start(bf16[1024,2,128]{2,1,0:T(2,128)(2,1)} %get-tuple-element.58) | copy-start | bytes 1572868
  100.7 20.5 %copy-start.9 = (bf16[384,64]{0,1:T(8,128)(2,1)S(1)}, bf16[384,64]{0,1:T(8,128)(2,1)}, u32[]{:S(2)}) copy-start(bf16[384,64]{0,1:T(8,128)(2,1)} %param.15) | copy-start | bytes 147460
  105.3 15.8 %all-to-all-start.2 = ((bf16[8,64,384]{2,1,0:T(8,128)(2,1)}), bf16[8,64,384]{2,1,0:T(8,128)(2,1)S(1)}, u32[]{:S(2)}, u32[]{:S(2)}) async-start(bf16[8,64,384]{2,1,0:T(8,128)(2,1)} %bitcast.107), calls=%async_computation.2 | async-start | bytes 786432 | tf_op jit(solution)/shard_map/all_to_all | solution.py:151
  109.7 16.2 %collective-permute-start.8 = (bf16[1024,2,128]{2,1,0:T(2,128)(2,1)}, bf16[1024,2,128]{2,1,0:T(2,128)(2,1)}, u32[]{:S(2)}, u32[]{:S(2)}) collective-permute-start(bf16[1024,2,128]{2,1,0:T(2,128)(2,1)} %get-tuple-element.57), channel_id=1, source_target_pairs={{0,64},{64,128},{128,192},{192,0},{1,65},{65,129},{129,193},{193,1... | collective-permute-start | bytes 1572872 | tf_op jit(solution)/shard_map/ppermute | solution.py:25
  111.7 14.9 %collective-permute-start.9 = (bf16[1024,2,128]{2,1,0:T(2,128)(2,1)S(1)}, bf16[1024,2,128]{2,1,0:T(2,128)(2,1)}, u32[]{:S(2)}, u32[]{:S(2)}) collective-permute-start(bf16[1024,2,128]{2,1,0:T(2,128)(2,1)S(1)} %copy-done.7), channel_id=1, source_target_pairs={{0,192},{64,0},{128,64},{192,128},{1,193},{65,1},{129,65},{193,129... | collective-permute-start | bytes 1572872 | tf_op jit(solution)/shard_map/ppermute | solution.py:25
  131.8 32.3 %all-to-all-start.3 = ((bf16[128,2,1152]{2,1,0:T(2,128)(2,1)}), bf16[128,2,1152]{2,1,0:T(2,128)(2,1)}, u32[]{:S(2)}, u32[]{:S(2)}) async-start(bf16[128,2,1152]{2,1,0:T(2,128)(2,1)} %reshape.200), calls=%async_computation.3 | async-start | bytes 1179648 | tf_op jit(solution)/shard_map/all_to_all | solution.py:175
  143.3 57.0 %collective-permute-start.12 = (bf16[1024,2,128]{2,1,0:T(2,128)(2,1)}, bf16[1024,2,128]{2,1,0:T(2,128)(2,1)}, u32[]{:S(2)}, u32[]{:S(2)}) collective-permute-start(bf16[1024,2,128]{2,1,0:T(2,128)(2,1)} %get-tuple-element.68), channel_id=1, source_target_pairs={{0,192},{64,0},{128,64},{192,128},{1,193},{65,1},{129,65},{193,129... | collective-permute-start | bytes 1572872 | tf_op jit(solution)/shard_map/ppermute | solution.py:25
  148.8 40.4 %collective-permute-start.10 = (bf16[1024,2,128]{2,1,0:T(2,128)(2,1)}, bf16[1024,2,128]{2,1,0:T(2,128)(2,1)}, u32[]{:S(2)}, u32[]{:S(2)}) collective-permute-start(bf16[1024,2,128]{2,1,0:T(2,128)(2,1)} %get-tuple-element.65), channel_id=1, source_target_pairs={{0,64},{64,128},{128,192},{192,0},{1,65},{65,129},{129,193},{193,1... | collective-permute-start | bytes 1572872 | tf_op jit(solution)/shard_map/ppermute | solution.py:25
  150.7 42.0 %collective-permute-start.11 = (bf16[64,4096]{1,0:T(8,128)(2,1)}, bf16[64,4096]{1,0:T(8,128)(2,1)}, u32[]{:S(2)}, u32[]{:S(2)}) collective-permute-start(bf16[64,4096]{1,0:T(8,128)(2,1)} %get-tuple-element.67), channel_id=1, source_target_pairs={{0,64},{64,128},{128,192},{192,0},{1,65},{65,129},{129,193},{193,1... | collective-permute-start | bytes 1572872 | tf_op jit(solution)/shard_map/ppermute | solution.py:25
  152.6 29.2 %collective-permute-start.15 = (bf16[2048,2,128]{2,1,0:T(2,128)(2,1)}, bf16[2048,2,128]{2,1,0:T(2,128)(2,1)}, u32[]{:S(2)}, u32[]{:S(2)}) collective-permute-start(bf16[2048,2,128]{2,1,0:T(2,128)(2,1)} %collective-permute-done.7), channel_id=1, source_target_pairs={{0,192},{64,0},{128,64},{192,128},{1,193},{65,1},{129,65},{193,129... | collective-permute-start | bytes 3145736 | tf_op jit(solution)/shard_map/ppermute | solution.py:25
  157.2 44.4 %collective-permute-start.14 = (bf16[2048,2,128]{2,1,0:T(2,128)(2,1)}, bf16[2048,2,128]{2,1,0:T(2,128)(2,1)}, u32[]{:S(2)}, u32[]{:S(2)}) collective-permute-start(bf16[2048,2,128]{2,1,0:T(2,128)(2,1)} %collective-permute-done.6), channel_id=1, source_target_pairs={{0,64},{64,128},{128,192},{192,0},{1,65},{65,129},{129,193},{193,1... | collective-permute-start | bytes 3145736 | tf_op jit(solution)/shard_map/ppermute | solution.py:25
  169.7 6.2 %copy-start.10 = (f32[4096]{0:T(1024)S(1)}, f32[4096]{0:T(1024)}, u32[]{:S(2)}) copy-start(f32[4096]{0:T(1024)} %param.23) | copy-start | bytes 49156
  176.1 5.7 %copy-start.6 = (bf16[64,4096]{1,0:T(8,128)(2,1)S(1)}, bf16[64,4096]{1,0:T(8,128)(2,1)}, u32[]{:S(2)}) copy-start(bf16[64,4096]{1,0:T(8,128)(2,1)} %get-tuple-element.71) | copy-start | bytes 1572868
  181.8 27.7 %collective-permute-start.13 = (bf16[64,4096]{1,0:T(8,128)(2,1)S(1)}, bf16[64,4096]{1,0:T(8,128)(2,1)S(1)}, u32[]{:S(2)}, u32[]{:S(2)}) collective-permute-start(bf16[64,4096]{1,0:T(8,128)(2,1)S(1)} %copy-done.6), channel_id=1, source_target_pairs={{0,192},{64,0},{128,64},{192,128},{1,193},{65,1},{129,65},{193,129... | collective-permute-start | bytes 1572872 | tf_op jit(solution)/shard_map/ppermute | solution.py:25
  188.7 3.7 %copy-start.2 = (bf16[1,128,4096]{2,1,0:T(8,128)(2,1)S(1)}, bf16[1,128,4096]{2,1,0:T(8,128)(2,1)}, u32[]{:S(2)}) copy-start(bf16[1,128,4096]{2,1,0:T(8,128)(2,1)} %param.27) | copy-start | bytes 3145732
  189.2 20.0 %collective-permute-start.16 = (bf16[64,4096]{1,0:T(8,128)(2,1)}, bf16[64,4096]{1,0:T(8,128)(2,1)S(1)}, u32[]{:S(2)}, u32[]{:S(2)}) collective-permute-start(bf16[64,4096]{1,0:T(8,128)(2,1)} %collective-permute-done.4), channel_id=1, source_target_pairs={{0,64},{64,128},{128,192},{192,0},{1,65},{65,129},{129,193},{193,1... | collective-permute-start | bytes 1572872 | tf_op jit(solution)/shard_map/ppermute | solution.py:25
  192.7 16.5 %collective-permute-start.17 = (bf16[64,4096]{1,0:T(8,128)(2,1)}, bf16[64,4096]{1,0:T(8,128)(2,1)S(1)}, u32[]{:S(2)}, u32[]{:S(2)}) collective-permute-start(bf16[64,4096]{1,0:T(8,128)(2,1)} %collective-permute-done.5), channel_id=1, source_target_pairs={{0,192},{64,0},{128,64},{192,128},{1,193},{65,1},{129,65},{193,129... | collective-permute-start | bytes 1572872 | tf_op jit(solution)/shard_map/ppermute | solution.py:25
  214.7 17.3 %copy-start.13 = (s32[384,2]{0,1:T(2,128)S(1)}, s32[384,2]{0,1:T(2,128)}, u32[]{:S(2)}) copy-start(s32[384,2]{0,1:T(2,128)} %param.25) | copy-start | bytes 9220
  216.3 36.8 %all-to-all-start.4 = ((bf16[128,2,1152]{2,1,0:T(2,128)(2,1)}), bf16[128,2,1152]{2,1,0:T(2,128)(2,1)S(1)}, u32[]{:S(2)}, u32[]{:S(2)}) async-start(bf16[128,2,1152]{2,1,0:T(2,128)(2,1)} %reshape.202), calls=%async_computation.4 | async-start | bytes 1179648 | tf_op jit(solution)/shard_map/all_to_all | solution.py:221

commit v4 on v2

--- a/solution.py
+++ b/solution.py
@@ -29,11 +29,6 @@
     return lax.optimization_barrier(values)
 
 
-def spread(v, axis):
-    n = lax.axis_size(axis)
-    return lax.all_to_all(jnp.broadcast_to(v[None], (n,) + v.shape), axis, 0, 0, tiled=True)
-
-
 def route_tables(expert_ids, gate_fixed, experts, capacity):
     token_count, top_count = expert_ids.shape
     flat_ids = expert_ids.reshape(-1)
@@ -52,20 +47,19 @@
     return selectors, weights
 
 
-def attention(queries, keys, values, slot, frame_ids, frame_rows):
+def attention(queries, keys, values, local_frame, frame_rows):
     width = keys.shape[0]
     scale = 1.0 / math.sqrt(queries.shape[1])
     scores = lax.dot_general(queries, keys, (((1,), (1,)), ((), ())), preferred_element_type=f32) * scale
-    column_frame = jnp.repeat(frame_ids, frame_rows, total_repeat_length=width)
-    inside = column_frame[None, :] == slot[:, None]
+    column_frame = lax.broadcasted_iota(jnp.int32, (1, width), 1) // frame_rows
+    inside = column_frame == local_frame[:, None]
     scores = jnp.where(inside, scores, MASKED_SCORE)
     row_max = jnp.max(scores, axis=1, keepdims=True)
     expon = jnp.exp(scores - row_max)
     row_total = jnp.sum(expon, axis=1, keepdims=True)
     probability = (expon / row_total).astype(bf16)
     mixed = jnp.dot(probability, values, preferred_element_type=f32)
-    present = jnp.any(frame_ids[None, :] == slot[:, None], axis=1, keepdims=True)
-    return jnp.where(present, mixed, 0.0).astype(bf16)
+    return jnp.where(local_frame[:, None] >= 0, mixed, 0.0).astype(bf16)
 
 
 def per_device(
@@ -91,8 +85,6 @@
     feats = hidden_in.shape[1]
     yh, x, z = lax.axis_index("yh"), lax.axis_index("x"), lax.axis_index("z")
     held, frame_rows = frame_keys.shape[0], frame_keys.shape[1]
-    in_left, in_right = shift(w_in[0], "x", 1), shift(w_in[0], "x", -1)
-    down_left, down_right = shift(w_down[0], "x", 1), shift(w_down[0], "x", -1)
     own = jnp.concatenate(
         [
             lax.dynamic_slice_in_dim(frame_keys, z * head, head, 2).reshape(held * frame_rows, head),
@@ -110,32 +102,30 @@
         token_slot.reshape(tokens // head, head).astype(bf16)
     )
     packed = jnp.concatenate([queries, slot_rows])
-    gathered = spread(packed, "x")
-    gathered, turned = tie(gathered, out_weight.T)
-    turned = turned.reshape(feats, nz, near * head).transpose(1, 0, 2)
+    gathered = jnp.stack([packed] + [shift(packed, "x", k) for k in range(1, nx)])
+    turned = out_weight.T.reshape(feats, nz, near * head).transpose(1, 0, 2)
     near_weight = lax.all_to_all(turned, "z", 0, 0, tiled=True).reshape(nz * feats, near * head)
+    in_rows = jnp.concatenate([w_in[0, :, 0], w_in[0, :, 1]], axis=0)
+    in_all = lax.all_gather(in_rows, "x")
+    down_all = lax.all_gather(w_down[0], "x", tiled=True)
     all_queries = gathered[:, :tokens].reshape(nx * tokens, head)
     all_slots = gathered[:, tokens : tokens + tokens // head].reshape(nx * tokens).astype(jnp.int32)
-    frame_ids = jnp.concatenate(
-        [held * (h * nx + x) + jnp.arange(held, dtype=jnp.int32) for h in (yh, 1 - yh)]
+    own_frame = all_slots - held * (yh * nx + x)
+    other_frame = all_slots - held * ((1 - yh) * nx + x)
+    local_frame = jnp.where(
+        (own_frame >= 0) & (own_frame < held),
+        own_frame,
+        jnp.where((other_frame >= 0) & (other_frame < held), other_frame + held, -1),
     )
-    mixed = attention(all_queries, keys, values, all_slots, frame_ids, frame_rows)
+    mixed = attention(all_queries, keys, values, local_frame, frame_rows)
     back = mixed.reshape(nx, tokens, head)
-    attended = lax.dynamic_index_in_dim(back, x, 0, keepdims=False).astype(f32)
-    for k in range(1, nx):
-        piece = lax.dynamic_index_in_dim(back, (x + k) % nx, 0, keepdims=False)
-        attended = attended + shift(piece, "x", k).astype(f32)
-    attended, near_weight = tie(attended.astype(bf16), near_weight)
+    attended = sum(
+        (shift(back[k], "x", -k) if k else back[k]).astype(f32) for k in range(nx)
+    ).astype(bf16)
     heads = lax.all_gather(attended, NEAR, axis=1, tiled=True)
     partial = lax.dot_general(
         near_weight, heads, (((1,), (1,)), ((), ())), preferred_element_type=f32
     ).astype(bf16)
-    partial, in_left, in_right, down_left, down_right = tie(
-        partial, in_left, in_right, down_left, down_right
-    )
-    half_in, half_down = w_in.shape[1] // 2, w_down.shape[1] // 2
-    in_far = shift(in_left[:half_in], "x", 1), shift(in_right[half_in:], "x", -1)
-    down_far = shift(down_left[:half_down], "x", 1), shift(down_right[half_down:], "x", -1)
     parts = lax.all_to_all(partial.reshape(nz, feats, tokens), "z", 0, 0, tiled=True)
     projected = jnp.sum(parts.astype(f32), axis=0)
     mid = (hidden_in.T.astype(f32) + jnp.tanh(attn_gate)[:, None] * projected).astype(bf16)
@@ -152,20 +142,15 @@
     wide = rows.astype(f32)
     mean_square = jnp.mean(wide * wide, axis=1, keepdims=True)
     normed = (wide * lax.rsqrt(mean_square + NORM_EPSILON) * mlp_gain).astype(bf16)
-    hidden_units = w_in.shape[3]
+    width = w_in.shape[1]
 
-    def up(part, weight):
-        weight = weight.reshape(weight.shape[0], 2 * hidden_units)
-        return jnp.dot(part, weight, preferred_element_type=f32)
+    def gated(weight):
+        gate = jnp.dot(normed, weight[:width], preferred_element_type=f32)
+        up = jnp.dot(normed, weight[width:], preferred_element_type=f32)
+        return (jax.nn.silu(gate) * up).astype(bf16)
 
-    def gated(gate_up):
-        return (jax.nn.silu(gate_up[:, :hidden_units]) * gate_up[:, hidden_units:]).astype(bf16)
-
-    ups = [up(normed, weight) for weight in (w_in[0], in_left, in_right)]
-    ups.append(up(normed[:, :half_in], in_far[0]) + up(normed[:, half_in:], in_far[1]))
-    act = [gated(u) for u in ups]
-    weights_down = [w_down[0], down_left, down_right, jnp.concatenate(down_far)]
-    down = sum(jnp.dot(p, w, preferred_element_type=f32) for p, w in zip(act, weights_down))
+    act = jnp.concatenate([gated(in_all[k]) for k in range(nx)], axis=1)
+    down = jnp.dot(act, down_all, preferred_element_type=f32)
     (down,) = tie(down.astype(bf16))
     dealt = down.reshape(nh, capacity, experts, feats).transpose(0, 2, 1, 3).reshape(-1, capacity, feats)
     back_sums = lax.all_to_all(dealt, BOTH, 0, 0, tiled=True)

time: 264 us -> 231 us (0.88)
  waiting for transfers between devices: 92.9 us -> 49.4 us
  starting transfers between devices: 89.2 us -> 61.1 us
  blocking collectives: 20 us -> 46.7 us
  between operations: 0.77 us -> 14 us
  local copies, waits for them, and re-layouts: 29.4 us -> 33.2 us
    all_to_all x0 -> x1, blocking collectives: none -> 29.2 us  [per_device(): lax.all_to_all(sent.reshape(-1, capacity, feats), BOTH, 0, 0, tiled=True)]
    all_to_all x2 -> x0, waiting for transfers between devices: 28.9 us -> none  [the longest x1 28.4 us: spread(): lax.all_to_all(jnp.broadcast_to(v[None], (n,) + v.shape), axis, 0, 0, til...]
    ppermute x11 -> x6, waiting for transfers between devices: 28.9 us -> 8.12 us  [shift(): return lax.ppermute(v, axis, [(i, (i + by) % n) for i in range(n)])]
    ppermute x11 -> x6, starting transfers between devices: 37.4 us -> 19.2 us  [shift(): return lax.ppermute(v, axis, [(i, (i + by) % n) for i in range(n)])]
    all_to_all x2 -> x0, starting transfers between devices: 11.9 us -> none  [the longest x1 8.4 us: per_device(): lax.all_to_all(sent.reshape(-1, capacity, feats), BOTH, 0, 0, tiled=True)]
    all_gather x0 -> x2, waiting for transfers between devices: none -> 5.37 us  [the longest x1 5.36 us: per_device(): down_all = lax.all_gather(w_down[0], 'x', tiled=True)]
    gather x1 -> x0, other arithmetic: 3.79 us -> none  [attention(): column_frame = jnp.repeat(frame_ids, frame_rows, total_repeat_length=width)]
    all_to_all x1, starting transfers between devices: 6.66 us -> 10.1 us  [per_device(): lax.all_to_all(partial.reshape(nz, feats, tokens), 'z', 0, 0, tiled=True)]
  transfers between devices with their start and end apart: 17 -> 12, of which waited for: 7 -> 6; matrix products, arithmetic and copies ran while one was open for 17% -> 14% of each run, Pallas kernels for 0% -> 0%
where the time goes in v4:
time: 231 us; the launch traced here: 230 us
  starting transfers between devices  61.1 us (26%)
  waiting for transfers between devices  49.4 us (21%)
  blocking collectives  46.7 us (20%)
  local copies, waits for them, and re-layouts  33.2 us (14%)
  matrix products  19 us (8%)
  between operations  14 us (6%)
  other arithmetic  6.39 us (3%)
    all_to_all x1, blocking collectives, per_device(): lax.all_to_all(sent.reshape(-1, capacity, feats), BOTH, 0, 0, tiled=True)  29.2 us
    all_to_all x1, waiting for transfers between devices, per_device(): back_sums = lax.all_to_all(dealt, BOTH, 0, 0, tiled=True)  21 us
    ppermute x6, starting transfers between devices, shift(): return lax.ppermute(v, axis, [(i, (i + by) % n) for i in range(n)])  19.2 us
    all_gather x1, blocking collectives, per_device(): heads = lax.all_gather(attended, NEAR, axis=1, tiled=True)  17.5 us
    all_to_all x1, starting transfers between devices, per_device(): back_sums = lax.all_to_all(dealt, BOTH, 0, 0, tiled=True)  14.3 us
    all_to_all x1, waiting for transfers between devices, per_device(): lax.all_to_all(partial.reshape(nz, feats, tokens), 'z', 0, 0, tiled=True)  14.1 us
    all_to_all x1, starting transfers between devices, per_device(): lax.all_to_all(partial.reshape(nz, feats, tokens), 'z', 0, 0, tiled=True)  10.1 us
    all_to_all x1, starting transfers between devices, per_device(): lax.all_to_all(turned, 'z', 0, 0, tiled=True)  10 us
  transfers between devices with their start and end apart: 12, of which 6 were waited for; matrix products, arithmetic and copies ran while one was open for 14% of the time, Pallas kernels for 0%

profile of v4, /device:TPU:1, one launch (start us, length us, event | category | flops | bytes accessed | tf_op | source)
XLA Modules:
  0.0 229.7 jit_solution(6140297716444577920)
XLA Ops:
  6.5 5.7 %fusion.77 = (bf16[1,4096,1,128]{3,2,1,0:T(2,128)(2,1)S(1)}, bf16[1,4096,1,128]{3,2,1,0:T(2,128)(2,1)S(1)}) fusion(bf16[1,4096,2,128]{3,2,1,0:T(2,128)(2,1)} %param.26), kind=kLoop, calls=%fused_computation.122 | loop fusion | bytes 4194304 | tf_op jit(solution)/shard_map/slice | solution.py:108
  12.6 1.5 pad_maximum_fusion
  14.1 0.6 copy-done.5
  15.6 3.9 %collective-permute-start = (bf16[400,128]{1,0:T(8,128)(2,1)}, bf16[400,128]{1,0:T(8,128)(2,1)S(1)}, u32[]{:S(2)}, u32[]{:S(2)}) collective-permute-start(bf16[400,128]{1,0:T(8,128)(2,1)} %get-tuple-element.33), channel_id=1, source_target_pairs={{0,64},{64,128},{128,192},{192,0},{1,65},{65,129},{129,193},{193,1... | collective-permute-start | bytes 307208 | tf_op jit(solution)/shard_map/ppermute | solution.py:25
  19.5 4.4 %collective-permute-start.1 = (bf16[400,128]{1,0:T(8,128)(2,1)}, bf16[400,128]{1,0:T(8,128)(2,1)S(1)}, u32[]{:S(2)}, u32[]{:S(2)}) collective-permute-start(bf16[400,128]{1,0:T(8,128)(2,1)} %get-tuple-element.33), channel_id=1, source_target_pairs={{0,128},{64,192},{128,0},{192,64},{1,129},{65,193},{129,1},{193,65... | collective-permute-start | bytes 307208 | tf_op jit(solution)/shard_map/ppermute | solution.py:25
  23.9 3.1 %collective-permute-start.2 = (bf16[400,128]{1,0:T(8,128)(2,1)}, bf16[400,128]{1,0:T(8,128)(2,1)S(1)}, u32[]{:S(2)}, u32[]{:S(2)}) collective-permute-start(bf16[400,128]{1,0:T(8,128)(2,1)} %get-tuple-element.33), channel_id=1, source_target_pairs={{0,192},{64,0},{128,64},{192,128},{1,193},{65,1},{129,65},{193,129... | collective-permute-start | bytes 307208 | tf_op jit(solution)/shard_map/ppermute | solution.py:25
  27.1 0.9 constant_dynamic-slice_fusion
  28.1 0.8 pad_maximum_fusion.4
  28.9 7.4 %collective-permute-start.3 = (bf16[1206,128]{1,0:T(8,128)(2,1)}, bf16[1206,128]{1,0:T(8,128)(2,1)S(1)}, u32[]{:S(2)}, u32[]{:S(2)}) collective-permute-start(bf16[1206,128]{1,0:T(8,128)(2,1)} %pad_maximum_fusion.4), channel_id=1, source_target_pairs={{0,256},{256,0},{1,257},{257,1},{2,258},{258,2},{3,259},{259,3},{4... | collective-permute-start | bytes 926216 | tf_op jit(solution)/shard_map/ppermute | solution.py:20
  36.9 1.6 copy.61
  38.5 10.0 %all-to-all-start = ((bf16[8,64,1024]{2,1,0:T(8,128)(2,1)}), bf16[8,64,1024]{2,1,0:T(8,128)(2,1)S(1)}, u32[]{:S(2)}, u32[]{:S(2)}) async-start(bf16[8,64,1024]{2,1,0:T(8,128)(2,1)} %copy.61), calls=%async_computation | async-start | bytes 2097152 | tf_op jit(solution)/shard_map/all_to_all | solution.py:107
  48.6 0.7 all-gather.7.cloned.1.call-update
  49.5 1.3 fusion.80
  50.8 1.1 fusion.1
  51.9 1.5 fusion.13
  53.4 1.9 collective-permute-start.4
  55.3 4.0 %collective-permute-start.5 = (bf16[384,128]{1,0:T(8,128)(2,1)S(1)}, bf16[384,128]{1,0:T(8,128)(2,1)S(1)}, u32[]{:S(2)}, u32[]{:S(2)}) collective-permute-start(bf16[384,128]{1,0:T(8,128)(2,1)S(1)} %get-tuple-element.29), channel_id=1, source_target_pairs={{0,128},{64,192},{128,0},{192,64},{1,129},{65,193},{129,1},{193,65... | collective-permute-start | bytes 294920 | tf_op jit(solution)/shard_map/ppermute | solution.py:25
  59.3 1.9 collective-permute-start.6
  61.4 3.3 %collective-permute-done.5 = bf16[384,128]{1,0:T(8,128)(2,1)S(1)} collective-permute-done((bf16[384,128]{1,0:T(8,128)(2,1)S(1)}, bf16[384,128]{1,0:T(8,128)(2,1)S(1)}, u32[]{:S(2)}, u32[]{:S(2)}) %collective-permute-start.5) | collective-permute-done | bytes 98336 | tf_op jit(solution)/shard_map/ppermute | solution.py:25
  64.8 4.6 %collective-permute-done.6 = bf16[384,128]{1,0:T(8,128)(2,1)S(1)} collective-permute-done((bf16[384,128]{1,0:T(8,128)(2,1)S(1)}, bf16[384,128]{1,0:T(8,128)(2,1)S(1)}, u32[]{:S(2)}, u32[]{:S(2)}) %collective-permute-start.6) | collective-permute-done | bytes 98336 | tf_op jit(solution)/shard_map/ppermute | solution.py:25
  69.4 17.5 %all_gather.12 = bf16[384,1024]{1,0:T(8,128)(2,1)S(1)} all-gather(bf16[384,128]{1,0:T(8,128)(2,1)S(1)} %add_convert_fusion), channel_id=1, replica_groups=mesh['yh'=2,'x'=4,'z'=8,'yl'=4,'core'=2] {'yl','core'}, dimensions={1}, use_global_device_ids=true | all-gather | bytes 884736 | tf_op jit(solution)/shard_map/all_gather | solution.py:125
  87.6 0.9 copy.62
  88.5 10.1 %all-to-all-start.1 = ((bf16[8,64,384]{2,1,0:T(8,128)(2,1)}), bf16[8,64,384]{2,1,0:T(8,128)(2,1)S(1)}, u32[]{:S(2)}, u32[]{:S(2)}) async-start(bf16[8,64,384]{2,1,0:T(8,128)(2,1)} %bitcast.10), calls=%async_computation.1 | async-start | bytes 786432 | tf_op jit(solution)/shard_map/all_to_all | solution.py:129
  99.7 14.1 %all-to-all-done.1 = bf16[8,64,384]{2,1,0:T(8,128)(2,1)S(1)} async-done(((bf16[8,64,384]{2,1,0:T(8,128)(2,1)}), bf16[8,64,384]{2,1,0:T(8,128)(2,1)S(1)}, u32[]{:S(2)}, u32[]{:S(2)}) %all-to-all-start.1) | async-done | bytes 393248 | tf_op jit(solution)/shard_map/all_to_all | solution.py:129
  113.9 1.1 fusion.9
  115.7 0.7 reshape.179
  116.4 29.2 %all_to_all.20 = bf16[128,2,1152]{2,1,0:T(2,128)(2,1)} all-to-all(bf16[128,2,1152]{2,1,0:T(2,128)(2,1)S(1)} %reshape.179), channel_id=1, replica_groups=mesh['yh'=2,'x'=4,'z'=8,'yl'=4,'core'=2] {'yh','z','yl','core'}, dimensions={0} | all-to-all | bytes 1179648 | tf_op jit(solution)/shard_map/all_to_all | solution.py:139
  145.7 2.7 %reshape.180 = bf16[128,36,64]{2,1,0:T(8,128)(2,1)S(1)} reshape(bf16[128,2,1152]{2,1,0:T(2,128)(2,1)} %all_to_all.20) | data formatting | bytes 1179648
  148.4 2.9 %copy.72 = bf16[2,64,36,64]{1,0,3,2:T(2,128)(2,1)} copy(bf16[2,64,36,64]{3,2,1,0:T(8,128)(2,1)S(1)} %bitcast.72) | data formatting | bytes 1179648 | tf_op jit(solution)/shard_map/reshape | solution.py:140
  151.3 2.6 %copy.67 = bf16[2,36,64,64]{3,2,1,0:T(8,128)(2,1)S(1)} copy(bf16[2,36,64,64]{2,0,3,1:T(2,128)(2,1)} %bitcast.75) | data formatting | bytes 1179648 | tf_op jit(solution)/shard_map/transpose | solution.py:140
  153.9 0.9 reshape.167
  155.1 1.8 fusion.37
  156.9 2.0 fusion.36
  158.9 1.6 fusion.35
  160.6 1.6 fusion.34
  163.8 5.4 %all-gather.7.cloned.1.call-done = bf16[1,512,4096]{2,1,0:T(8,128)(2,1)} async-done(((bf16[1,128,4096]{2,1,0:T(8,128)(2,1)}), bf16[1,512,4096]{2,1,0:T(8,128)(2,1)}) %all-gather.7.cloned.1.call-update) | async-done | bytes 4194320 | tf_op jit(solution)/shard_map/all_gather | solution.py:110
  169.1 3.0 %convolution_convert_fusion = bf16[72,4096]{1,0:T(8,128)(2,1)S(1)} fusion(bf16[1,512,4096]{2,1,0:T(8,128)(2,1)} %all-gather.7.cloned.1.call-done, bf16[72,128]{1,0:T(8,128)(2,1)S(1)} %fusion.33, bf16[72,128]{1,0:T(8,128)(2,1)S(1)} %fusion.32, bf16[72,128]{1,0:T(8,128)(2,1)S(1)} %fusion.31, bf16[72,128]{1,0:T(8,128)(2,1)S(1)} %fusion.30), kind=kOutput, calls=%fused_computation.5 | convolution fusion | flops 302579712 | bytes 4857856 | tf_op jit(solution)/shard_map/dot_general | solution.py:153
  172.1 1.3 reshape.168
  173.4 2.1 copy.70
  175.5 3.6 %copy.73 = bf16[2,64,36,64]{3,2,1,0:T(8,128)(2,1)S(1)} copy(bf16[2,64,36,64]{1,0,3,2:T(2,128)(2,1)} %bitcast.76) | data formatting | bytes 1179648 | tf_op jit(solution)/shard_map/reshape | solution.py:155
  179.2 1.6 reshape.181
  180.7 14.3 %all-to-all-start.3 = ((bf16[128,2,1152]{2,1,0:T(2,128)(2,1)}), bf16[128,2,1152]{2,1,0:T(2,128)(2,1)S(1)}, u32[]{:S(2)}, u32[]{:S(2)}) async-start(bf16[128,2,1152]{2,1,0:T(2,128)(2,1)} %reshape.181), calls=%async_computation.3 | async-start | bytes 1179648 | tf_op jit(solution)/shard_map/all_to_all | solution.py:156
  195.1 21.0 %all-to-all-done.3 = bf16[128,2,1152]{2,1,0:T(2,128)(2,1)S(1)} async-done(((bf16[128,2,1152]{2,1,0:T(2,128)(2,1)}), bf16[128,2,1152]{2,1,0:T(2,128)(2,1)S(1)}, u32[]{:S(2)}, u32[]{:S(2)}) %all-to-all-start.3) | async-done | bytes 589856 | tf_op jit(solution)/shard_map/all_to_all | solution.py:156
  216.1 1.1 reshape.182
  217.2 1.3 reshape.170
  218.5 1.9 reduce_sum.62
  220.4 0.9 fusion.28
  221.3 1.5 fusion.29
  (73 shorter events, 6.5 us)
Async XLA Ops:
  6.5 20.4 %copy-start = (bf16[3,201,1024]{2,1,0:T(8,128)(2,1)S(1)}, bf16[3,201,1024]{2,1,0:T(8,128)(2,1)}, u32[]{:S(2)}) copy-start(bf16[3,201,1024]{2,1,0:T(8,128)(2,1)} %param.17) | copy-start | bytes 3704836
  6.5 148.5 %all-gather.5.cloned.1.call-start = ((), (), s32[]{:S(2)}) async-start(), calls=%async_computation.4 | async-start | bytes 10485760 | tf_op jit(solution)/shard_map/all_gather | solution.py:109
  14.0 0.7 copy-start.5
  14.0 0.7 copy-start.6
  14.0 0.9 copy-start.2
  14.0 22.3 %copy-start.1 = (bf16[8192,64]{0,1:T(8,128)(2,1)S(1)}, bf16[8192,64]{0,1:T(8,128)(2,1)}, u32[]{:S(2)}) copy-start(bf16[8192,64]{0,1:T(8,128)(2,1)} %param.22) | copy-start | bytes 3145732
  15.6 33.7 %collective-permute-start = (bf16[400,128]{1,0:T(8,128)(2,1)}, bf16[400,128]{1,0:T(8,128)(2,1)S(1)}, u32[]{:S(2)}, u32[]{:S(2)}) collective-permute-start(bf16[400,128]{1,0:T(8,128)(2,1)} %get-tuple-element.33), channel_id=1, source_target_pairs={{0,64},{64,128},{128,192},{192,0},{1,65},{65,129},{129,193},{193,1... | collective-permute-start | bytes 307208 | tf_op jit(solution)/shard_map/ppermute | solution.py:25
  19.5 29.8 %collective-permute-start.1 = (bf16[400,128]{1,0:T(8,128)(2,1)}, bf16[400,128]{1,0:T(8,128)(2,1)S(1)}, u32[]{:S(2)}, u32[]{:S(2)}) collective-permute-start(bf16[400,128]{1,0:T(8,128)(2,1)} %get-tuple-element.33), channel_id=1, source_target_pairs={{0,128},{64,192},{128,0},{192,64},{1,129},{65,193},{129,1},{193,65... | collective-permute-start | bytes 307208 | tf_op jit(solution)/shard_map/ppermute | solution.py:25
  23.9 25.4 %collective-permute-start.2 = (bf16[400,128]{1,0:T(8,128)(2,1)}, bf16[400,128]{1,0:T(8,128)(2,1)S(1)}, u32[]{:S(2)}, u32[]{:S(2)}) collective-permute-start(bf16[400,128]{1,0:T(8,128)(2,1)} %get-tuple-element.33), channel_id=1, source_target_pairs={{0,192},{64,0},{128,64},{192,128},{1,193},{65,1},{129,65},{193,129... | collective-permute-start | bytes 307208 | tf_op jit(solution)/shard_map/ppermute | solution.py:25
  28.9 20.6 %collective-permute-start.3 = (bf16[1206,128]{1,0:T(8,128)(2,1)}, bf16[1206,128]{1,0:T(8,128)(2,1)S(1)}, u32[]{:S(2)}, u32[]{:S(2)}) collective-permute-start(bf16[1206,128]{1,0:T(8,128)(2,1)} %pad_maximum_fusion.4), channel_id=1, source_target_pairs={{0,256},{256,0},{1,257},{257,1},{2,258},{258,2},{3,259},{259,3},{4... | collective-permute-start | bytes 926216 | tf_op jit(solution)/shard_map/ppermute | solution.py:20
  38.5 48.5 %all-to-all-start = ((bf16[8,64,1024]{2,1,0:T(8,128)(2,1)}), bf16[8,64,1024]{2,1,0:T(8,128)(2,1)S(1)}, u32[]{:S(2)}, u32[]{:S(2)}) async-start(bf16[8,64,1024]{2,1,0:T(8,128)(2,1)} %copy.61), calls=%async_computation | async-start | bytes 2097152 | tf_op jit(solution)/shard_map/all_to_all | solution.py:107
  48.5 120.6 %all-gather.7.cloned.1.call-start = ((), (), s32[]{:S(2)}) async-start(), calls=%async_computation.5 | async-start | bytes 5242880 | tf_op jit(solution)/shard_map/all_gather | solution.py:110
  53.4 8.0 %collective-permute-start.4 = (bf16[384,128]{1,0:T(8,128)(2,1)S(1)}, bf16[384,128]{1,0:T(8,128)(2,1)S(1)}, u32[]{:S(2)}, u32[]{:S(2)}) collective-permute-start(bf16[384,128]{1,0:T(8,128)(2,1)S(1)} %get-tuple-element.27), channel_id=1, source_target_pairs={{0,192},{64,0},{128,64},{192,128},{1,193},{65,1},{129,65},{193,129... | collective-permute-start | bytes 294920 | tf_op jit(solution)/shard_map/ppermute | solution.py:25
  55.3 9.4 %collective-permute-start.5 = (bf16[384,128]{1,0:T(8,128)(2,1)S(1)}, bf16[384,128]{1,0:T(8,128)(2,1)S(1)}, u32[]{:S(2)}, u32[]{:S(2)}) collective-permute-start(bf16[384,128]{1,0:T(8,128)(2,1)S(1)} %get-tuple-element.29), channel_id=1, source_target_pairs={{0,128},{64,192},{128,0},{192,64},{1,129},{65,193},{129,1},{193,65... | collective-permute-start | bytes 294920 | tf_op jit(solution)/shard_map/ppermute | solution.py:25
  59.3 10.0 %collective-permute-start.6 = (bf16[384,128]{1,0:T(8,128)(2,1)S(1)}, bf16[384,128]{1,0:T(8,128)(2,1)S(1)}, u32[]{:S(2)}, u32[]{:S(2)}) collective-permute-start(bf16[384,128]{1,0:T(8,128)(2,1)S(1)} %get-tuple-element.28), channel_id=1, source_target_pairs={{0,64},{64,128},{128,192},{192,0},{1,65},{65,129},{129,193},{193,1... | collective-permute-start | bytes 294920 | tf_op jit(solution)/shard_map/ppermute | solution.py:25
  87.0 11.7 %copy-start.3 = (s32[384,2]{0,1:T(2,128)S(1)}, s32[384,2]{0,1:T(2,128)}, u32[]{:S(2)}) copy-start(s32[384,2]{0,1:T(2,128)} %param.24) | copy-start | bytes 9220
  87.6 12.0 %copy-start.11 = (f32[64]{0:T(128)S(1)}, f32[64]{0:T(128)}, u32[]{:S(2)}) copy-start(f32[64]{0:T(128)} %param.21) | copy-start | bytes 772
  87.6 26.3 %copy-start.8 = (bf16[384,64]{0,1:T(8,128)(2,1)S(1)}, bf16[384,64]{0,1:T(8,128)(2,1)}, u32[]{:S(2)}) copy-start(bf16[384,64]{0,1:T(8,128)(2,1)} %param.15) | copy-start | bytes 147460
  88.5 25.3 %all-to-all-start.1 = ((bf16[8,64,384]{2,1,0:T(8,128)(2,1)}), bf16[8,64,384]{2,1,0:T(8,128)(2,1)S(1)}, u32[]{:S(2)}, u32[]{:S(2)}) async-start(bf16[8,64,384]{2,1,0:T(8,128)(2,1)} %bitcast.10), calls=%async_computation.1 | async-start | bytes 786432 | tf_op jit(solution)/shard_map/all_to_all | solution.py:129
  151.3 3.8 %copy-start.10 = (f32[4096]{0:T(1024)S(1)}, f32[4096]{0:T(1024)}, u32[]{:S(2)}) copy-start(f32[4096]{0:T(1024)} %param.23) | copy-start | bytes 49156
  155.1 7.1 %copy-start.7 = (bf16[32768,128]{1,0:T(8,128)(2,1)S(1)}, bf16[32768,128]{1,0:T(8,128)(2,1)}, u32[]{:S(2)}) copy-start(bf16[32768,128]{1,0:T(8,128)(2,1)} %all-gather.5.cloned.1.call-done) | copy-start | bytes 25165828
  179.2 15.9 %copy-start.4 = (s32[384,2]{0,1:T(2,128)S(1)}, s32[384,2]{0,1:T(2,128)}, u32[]{:S(2)}) copy-start(s32[384,2]{0,1:T(2,128)} %param.25) | copy-start | bytes 9220
  180.7 35.4 %all-to-all-start.3 = ((bf16[128,2,1152]{2,1,0:T(2,128)(2,1)}), bf16[128,2,1152]{2,1,0:T(2,128)(2,1)S(1)}, u32[]{:S(2)}, u32[]{:S(2)}) async-start(bf16[128,2,1152]{2,1,0:T(2,128)(2,1)} %reshape.181), calls=%async_computation.3 | async-start | bytes 1179648 | tf_op jit(solution)/shard_map/all_to_all | solution.py:156
  218.5 2.8 %copy-start.9 = (bf16[384,64]{0,1:T(8,128)(2,1)S(1)}, bf16[384,64]{0,1:T(8,128)(2,1)}, u32[]{:S(2)}) copy-start(bf16[384,64]{0,1:T(8,128)(2,1)} %param.15) | copy-start | bytes 147460
Sparse Core Ops, SparseCore 0:
  14.2 98.1 all-gather.4
  114.5 54.5 all-gather.6

commit v5 on v4

--- a/solution.py
+++ b/solution.py
@@ -1,8 +1,12 @@
+import functools
 import math
 
 import jax
 import jax.numpy as jnp
+import numpy as np
 from jax import lax
+from jax.experimental import pallas as pl
+from jax.experimental.pallas import tpu as pltpu
 from jax.sharding import Mesh
 from jax.sharding import PartitionSpec as P
 
@@ -29,7 +33,7 @@
     return lax.optimization_barrier(values)
 
 
-def route_tables(expert_ids, gate_fixed, experts, capacity):
+def slots_of(expert_ids, capacity, experts):
     token_count, top_count = expert_ids.shape
     flat_ids = expert_ids.reshape(-1)
     assigned = flat_ids.shape[0]
@@ -40,11 +44,119 @@
     )
     counts = jnp.dot(before.astype(bf16), matches.astype(bf16), preferred_element_type=f32)
     rank_of = jnp.sum(jnp.where(matches, counts, 0.0), axis=1).astype(jnp.int32)
-    slot_of = (flat_ids * capacity + rank_of).reshape(token_count, top_count)
-    slot_cols = lax.broadcasted_iota(jnp.int32, (token_count, experts * capacity), 1)
-    selectors = [(slot_of[:, k : k + 1] == slot_cols) for k in range(top_count)]
-    weights = gate_fixed.astype(f32) * FIXED_SCALE
-    return selectors, weights
+    return (flat_ids * capacity + rank_of).reshape(token_count, top_count).T
+
+
+def row_slots(experts, capacity, padded):
+    half = capacity // 2
+    row = np.arange(experts * padded)
+    at = row % padded
+    return np.where(at < half, row // padded * capacity + at, -4 * capacity).astype(np.int32)[:, None]
+
+
+def chosen(rows, slot):
+    return jnp.where(rows == slot, 1.0, 0.0)
+
+
+def dispatch_kernel(experts, half, padded, parts, hidden, gate, slots, rows, mid_out, sent):
+    summed = jnp.sum(parts[...].astype(f32), axis=0)
+    mid = (hidden[...].astype(f32) + jnp.tanh(gate[...]) * summed).astype(bf16)
+    mid_out[...] = mid
+    nothing = jnp.zeros_like(mid)
+    low = rows[...]
+    first, second = slots[0:1], slots[1:2]
+    total = 0.0
+    for at, wide in ((low, (mid, nothing)), (low + half, (nothing, mid))):
+        pick = (chosen(at, first) + chosen(at, second)).astype(bf16)
+        total = total + lax.dot_general(
+            pick, jnp.concatenate(wide, axis=0), (((1,), (1,)), ((), ())), preferred_element_type=f32
+        )
+    for e in range(experts):
+        block = total[e * padded : e * padded + half].astype(bf16)
+        for copy in range(sent.shape[0] // experts):
+            sent[copy * experts + e] = block
+
+
+def assemble_kernel(experts, half, padded, came, gain, normed, wide):
+    wide[...] = jnp.zeros_like(wide)
+    lanes = came.shape[2]
+    left = lax.broadcasted_iota(jnp.int32, (half, lanes), 1) < lanes // 2
+    for group in range(came.shape[0] // experts):
+        for pair in range(experts // 2):
+            one = came[group * experts + 2 * pair].astype(f32)
+            two = came[group * experts + 2 * pair + 1].astype(f32)
+            cols = pl.ds(pair * lanes, lanes)
+            at = 2 * group * padded
+            wide[pl.ds(at, half), cols] = jnp.where(left, one, pltpu.roll(two, lanes // 2, 1))
+            wide[pl.ds(at + padded, half), cols] = jnp.where(left, pltpu.roll(one, lanes // 2, 1), two)
+    rows = wide[...]
+    mean_square = jnp.mean(rows * rows, axis=1, keepdims=True)
+    normed[...] = (rows * lax.rsqrt(mean_square + NORM_EPSILON) * gain[...]).astype(bf16)
+
+
+def expert_kernel(experts, half, padded, place, normed, weights, *rest):
+    del place
+    *downs, out, wide = rest
+    step = pl.program_id(0)
+    inner = normed.shape[1]
+    gate = jnp.dot(normed[...], weights[0, :inner], preferred_element_type=f32)
+    up = jnp.dot(normed[...], weights[0, inner:], preferred_element_type=f32)
+    act = (gate / (1.0 + jnp.exp(-gate)) * up).astype(bf16)
+    for k, down in enumerate(downs):
+
+        @pl.when(step == k)
+        def _():
+            product = jnp.dot(act, down[...], preferred_element_type=f32)
+            wide[...] = product if k == 0 else wide[...] + product
+
+    @pl.when(step == len(downs) - 1)
+    def _():
+        lanes = out.shape[2]
+        left = lax.broadcasted_iota(jnp.int32, (half, lanes), 1) < lanes // 2
+        for group in range(out.shape[0] // experts):
+            for pair in range(experts // 2):
+                cols = pl.ds(pair * lanes, lanes)
+                at = 2 * group * padded
+                low = wide[pl.ds(at, half), cols]
+                high = wide[pl.ds(at + padded, half), cols]
+                out[group * experts + 2 * pair] = jnp.where(
+                    left, low, pltpu.roll(high, lanes // 2, 1)
+                ).astype(bf16)
+                out[group * experts + 2 * pair + 1] = jnp.where(
+                    left, pltpu.roll(low, lanes // 2, 1), high
+                ).astype(bf16)
+
+
+def combine_kernel(experts, half, padded, back, mid, slots, fixed, rows, out, table):
+    table[...] = jnp.zeros_like(table)
+    for e in range(experts):
+        total = back[e].astype(f32)
+        for copy in range(1, back.shape[0] // experts):
+            total = total + back[copy * experts + e].astype(f32)
+        table[pl.ds(e * padded, half), :] = total
+    rounded = table[...].astype(bf16)
+    feats = mid.shape[0]
+    low = rows[...]
+    total = mid[...].astype(f32)
+    for k in range(slots.shape[0]):
+        slot = slots[k : k + 1]
+        picked = 0.0
+        for at, begin in ((low, 0), (low + half, feats)):
+            both = lax.dot_general(
+                rounded, chosen(at, slot).astype(bf16), (((0,), (0,)), ((), ())), preferred_element_type=f32
+            )
+            picked = picked + both[begin : begin + feats]
+        total = total + picked * (fixed[k : k + 1].astype(f32) * FIXED_SCALE)
+    out[...] = total.astype(bf16)
+
+
+def local_kernel(body, *out_shapes, scratch=()):
+    return pl.pallas_call(
+        body,
+        out_shape=out_shapes,
+        scratch_shapes=scratch,
+        compiler_params=pltpu.CompilerParams(vmem_limit_bytes=40 * 1024 * 1024),
+    )
 
 
 def attention(queries, keys, values, local_frame, frame_rows):
@@ -103,11 +215,10 @@
     )
     packed = jnp.concatenate([queries, slot_rows])
     gathered = jnp.stack([packed] + [shift(packed, "x", k) for k in range(1, nx)])
+    gathered, wide_in = tie(gathered, w_in[0])
+    in_all = lax.all_gather(jnp.concatenate([wide_in[:, 0], wide_in[:, 1]], axis=0), "x")
     turned = out_weight.T.reshape(feats, nz, near * head).transpose(1, 0, 2)
     near_weight = lax.all_to_all(turned, "z", 0, 0, tiled=True).reshape(nz * feats, near * head)
-    in_rows = jnp.concatenate([w_in[0, :, 0], w_in[0, :, 1]], axis=0)
-    in_all = lax.all_gather(in_rows, "x")
-    down_all = lax.all_gather(w_down[0], "x", tiled=True)
     all_queries = gathered[:, :tokens].reshape(nx * tokens, head)
     all_slots = gathered[:, tokens : tokens + tokens // head].reshape(nx * tokens).astype(jnp.int32)
     own_frame = all_slots - held * (yh * nx + x)
@@ -122,45 +233,57 @@
     attended = sum(
         (shift(back[k], "x", -k) if k else back[k]).astype(f32) for k in range(nx)
     ).astype(bf16)
+    attended, own_down = tie(attended, w_down[0])
+    down_pieces = [own_down] + [shift(own_down, "x", k) for k in range(1, nx)]
     heads = lax.all_gather(attended, NEAR, axis=1, tiled=True)
     partial = lax.dot_general(
         near_weight, heads, (((1,), (1,)), ((), ())), preferred_element_type=f32
     ).astype(bf16)
     parts = lax.all_to_all(partial.reshape(nz, feats, tokens), "z", 0, 0, tiled=True)
-    projected = jnp.sum(parts.astype(f32), axis=0)
-    mid = (hidden_in.T.astype(f32) + jnp.tanh(attn_gate)[:, None] * projected).astype(bf16)
     capacity = 6 * tokens // experts
-    selectors, weights = route_tables(expert_ids, gate_fixed, experts, capacity)
-    select_rows = (selectors[0] | selectors[1]).astype(bf16)
-    sent = lax.dot_general(
-        select_rows, mid, (((0,), (1,)), ((), ())), preferred_element_type=f32
-    ).astype(bf16)
-    sent = jnp.broadcast_to(sent.reshape(1, experts, capacity, feats), (nh, experts, capacity, feats))
-    came = lax.all_to_all(sent.reshape(-1, capacity, feats), BOTH, 0, 0, tiled=True)
-    rows = came.reshape(nh, experts, capacity, feats).transpose(0, 2, 1, 3)
-    (rows,) = tie(rows.reshape(nh * capacity, experts * feats))
-    wide = rows.astype(f32)
-    mean_square = jnp.mean(wide * wide, axis=1, keepdims=True)
-    normed = (wide * lax.rsqrt(mean_square + NORM_EPSILON) * mlp_gain).astype(bf16)
-    width = w_in.shape[1]
-
-    def gated(weight):
-        gate = jnp.dot(normed, weight[:width], preferred_element_type=f32)
-        up = jnp.dot(normed, weight[width:], preferred_element_type=f32)
-        return (jax.nn.silu(gate) * up).astype(bf16)
-
-    act = jnp.concatenate([gated(in_all[k]) for k in range(nx)], axis=1)
-    down = jnp.dot(act, down_all, preferred_element_type=f32)
-    (down,) = tie(down.astype(bf16))
-    dealt = down.reshape(nh, capacity, experts, feats).transpose(0, 2, 1, 3).reshape(-1, capacity, feats)
+    half, padded = capacity // 2, -(-(capacity // 2) // 8) * 8
+    lanes = 2 * feats
+    table = row_slots(experts, capacity, padded)
+    slots = slots_of(expert_ids, capacity, experts)
+    mid, sent = local_kernel(
+        functools.partial(dispatch_kernel, experts, half, padded),
+        jax.ShapeDtypeStruct((feats, tokens), bf16),
+        jax.ShapeDtypeStruct((nh * experts, half, lanes), bf16),
+    )(parts, hidden_in.T, attn_gate[:, None], slots, table)
+    sent, down_pieces[1], down_pieces[3] = tie(sent, down_pieces[1], down_pieces[3])
+    came = lax.all_to_all(sent, BOTH, 0, 0, tiled=True)
+    came, *down_pieces = tie(came, *down_pieces)
+    rows = 2 * nh * padded
+    (normed,) = local_kernel(
+        functools.partial(assemble_kernel, experts, half, padded),
+        jax.ShapeDtypeStruct((rows, experts * feats), bf16),
+        scratch=(pltpu.VMEM((rows, experts * feats), f32),),
+    )(came, mlp_gain[None])
+
+    whole = lambda v: pl.BlockSpec(v.shape, lambda k, place: (0,) * v.ndim)
+    dealt = pl.pallas_call(
+        functools.partial(expert_kernel, experts, half, padded),
+        grid_spec=pltpu.PrefetchScalarGridSpec(
+            num_scalar_prefetch=1,
+            grid=(nx,),
+            in_specs=[
+                whole(normed),
+                pl.BlockSpec((1,) + in_all.shape[1:], lambda k, place: ((place[0] + nx - k) % nx, 0, 0)),
+            ]
+            + [whole(piece) for piece in down_pieces],
+            out_specs=whole(came),
+            scratch_shapes=[pltpu.VMEM((rows, experts * feats), f32)],
+        ),
+        out_shape=jax.ShapeDtypeStruct(came.shape, bf16),
+        compiler_params=pltpu.CompilerParams(vmem_limit_bytes=40 * 1024 * 1024),
+    )(x[None], normed, in_all, *down_pieces)
     back_sums = lax.all_to_all(dealt, BOTH, 0, 0, tiled=True)
-    back_sums = back_sums.reshape(nh, experts * capacity, feats).astype(f32)
-    came_back = jnp.sum(back_sums, axis=0).astype(bf16)
-    mixed_out = sum(
-        jnp.dot(s.astype(bf16), came_back, preferred_element_type=f32) * weights[:, k : k + 1]
-        for k, s in enumerate(selectors)
-    )
-    return (mid.T.astype(f32) + mixed_out).astype(bf16)
+    (out,) = local_kernel(
+        functools.partial(combine_kernel, experts, half, padded),
+        jax.ShapeDtypeStruct((feats, tokens), bf16),
+        scratch=(pltpu.VMEM((experts * padded, lanes), f32),),
+    )(back_sums, mid, slots, gate_fixed.T, table)
+    return out.T
 
 
 def solution(mesh):

time: 231 us -> 228 us (0.987)
  local copies, waits for them, and re-layouts: 33.2 us -> 12.7 us
  matrix products: 19 us -> 4.92 us
  blocking collectives: 46.7 us -> 59.4 us
  starting transfers between devices: 61.1 us -> 72.1 us
  Pallas kernels: 0 us -> 10 us
    ppermute x6 -> x9, waiting for transfers between devices: 8.12 us -> 34.8 us  [shift(): return lax.ppermute(v, axis, [(i, (i + by) % n) for i in range(n)])]
    all_to_all x1, waiting for transfers between devices: 21 us -> 0.01 us  [per_device(): came = lax.all_to_all(sent, BOTH, 0, 0, tiled=True)]
    dot_general x13 -> x1, matrix products: 15.6 us -> 0.38 us  [slots_of(): jnp.dot(before.astype(bf16), matches.astype(bf16), preferred_element_type...]
    reshape x6 -> x0, local copies, waits for them, and re-layouts: 12.1 us -> none  [the longest x3 6.99 us: per_device(): down.reshape(nh, capacity, experts, feats).transpose(0, 2, 1, 3)]
    ppermute x6 -> x9, starting transfers between devices: 19.2 us -> 30.8 us  [shift(): return lax.ppermute(v, axis, [(i, (i + by) % n) for i in range(n)])]
    all_to_all x1, blocking collectives: 29.2 us -> 39.5 us  [per_device(): back_sums = lax.all_to_all(dealt, BOTH, 0, 0, tiled=True)]
    pallas_call x0 -> x4, Pallas kernels: none -> 10 us  [the longest x1 5.55 us: per_device(): pl.pallas_call(functools.partial(expert_kernel, experts, half, padded), g...]
    slice x3 -> x1, local copies, waits for them, and re-layouts: 5.78 us -> 0.03 us  [per_device(): all_queries = gathered[:, :tokens].reshape(nx * tokens, head)]
  transfers between devices with their start and end apart: 12 -> 14, of which waited for: 6 -> 5; matrix products, arithmetic and copies ran while one was open for 14% -> 6% of each run, Pallas kernels for 0% -> 1%
where the time goes in v5:
time: 228 us; the launch traced here: 227 us
  starting transfers between devices  72.1 us (32%)
  blocking collectives  59.4 us (26%)
  waiting for transfers between devices  48.9 us (21%)
  between operations  13.8 us (6%)
  local copies, waits for them, and re-layouts  12.7 us (6%)
  Pallas kernels  10 us (4%)
  other arithmetic  5.26 us (2%)
  matrix products  4.92 us (2%)
    all_to_all x1, blocking collectives, per_device(): back_sums = lax.all_to_all(dealt, BOTH, 0, 0, tiled=True)  39.5 us
    ppermute x9, waiting for transfers between devices, shift(): return lax.ppermute(v, axis, [(i, (i + by) % n) for i in range(n)])  34.8 us
    ppermute x9, starting transfers between devices, shift(): return lax.ppermute(v, axis, [(i, (i + by) % n) for i in range(n)])  30.8 us
    all_gather x1, blocking collectives, per_device(): heads = lax.all_gather(attended, NEAR, axis=1, tiled=True)  19.9 us
    all_to_all x1, starting transfers between devices, per_device(): came = lax.all_to_all(sent, BOTH, 0, 0, tiled=True)  14.2 us
    all_to_all x1, waiting for transfers between devices, per_device(): lax.all_to_all(partial.reshape(nz, feats, tokens), 'z', 0, 0, tiled=True)  14.1 us
    all_to_all x1, starting transfers between devices, per_device(): lax.all_to_all(turned, 'z', 0, 0, tiled=True)  10 us
    all_to_all x1, starting transfers between devices, per_device(): lax.all_to_all(partial.reshape(nz, feats, tokens), 'z', 0, 0, tiled=True)  9.96 us
  transfers between devices with their start and end apart: 14, of which 5 were waited for; matrix products, arithmetic and copies ran while one was open for 6% of the time, Pallas kernels for 1%

profile of v5, /device:TPU:1, one launch (start us, length us, event | category | flops | bytes accessed | tf_op | source)
XLA Modules:
  0.0 227.2 jit_solution(6872214289453421306)
XLA Ops:
  6.5 0.8 select_reduce_fusion
  7.3 0.9 fusion.26
  8.3 3.9 %collective-permute-start = (bf16[400,128]{1,0:T(8,128)(2,1)S(1)}, bf16[400,128]{1,0:T(8,128)(2,1)S(1)}, u32[]{:S(2)}, u32[]{:S(2)}) collective-permute-start(bf16[400,128]{1,0:T(8,128)(2,1)S(1)} %get-tuple-element.57), channel_id=1, source_target_pairs={{0,64},{64,128},{128,192},{192,0},{1,65},{65,129},{129,193},{193,1... | collective-permute-start | bytes 307208 | tf_op jit(solution)/shard_map/ppermute | solution.py:29
  12.2 4.4 %collective-permute-start.1 = (bf16[400,128]{1,0:T(8,128)(2,1)S(1)}, bf16[400,128]{1,0:T(8,128)(2,1)S(1)}, u32[]{:S(2)}, u32[]{:S(2)}) collective-permute-start(bf16[400,128]{1,0:T(8,128)(2,1)S(1)} %get-tuple-element.57), channel_id=1, source_target_pairs={{0,128},{64,192},{128,0},{192,64},{1,129},{65,193},{129,1},{193,65... | collective-permute-start | bytes 307208 | tf_op jit(solution)/shard_map/ppermute | solution.py:29
  16.6 3.1 %collective-permute-start.2 = (bf16[400,128]{1,0:T(8,128)(2,1)S(1)}, bf16[400,128]{1,0:T(8,128)(2,1)S(1)}, u32[]{:S(2)}, u32[]{:S(2)}) collective-permute-start(bf16[400,128]{1,0:T(8,128)(2,1)S(1)} %get-tuple-element.57), channel_id=1, source_target_pairs={{0,192},{64,0},{128,64},{192,128},{1,193},{65,1},{129,65},{193,129... | collective-permute-start | bytes 307208 | tf_op jit(solution)/shard_map/ppermute | solution.py:29
  19.6 1.9 copy.43
  21.5 0.7 collective-permute-done.2
  22.3 0.1 slice_bitcast_fusion.1
  22.5 1.5 pad_maximum_fusion
  24.0 1.0 constant_dynamic-slice_fusion
  25.2 0.8 pad_maximum_fusion.2
  26.0 7.1 %collective-permute-start.3 = (bf16[1206,128]{1,0:T(8,128)(2,1)}, bf16[1206,128]{1,0:T(8,128)(2,1)S(1)}, u32[]{:S(2)}, u32[]{:S(2)}) collective-permute-start(bf16[1206,128]{1,0:T(8,128)(2,1)} %pad_maximum_fusion.2), channel_id=1, source_target_pairs={{0,256},{256,0},{1,257},{257,1},{2,258},{258,2},{3,259},{259,3},{4... | collective-permute-start | bytes 926216 | tf_op jit(solution)/shard_map/ppermute | solution.py:24
  33.1 0.6 copy.41
  33.7 1.6 copy.36
  35.3 10.0 %all-to-all-start = ((bf16[8,64,1024]{2,1,0:T(8,128)(2,1)}), bf16[8,64,1024]{2,1,0:T(8,128)(2,1)S(1)}, u32[]{:S(2)}, u32[]{:S(2)}) async-start(bf16[8,64,1024]{2,1,0:T(8,128)(2,1)} %copy.36), calls=%async_computation | async-start | bytes 2097152 | tf_op jit(solution)/shard_map/all_to_all | solution.py:221
  45.5 1.3 fusion.29
  46.8 1.1 fusion.1
  47.9 1.5 fusion.4
  49.5 4.4 %collective-permute-start.4 = (bf16[384,128]{1,0:T(8,128)(2,1)S(1)}, bf16[384,128]{1,0:T(8,128)(2,1)S(1)}, u32[]{:S(2)}, u32[]{:S(2)}) collective-permute-start(bf16[384,128]{1,0:T(8,128)(2,1)S(1)} %get-tuple-element.51), channel_id=1, source_target_pairs={{0,192},{64,0},{128,64},{192,128},{1,193},{65,1},{129,65},{193,129... | collective-permute-start | bytes 294920 | tf_op jit(solution)/shard_map/ppermute | solution.py:29
  53.9 2.6 %collective-permute-start.5 = (bf16[384,128]{1,0:T(8,128)(2,1)S(1)}, bf16[384,128]{1,0:T(8,128)(2,1)S(1)}, u32[]{:S(2)}, u32[]{:S(2)}) collective-permute-start(bf16[384,128]{1,0:T(8,128)(2,1)S(1)} %get-tuple-element.53), channel_id=1, source_target_pairs={{0,128},{64,192},{128,0},{192,64},{1,129},{65,193},{129,1},{193,65... | collective-permute-start | bytes 294920 | tf_op jit(solution)/shard_map/ppermute | solution.py:29
  56.5 1.9 collective-permute-start.6
  58.5 4.7 %collective-permute-done.5 = bf16[384,128]{1,0:T(8,128)(2,1)S(1)} collective-permute-done((bf16[384,128]{1,0:T(8,128)(2,1)S(1)}, bf16[384,128]{1,0:T(8,128)(2,1)S(1)}, u32[]{:S(2)}, u32[]{:S(2)}) %collective-permute-start.5) | collective-permute-done | bytes 98336 | tf_op jit(solution)/shard_map/ppermute | solution.py:29
  63.2 3.6 %collective-permute-done.6 = bf16[384,128]{1,0:T(8,128)(2,1)S(1)} collective-permute-done((bf16[384,128]{1,0:T(8,128)(2,1)S(1)}, bf16[384,128]{1,0:T(8,128)(2,1)S(1)}, u32[]{:S(2)}, u32[]{:S(2)}) %collective-permute-start.6) | collective-permute-done | bytes 98336 | tf_op jit(solution)/shard_map/ppermute | solution.py:29
  66.8 0.1 add_convert_fusion
  66.9 1.9 collective-permute-start.7
  68.8 4.6 %collective-permute-start.8 = (bf16[128,4096]{1,0:T(8,128)(2,1)S(1)}, bf16[128,4096]{1,0:T(8,128)(2,1)}, u32[]{:S(2)}, u32[]{:S(2)}) collective-permute-start(bf16[128,4096]{1,0:T(8,128)(2,1)S(1)} %bitcast.39), channel_id=1, source_target_pairs={{0,192},{64,0},{128,64},{192,128},{1,193},{65,1},{129,65},{193,129... | collective-permute-start | bytes 3145736 | tf_op jit(solution)/shard_map/ppermute | solution.py:29
  73.4 19.9 %all_gather.9 = bf16[384,1024]{1,0:T(8,128)(2,1)} all-gather(bf16[384,128]{1,0:T(8,128)(2,1)S(1)} %add_convert_fusion), channel_id=1, replica_groups=mesh['yh'=2,'x'=4,'z'=8,'yl'=4,'core'=2] {'yl','core'}, dimensions={1}, use_global_device_ids=true | all-gather | bytes 884736 | tf_op jit(solution)/shard_map/all_gather | solution.py:238
  93.3 1.8 fusion.6
  95.1 1.0 copy.37
  96.0 10.0 %all-to-all-start.1 = ((bf16[8,64,384]{2,1,0:T(8,128)(2,1)}), bf16[8,64,384]{2,1,0:T(8,128)(2,1)S(1)}, u32[]{:S(2)}, u32[]{:S(2)}) async-start(bf16[8,64,384]{2,1,0:T(8,128)(2,1)} %bitcast.13), calls=%async_computation.1 | async-start | bytes 786432 | tf_op jit(solution)/shard_map/all_to_all | solution.py:242
  106.0 0.1 copy.38
  106.1 0.1 eq.36
  106.3 0.4 fusion.8
  106.7 0.2 convert_element_type.66
  106.9 0.1 copy.39
  107.0 0.1 copy.40.gate
  107.1 14.1 %all-to-all-done.1.parts = bf16[8,64,384]{2,1,0:T(8,128)(2,1)S(1)} async-done(((bf16[8,64,384]{2,1,0:T(8,128)(2,1)}), bf16[8,64,384]{2,1,0:T(8,128)(2,1)S(1)}, u32[]{:S(2)}, u32[]{:S(2)}) %all-to-all-start.1) | async-done | bytes 393248 | tf_op jit(solution)/shard_map/all_to_all | solution.py:242
  121.2 2.1 shard_map.136
  123.2 14.2 %all-to-all-start.2 = ((bf16[128,18,128]{2,1,0:T(8,128)(2,1)}), bf16[128,18,128]{2,1,0:T(8,128)(2,1)S(1)}, u32[]{:S(2)}, u32[]{:S(2)}) async-start(bf16[128,18,128]{2,1,0:T(8,128)(2,1)} %get-tuple-element.35), calls=%async_computation.2 | async-start | bytes 1572864 | tf_op jit(solution)/shard_map/all_to_all | solution.py:254
  137.5 3.9 %collective-permute-start.9 = (bf16[128,4096]{1,0:T(8,128)(2,1)S(1)}, bf16[128,4096]{1,0:T(8,128)(2,1)S(1)}, u32[]{:S(2)}, u32[]{:S(2)}) collective-permute-start(bf16[128,4096]{1,0:T(8,128)(2,1)S(1)} %bitcast.40), channel_id=1, source_target_pairs={{0,128},{64,192},{128,0},{192,64},{1,129},{65,193},{129,1},{193,65... | collective-permute-start | bytes 3145736 | tf_op jit(solution)/shard_map/ppermute | solution.py:29
  141.4 25.8 %collective-permute-done.9.rest_2_ = bf16[128,4096]{1,0:T(8,128)(2,1)S(1)} collective-permute-done((bf16[128,4096]{1,0:T(8,128)(2,1)S(1)}, bf16[128,4096]{1,0:T(8,128)(2,1)S(1)}, u32[]{:S(2)}, u32[]{:S(2)}) %collective-permute-start.9) | collective-permute-done | bytes 1048608 | tf_op jit(solution)/shard_map/ppermute | solution.py:29
  167.2 1.0 copy-done.3
  168.2 0.6 shard_map.137.normed
  168.9 3.4 %copy-done = bf16[32768,128]{1,0:T(8,128)(2,1)S(1)} copy-done((bf16[32768,128]{1,0:T(8,128)(2,1)S(1)}, bf16[32768,128]{1,0:T(8,128)(2,1)}, u32[]{:S(2)}) %copy-start) | copy-done | bytes 8388632
  172.2 1.2 copy-done.4
  173.5 5.6 %shard_map.138 = bf16[128,18,128]{2,1,0:T(8,128)(2,1)S(1)} custom-call(s32[1]{0:T(128)} %bitcast.place, bf16[96,4096]{1,0:T(8,128)(2,1)S(1)} %shard_map.137.normed, bf16[4,8192,128]{2,1,0:T(8,128)(2,1)S(1)} %bitcast.37, bf16[128,4096]{1,0:T(8,128)(2,1)S(1)} %bitcast.41, bf16[128,4096]{1,0:T(8,128)(2,1)} %collective-permute-done.7.rest_1_, ...), custom_call_target="tpu_custom_call" | custom-call | tf_op jit(solution)/shard_map/pallas_call | solution.py:264
  179.0 39.5 %all_to_all.20.back = bf16[128,18,128]{2,1,0:T(8,128)(2,1)S(1)} all-to-all(bf16[128,18,128]{2,1,0:T(8,128)(2,1)S(1)} %shard_map.138), channel_id=1, replica_groups=mesh['yh'=2,'x'=4,'z'=8,'yl'=4,'core'=2] {'yh','z','yl','core'}, dimensions={0} | all-to-all | bytes 1179648 | tf_op jit(solution)/shard_map/all_to_all | solution.py:280
  218.5 1.8 shard_map.139
  (44 shorter events, 0.4 us)
Async XLA Ops:
  6.5 162.3 %all-gather.3.cloned.1.call-start = ((), (), s32[]{:S(2)}) async-start(), calls=%async_computation.4 | async-start | bytes 10485760 | tf_op jit(solution)/shard_map/all_gather | solution.py:219
  8.3 13.3 %collective-permute-start = (bf16[400,128]{1,0:T(8,128)(2,1)S(1)}, bf16[400,128]{1,0:T(8,128)(2,1)S(1)}, u32[]{:S(2)}, u32[]{:S(2)}) collective-permute-start(bf16[400,128]{1,0:T(8,128)(2,1)S(1)} %get-tuple-element.57), channel_id=1, source_target_pairs={{0,64},{64,128},{128,192},{192,0},{1,65},{65,129},{129,193},{193,1... | collective-permute-start | bytes 307208 | tf_op jit(solution)/shard_map/ppermute | solution.py:29
  12.2 9.3 %collective-permute-start.1 = (bf16[400,128]{1,0:T(8,128)(2,1)S(1)}, bf16[400,128]{1,0:T(8,128)(2,1)S(1)}, u32[]{:S(2)}, u32[]{:S(2)}) collective-permute-start(bf16[400,128]{1,0:T(8,128)(2,1)S(1)} %get-tuple-element.57), channel_id=1, source_target_pairs={{0,128},{64,192},{128,0},{192,64},{1,129},{65,193},{129,1},{193,65... | collective-permute-start | bytes 307208 | tf_op jit(solution)/shard_map/ppermute | solution.py:29
  16.6 5.7 %collective-permute-start.2 = (bf16[400,128]{1,0:T(8,128)(2,1)S(1)}, bf16[400,128]{1,0:T(8,128)(2,1)S(1)}, u32[]{:S(2)}, u32[]{:S(2)}) collective-permute-start(bf16[400,128]{1,0:T(8,128)(2,1)S(1)} %get-tuple-element.57), channel_id=1, source_target_pairs={{0,192},{64,0},{128,64},{192,128},{1,193},{65,1},{129,65},{193,129... | collective-permute-start | bytes 307208 | tf_op jit(solution)/shard_map/ppermute | solution.py:29
  21.5 11.6 %copy-start.8 = (bf16[8192,64]{0,1:T(8,128)(2,1)S(1)}, bf16[8192,64]{0,1:T(8,128)(2,1)}, u32[]{:S(2)}) copy-start(bf16[8192,64]{0,1:T(8,128)(2,1)} %param.23) | copy-start | bytes 3145732
  26.0 19.5 %collective-permute-start.3 = (bf16[1206,128]{1,0:T(8,128)(2,1)}, bf16[1206,128]{1,0:T(8,128)(2,1)S(1)}, u32[]{:S(2)}, u32[]{:S(2)}) collective-permute-start(bf16[1206,128]{1,0:T(8,128)(2,1)} %pad_maximum_fusion.2), channel_id=1, source_target_pairs={{0,256},{256,0},{1,257},{257,1},{2,258},{258,2},{3,259},{259,3},{4... | collective-permute-start | bytes 926216 | tf_op jit(solution)/shard_map/ppermute | solution.py:24
  35.3 58.0 %all-to-all-start = ((bf16[8,64,1024]{2,1,0:T(8,128)(2,1)}), bf16[8,64,1024]{2,1,0:T(8,128)(2,1)S(1)}, u32[]{:S(2)}, u32[]{:S(2)}) async-start(bf16[8,64,1024]{2,1,0:T(8,128)(2,1)} %copy.36), calls=%async_computation | async-start | bytes 2097152 | tf_op jit(solution)/shard_map/all_to_all | solution.py:221
  47.9 19.0 %copy-start.2 = (bf16[1,128,4096]{2,1,0:T(8,128)(2,1)S(1)}, bf16[1,128,4096]{2,1,0:T(8,128)(2,1)}, u32[]{:S(2)}) copy-start(bf16[1,128,4096]{2,1,0:T(8,128)(2,1)} %param.28) | copy-start | bytes 3145732
  47.9 58.1 %copy-start.9 = (s32[384,2]{0,1:T(2,128)S(1)}, s32[384,2]{0,1:T(2,128)}, u32[]{:S(2)}) copy-start(s32[384,2]{0,1:T(2,128)} %param.25) | copy-start | bytes 9220
  49.4 57.5 %copy-start.10 = (f32[64]{0:T(128)S(1)}, f32[64]{0:T(128)}, u32[]{:S(2)}) copy-start(f32[64]{0:T(128)} %param.22) | copy-start | bytes 772
  49.4 71.7 %copy-start.1 = (s32[1536,1]{1,0:T(8,128)S(1)}, s32[1536,1]{1,0:T(8,128)}, u32[]{:S(2)}) copy-start(s32[1536,1]{1,0:T(8,128)} %constant.81.clone.rows) | copy-start | bytes 18436
  49.4 71.7 %copy-start.5 = (bf16[384,64]{0,1:T(8,128)(2,1)S(1)}, bf16[384,64]{0,1:T(8,128)(2,1)}, u32[]{:S(2)}) copy-start(bf16[384,64]{0,1:T(8,128)(2,1)} %param.16) | copy-start | bytes 147460
  49.5 118.8 %copy-start.6 = (f32[4096]{0:T(1024)S(1)}, f32[4096]{0:T(1024)}, u32[]{:S(2)}) copy-start(f32[4096]{0:T(1024)} %param.24) | copy-start | bytes 49156
  49.5 9.0 %collective-permute-start.4 = (bf16[384,128]{1,0:T(8,128)(2,1)S(1)}, bf16[384,128]{1,0:T(8,128)(2,1)S(1)}, u32[]{:S(2)}, u32[]{:S(2)}) collective-permute-start(bf16[384,128]{1,0:T(8,128)(2,1)S(1)} %get-tuple-element.51), channel_id=1, source_target_pairs={{0,192},{64,0},{128,64},{192,128},{1,193},{65,1},{129,65},{193,129... | collective-permute-start | bytes 294920 | tf_op jit(solution)/shard_map/ppermute | solution.py:29
  53.9 9.2 %collective-permute-start.5 = (bf16[384,128]{1,0:T(8,128)(2,1)S(1)}, bf16[384,128]{1,0:T(8,128)(2,1)S(1)}, u32[]{:S(2)}, u32[]{:S(2)}) collective-permute-start(bf16[384,128]{1,0:T(8,128)(2,1)S(1)} %get-tuple-element.53), channel_id=1, source_target_pairs={{0,128},{64,192},{128,0},{192,64},{1,129},{65,193},{129,1},{193,65... | collective-permute-start | bytes 294920 | tf_op jit(solution)/shard_map/ppermute | solution.py:29
  56.5 10.2 %collective-permute-start.6 = (bf16[384,128]{1,0:T(8,128)(2,1)S(1)}, bf16[384,128]{1,0:T(8,128)(2,1)S(1)}, u32[]{:S(2)}, u32[]{:S(2)}) collective-permute-start(bf16[384,128]{1,0:T(8,128)(2,1)S(1)} %get-tuple-element.52), channel_id=1, source_target_pairs={{0,64},{64,128},{128,192},{192,0},{1,65},{65,129},{129,193},{193,1... | collective-permute-start | bytes 294920 | tf_op jit(solution)/shard_map/ppermute | solution.py:29
  66.9 56.4 %collective-permute-start.7 = (bf16[128,4096]{1,0:T(8,128)(2,1)S(1)}, bf16[128,4096]{1,0:T(8,128)(2,1)}, u32[]{:S(2)}, u32[]{:S(2)}) collective-permute-start(bf16[128,4096]{1,0:T(8,128)(2,1)S(1)} %bitcast.38), channel_id=1, source_target_pairs={{0,64},{64,128},{128,192},{192,0},{1,65},{65,129},{129,193},{193,1... | collective-permute-start | bytes 3145736 | tf_op jit(solution)/shard_map/ppermute | solution.py:29
  68.8 54.4 %collective-permute-start.8 = (bf16[128,4096]{1,0:T(8,128)(2,1)S(1)}, bf16[128,4096]{1,0:T(8,128)(2,1)}, u32[]{:S(2)}, u32[]{:S(2)}) collective-permute-start(bf16[128,4096]{1,0:T(8,128)(2,1)S(1)} %bitcast.39), channel_id=1, source_target_pairs={{0,192},{64,0},{128,64},{192,128},{1,193},{65,1},{129,65},{193,129... | collective-permute-start | bytes 3145736 | tf_op jit(solution)/shard_map/ppermute | solution.py:29
  96.0 25.1 %all-to-all-start.1 = ((bf16[8,64,384]{2,1,0:T(8,128)(2,1)}), bf16[8,64,384]{2,1,0:T(8,128)(2,1)S(1)}, u32[]{:S(2)}, u32[]{:S(2)}) async-start(bf16[8,64,384]{2,1,0:T(8,128)(2,1)} %bitcast.13), calls=%async_computation.1 | async-start | bytes 786432 | tf_op jit(solution)/shard_map/all_to_all | solution.py:242
  123.2 45.0 %all-to-all-start.2 = ((bf16[128,18,128]{2,1,0:T(8,128)(2,1)}), bf16[128,18,128]{2,1,0:T(8,128)(2,1)S(1)}, u32[]{:S(2)}, u32[]{:S(2)}) async-start(bf16[128,18,128]{2,1,0:T(8,128)(2,1)} %get-tuple-element.35), calls=%async_computation.2 | async-start | bytes 1572864 | tf_op jit(solution)/shard_map/all_to_all | solution.py:254
  137.5 29.7 %collective-permute-start.9 = (bf16[128,4096]{1,0:T(8,128)(2,1)S(1)}, bf16[128,4096]{1,0:T(8,128)(2,1)S(1)}, u32[]{:S(2)}, u32[]{:S(2)}) collective-permute-start(bf16[128,4096]{1,0:T(8,128)(2,1)S(1)} %bitcast.40), channel_id=1, source_target_pairs={{0,128},{64,192},{128,0},{192,64},{1,129},{65,193},{129,1},{193,65... | collective-permute-start | bytes 3145736 | tf_op jit(solution)/shard_map/ppermute | solution.py:29
  167.2 1.0 copy-start.3
  168.8 3.4 %copy-start = (bf16[32768,128]{1,0:T(8,128)(2,1)S(1)}, bf16[32768,128]{1,0:T(8,128)(2,1)}, u32[]{:S(2)}) copy-start(bf16[32768,128]{1,0:T(8,128)(2,1)} %all-gather.3.cloned.1.call-done) | copy-start | bytes 25165828
  172.2 1.2 copy-start.4
  173.5 45.0 %copy-start.7 = (s32[384,2]{0,1:T(2,128)S(1)}, s32[384,2]{0,1:T(2,128)}, u32[]{:S(2)}) copy-start(s32[384,2]{0,1:T(2,128)} %param.26) | copy-start | bytes 9220
Sparse Core Ops, SparseCore 0:
  24.2 121.4 all-gather.2

commit v6 on v5

--- a/solution.py
+++ b/solution.py
@@ -94,37 +94,36 @@
     normed[...] = (rows * lax.rsqrt(mean_square + NORM_EPSILON) * gain[...]).astype(bf16)
 
 
-def expert_kernel(experts, half, padded, place, normed, weights, *rest):
-    del place
-    *downs, out, wide = rest
-    step = pl.program_id(0)
+def expert_kernel(experts, half, padded, place, normed, own, left_in, right_in, far_gate, far_up, downs, out, wide):
+    nx = downs.shape[0]
     inner = normed.shape[1]
-    gate = jnp.dot(normed[...], weights[0, :inner], preferred_element_type=f32)
-    up = jnp.dot(normed[...], weights[0, inner:], preferred_element_type=f32)
-    act = (gate / (1.0 + jnp.exp(-gate)) * up).astype(bf16)
-    for k, down in enumerate(downs):
-
-        @pl.when(step == k)
-        def _():
-            product = jnp.dot(act, down[...], preferred_element_type=f32)
-            wide[...] = product if k == 0 else wide[...] + product
-
-    @pl.when(step == len(downs) - 1)
-    def _():
-        lanes = out.shape[2]
-        left = lax.broadcasted_iota(jnp.int32, (half, lanes), 1) < lanes // 2
-        for group in range(out.shape[0] // experts):
-            for pair in range(experts // 2):
-                cols = pl.ds(pair * lanes, lanes)
-                at = 2 * group * padded
-                low = wide[pl.ds(at, half), cols]
-                high = wide[pl.ds(at + padded, half), cols]
-                out[group * experts + 2 * pair] = jnp.where(
-                    left, low, pltpu.roll(high, lanes // 2, 1)
-                ).astype(bf16)
-                out[group * experts + 2 * pair + 1] = jnp.where(
-                    left, pltpu.roll(low, lanes // 2, 1), high
-                ).astype(bf16)
+    rows = normed[...]
+    for k, (gates, ups) in enumerate(
+        (
+            (own.at[:inner], own.at[inner:]),
+            (left_in.at[:inner], left_in.at[inner:]),
+            (right_in.at[:inner], right_in.at[inner:]),
+            (far_gate, far_up),
+        )
+    ):
+        gate = jnp.dot(rows, gates[...], preferred_element_type=f32)
+        up = jnp.dot(rows, ups[...], preferred_element_type=f32)
+        act = (gate / (1.0 + jnp.exp(-gate)) * up).astype(bf16)
+        origin = (place[0] + (0, nx - 1, 1, 2)[k]) % nx
+        product = jnp.dot(act, downs[origin], preferred_element_type=f32)
+        wide[...] = product if k == 0 else wide[...] + product
+    lanes = out.shape[2]
+    left = lax.broadcasted_iota(jnp.int32, (half, lanes), 1) < lanes // 2
+    for group in range(out.shape[0] // experts):
+        for pair in range(experts // 2):
+            cols = pl.ds(pair * lanes, lanes)
+            at = 2 * group * padded
+            low = wide[pl.ds(at, half), cols]
+            high = wide[pl.ds(at + padded, half), cols]
+            out[group * experts + 2 * pair] = jnp.where(left, low, pltpu.roll(high, lanes // 2, 1)).astype(bf16)
+            out[group * experts + 2 * pair + 1] = jnp.where(
+                left, pltpu.roll(low, lanes // 2, 1), high
+            ).astype(bf16)
 
 
 def combine_kernel(experts, half, padded, back, mid, slots, fixed, rows, out, table):
@@ -204,19 +203,17 @@
         ],
         axis=0,
     )
-    other = swap(own, "yh")
-    half = held * frame_rows
-    keys = jnp.concatenate([own[:half], other[:half]], axis=0)
-    values = jnp.concatenate([own[half:], other[half:]], axis=0)
     frame_cols = lax.broadcasted_iota(jnp.int32, (tokens, frame_slot.shape[0]), 1)
     token_slot = jnp.sum(jnp.where(cited_frame[:, None] == frame_cols, frame_slot[None, :], 0), axis=1)
     slot_rows = jnp.zeros((16, head), bf16).at[: tokens // head].set(
         token_slot.reshape(tokens // head, head).astype(bf16)
     )
-    packed = jnp.concatenate([queries, slot_rows])
+    packed, own = tie(jnp.concatenate([queries, slot_rows]), own)
+    other = swap(own, "yh")
     gathered = jnp.stack([packed] + [shift(packed, "x", k) for k in range(1, nx)])
+    down_all = lax.all_gather(w_down[0], "x")
     gathered, wide_in = tie(gathered, w_in[0])
-    in_all = lax.all_gather(jnp.concatenate([wide_in[:, 0], wide_in[:, 1]], axis=0), "x")
+    own_in = jnp.concatenate([wide_in[:, 0], wide_in[:, 1]], axis=0)
     turned = out_weight.T.reshape(feats, nz, near * head).transpose(1, 0, 2)
     near_weight = lax.all_to_all(turned, "z", 0, 0, tiled=True).reshape(nz * feats, near * head)
     all_queries = gathered[:, :tokens].reshape(nx * tokens, head)
@@ -228,13 +225,16 @@
         own_frame,
         jnp.where((other_frame >= 0) & (other_frame < held), other_frame + held, -1),
     )
+    half = held * frame_rows
+    keys = jnp.concatenate([own[:half], other[:half]], axis=0)
+    values = jnp.concatenate([own[half:], other[half:]], axis=0)
     mixed = attention(all_queries, keys, values, local_frame, frame_rows)
     back = mixed.reshape(nx, tokens, head)
     attended = sum(
         (shift(back[k], "x", -k) if k else back[k]).astype(f32) for k in range(nx)
     ).astype(bf16)
-    attended, own_down = tie(attended, w_down[0])
-    down_pieces = [own_down] + [shift(own_down, "x", k) for k in range(1, nx)]
+    attended, own_in = tie(attended, own_in)
+    left_in, right_in = shift(own_in, "x", 1), shift(own_in, "x", -1)
     heads = lax.all_gather(attended, NEAR, axis=1, tiled=True)
     partial = lax.dot_general(
         near_weight, heads, (((1,), (1,)), ((), ())), preferred_element_type=f32
@@ -250,9 +250,10 @@
         jax.ShapeDtypeStruct((feats, tokens), bf16),
         jax.ShapeDtypeStruct((nh * experts, half, lanes), bf16),
     )(parts, hidden_in.T, attn_gate[:, None], slots, table)
-    sent, down_pieces[1], down_pieces[3] = tie(sent, down_pieces[1], down_pieces[3])
+    sent, left_in, right_in = tie(sent, left_in, right_in)
+    width = w_in.shape[1]
+    far_gate, far_up = shift(left_in[:width], "x", 1), shift(right_in[width:], "x", -1)
     came = lax.all_to_all(sent, BOTH, 0, 0, tiled=True)
-    came, *down_pieces = tie(came, *down_pieces)
     rows = 2 * nh * padded
     (normed,) = local_kernel(
         functools.partial(assemble_kernel, experts, half, padded),
@@ -260,23 +261,15 @@
         scratch=(pltpu.VMEM((rows, experts * feats), f32),),
     )(came, mlp_gain[None])
 
-    whole = lambda v: pl.BlockSpec(v.shape, lambda k, place: (0,) * v.ndim)
+    in_vmem = pl.BlockSpec(memory_space=pltpu.VMEM)
     dealt = pl.pallas_call(
         functools.partial(expert_kernel, experts, half, padded),
-        grid_spec=pltpu.PrefetchScalarGridSpec(
-            num_scalar_prefetch=1,
-            grid=(nx,),
-            in_specs=[
-                whole(normed),
-                pl.BlockSpec((1,) + in_all.shape[1:], lambda k, place: ((place[0] + nx - k) % nx, 0, 0)),
-            ]
-            + [whole(piece) for piece in down_pieces],
-            out_specs=whole(came),
-            scratch_shapes=[pltpu.VMEM((rows, experts * feats), f32)],
-        ),
+        in_specs=[pl.BlockSpec(memory_space=pltpu.SMEM)] + [in_vmem] * 7,
+        out_specs=in_vmem,
         out_shape=jax.ShapeDtypeStruct(came.shape, bf16),
+        scratch_shapes=[pltpu.VMEM((rows, experts * feats), f32)],
         compiler_params=pltpu.CompilerParams(vmem_limit_bytes=40 * 1024 * 1024),
-    )(x[None], normed, in_all, *down_pieces)
+    )(x[None], normed, own_in, left_in, right_in, far_gate, far_up, down_all)
     back_sums = lax.all_to_all(dealt, BOTH, 0, 0, tiled=True)
     (out,) = local_kernel(
         functools.partial(combine_kernel, experts, half, padded),

time: 228 us -> 248 us (1.088)
  waiting for transfers between devices: 48.9 us -> 62 us
  local copies, waits for them, and re-layouts: 12.7 us -> 24.1 us
  starting transfers between devices: 72.1 us -> 68.3 us
    all_to_all x1, waiting for transfers between devices: 0.01 us -> 15.4 us  [per_device(): came = lax.all_to_all(sent, BOTH, 0, 0, tiled=True)]
    slice x0 -> x2, local copies, waits for them, and re-layouts: none -> 4.58 us  [the longest x1 2.31 us: per_device(): left_in[:width]]
    all_to_all x1, waiting for transfers between devices: 14.1 us -> 10.8 us  [per_device(): lax.all_to_all(partial.reshape(nz, feats, tokens), 'z', 0, 0, tiled=True)]
    all_to_all x1, starting transfers between devices: 9.96 us -> 6.83 us  [per_device(): lax.all_to_all(partial.reshape(nz, feats, tokens), 'z', 0, 0, tiled=True)]
    unnamed x25 -> x29, local copies, waits for them, and re-layouts: 8.27 us -> 9.8 us
    ppermute x9 -> x10, waiting for transfers between devices: 34.8 us -> 35.2 us  [shift(): return lax.ppermute(v, axis, [(i, (i + by) % n) for i in range(n)])]
    ppermute x9 -> x10, starting transfers between devices: 30.8 us -> 31 us  [shift(): return lax.ppermute(v, axis, [(i, (i + by) % n) for i in range(n)])]
  transfers between devices with their start and end apart: 14 -> 15, of which waited for: 5 -> 7; matrix products, arithmetic and copies ran while one was open for 6% -> 10% of each run, Pallas kernels for 1% -> 1%
where the time goes in v6:
time: 248 us; the launch traced here: 247 us
  starting transfers between devices  68.3 us (28%)
  waiting for transfers between devices  62 us (25%)
  blocking collectives  59.3 us (24%)
  local copies, waits for them, and re-layouts  24.1 us (10%)
  between operations  13.8 us (6%)
  Pallas kernels  9.74 us (4%)
  matrix products  6.17 us (2%)
  other arithmetic  3.12 us (1%)
    all_to_all x1, blocking collectives, per_device(): back_sums = lax.all_to_all(dealt, BOTH, 0, 0, tiled=True)  40.6 us
    ppermute x10, waiting for transfers between devices, shift(): return lax.ppermute(v, axis, [(i, (i + by) % n) for i in range(n)])  35.2 us
    ppermute x10, starting transfers between devices, shift(): return lax.ppermute(v, axis, [(i, (i + by) % n) for i in range(n)])  31 us
    all_gather x1, blocking collectives, per_device(): heads = lax.all_gather(attended, NEAR, axis=1, tiled=True)  18.7 us
    all_to_all x1, waiting for transfers between devices, per_device(): came = lax.all_to_all(sent, BOTH, 0, 0, tiled=True)  15.4 us
    all_to_all x1, starting transfers between devices, per_device(): came = lax.all_to_all(sent, BOTH, 0, 0, tiled=True)  13 us
    all_to_all x1, waiting for transfers between devices, per_device(): lax.all_to_all(partial.reshape(nz, feats, tokens), 'z', 0, 0, tiled=True)  10.8 us
    all_to_all x1, starting transfers between devices, per_device(): lax.all_to_all(turned, 'z', 0, 0, tiled=True)  10 us
  transfers between devices with their start and end apart: 15, of which 7 were waited for; matrix products, arithmetic and copies ran while one was open for 10% of the time, Pallas kernels for 1%

profile of v6, /device:TPU:1, one launch (start us, length us, event | category | flops | bytes accessed | tf_op | source)
XLA Modules:
  0.0 246.5 jit_solution(9141557114457405050)
XLA Ops:
  6.5 1.0 constant_dynamic-slice_fusion
  7.7 0.8 select_reduce_fusion
  8.5 0.9 fusion.16
  9.4 3.9 %collective-permute-start = (bf16[400,128]{1,0:T(8,128)(2,1)S(1)}, bf16[400,128]{1,0:T(8,128)(2,1)S(1)}, u32[]{:S(2)}, u32[]{:S(2)}) collective-permute-start(bf16[400,128]{1,0:T(8,128)(2,1)S(1)} %fusion.16), channel_id=1, source_target_pairs={{0,64},{64,128},{128,192},{192,0},{1,65},{65,129},{129,193},{193,1... | collective-permute-start | bytes 307208 | tf_op jit(solution)/shard_map/ppermute | solution.py:29
  13.4 4.4 %collective-permute-start.1 = (bf16[400,128]{1,0:T(8,128)(2,1)S(1)}, bf16[400,128]{1,0:T(8,128)(2,1)S(1)}, u32[]{:S(2)}, u32[]{:S(2)}) collective-permute-start(bf16[400,128]{1,0:T(8,128)(2,1)S(1)} %fusion.16), channel_id=1, source_target_pairs={{0,128},{64,192},{128,0},{192,64},{1,129},{65,193},{129,1},{193,65... | collective-permute-start | bytes 307208 | tf_op jit(solution)/shard_map/ppermute | solution.py:29
  17.7 3.1 %collective-permute-start.2 = (bf16[400,128]{1,0:T(8,128)(2,1)S(1)}, bf16[400,128]{1,0:T(8,128)(2,1)S(1)}, u32[]{:S(2)}, u32[]{:S(2)}) collective-permute-start(bf16[400,128]{1,0:T(8,128)(2,1)S(1)} %fusion.16), channel_id=1, source_target_pairs={{0,192},{64,0},{128,64},{192,128},{1,193},{65,1},{129,65},{193,129... | collective-permute-start | bytes 307208 | tf_op jit(solution)/shard_map/ppermute | solution.py:29
  20.8 7.5 %collective-permute-start.3 = (bf16[1206,128]{1,0:T(8,128)(2,1)S(1)}, bf16[1206,128]{1,0:T(8,128)(2,1)}, u32[]{:S(2)}, u32[]{:S(2)}) collective-permute-start(bf16[1206,128]{1,0:T(8,128)(2,1)S(1)} %pad_maximum_fusion.2), channel_id=1, source_target_pairs={{0,256},{256,0},{1,257},{257,1},{2,258},{258,2},{3,259},{259,3},{4... | collective-permute-start | bytes 926216 | tf_op jit(solution)/shard_map/ppermute | solution.py:24
  28.3 1.8 copy.41
  30.1 1.6 copy.36
  31.7 10.0 %all-to-all-start = ((bf16[8,64,1024]{2,1,0:T(8,128)(2,1)}), bf16[8,64,1024]{2,1,0:T(8,128)(2,1)}, u32[]{:S(2)}, u32[]{:S(2)}) async-start(bf16[8,64,1024]{2,1,0:T(8,128)(2,1)} %copy.36), calls=%async_computation | async-start | bytes 2097152 | tf_op jit(solution)/shard_map/all_to_all | solution.py:218
  43.2 1.9 copy.43
  45.2 1.1 slice_bitcast_fusion.1
  46.4 1.0 fusion.30
  47.4 2.2 fusion.31
  49.6 1.1 fusion.1
  50.7 1.5 fusion.4
  52.3 1.9 collective-permute-start.4
  54.2 4.0 %collective-permute-start.5 = (bf16[384,128]{1,0:T(8,128)(2,1)S(1)}, bf16[384,128]{1,0:T(8,128)(2,1)S(1)}, u32[]{:S(2)}, u32[]{:S(2)}) collective-permute-start(bf16[384,128]{1,0:T(8,128)(2,1)S(1)} %get-tuple-element.47), channel_id=1, source_target_pairs={{0,128},{64,192},{128,0},{192,64},{1,129},{65,193},{129,1},{193,65... | collective-permute-start | bytes 294920 | tf_op jit(solution)/shard_map/ppermute | solution.py:29
  58.2 1.9 collective-permute-start.6
  60.3 3.3 %collective-permute-done.5 = bf16[384,128]{1,0:T(8,128)(2,1)S(1)} collective-permute-done((bf16[384,128]{1,0:T(8,128)(2,1)S(1)}, bf16[384,128]{1,0:T(8,128)(2,1)S(1)}, u32[]{:S(2)}, u32[]{:S(2)}) %collective-permute-start.5) | collective-permute-done | bytes 98336 | tf_op jit(solution)/shard_map/ppermute | solution.py:29
  63.6 4.6 %collective-permute-done.6 = bf16[384,128]{1,0:T(8,128)(2,1)S(1)} collective-permute-done((bf16[384,128]{1,0:T(8,128)(2,1)S(1)}, bf16[384,128]{1,0:T(8,128)(2,1)S(1)}, u32[]{:S(2)}, u32[]{:S(2)}) %collective-permute-start.6) | collective-permute-done | bytes 98336 | tf_op jit(solution)/shard_map/ppermute | solution.py:29
  68.3 1.9 collective-permute-start.7
  70.2 4.6 %collective-permute-start.8 = (bf16[8192,128]{1,0:T(8,128)(2,1)S(1)}, bf16[8192,128]{1,0:T(8,128)(2,1)}, u32[]{:S(2)}, u32[]{:S(2)}) collective-permute-start(bf16[8192,128]{1,0:T(8,128)(2,1)S(1)} %pad_maximum_fusion.own), channel_id=1, source_target_pairs={{0,192},{64,0},{128,64},{192,128},{1,193},{65,1},{129,65},{193,129... | collective-permute-start | bytes 6291464 | tf_op jit(solution)/shard_map/ppermute | solution.py:29
  74.8 18.7 %all_gather.6 = bf16[384,1024]{1,0:T(8,128)(2,1)} all-gather(bf16[384,128]{1,0:T(8,128)(2,1)S(1)} %add_convert_fusion), channel_id=1, replica_groups=mesh['yh'=2,'x'=4,'z'=8,'yl'=4,'core'=2] {'yl','core'}, dimensions={1}, use_global_device_ids=true | all-gather | bytes 884736 | tf_op jit(solution)/shard_map/all_gather | solution.py:238
  93.5 2.1 fusion.6
  95.6 1.0 copy.37
  96.6 6.8 %all-to-all-start.1 = ((bf16[8,64,384]{2,1,0:T(8,128)(2,1)}), bf16[8,64,384]{2,1,0:T(8,128)(2,1)S(1)}, u32[]{:S(2)}, u32[]{:S(2)}) async-start(bf16[8,64,384]{2,1,0:T(8,128)(2,1)} %bitcast.39), calls=%async_computation.1 | async-start | bytes 786432 | tf_op jit(solution)/shard_map/all_to_all | solution.py:242
  103.4 0.8 copy.38
  104.2 1.1 eq.36
  105.7 0.9 convert_element_type.66
  106.6 1.0 copy.39
  107.7 10.8 %all-to-all-done.1.parts = bf16[8,64,384]{2,1,0:T(8,128)(2,1)S(1)} async-done(((bf16[8,64,384]{2,1,0:T(8,128)(2,1)}), bf16[8,64,384]{2,1,0:T(8,128)(2,1)S(1)}, u32[]{:S(2)}, u32[]{:S(2)}) %all-to-all-start.1) | async-done | bytes 393248 | tf_op jit(solution)/shard_map/all_to_all | solution.py:242
  118.6 1.2 shard_map.136
  119.8 0.9 copy-done.5
  120.7 21.2 %collective-permute-done.7.left_in = bf16[8192,128]{1,0:T(8,128)(2,1)} collective-permute-done((bf16[8192,128]{1,0:T(8,128)(2,1)S(1)}, bf16[8192,128]{1,0:T(8,128)(2,1)}, u32[]{:S(2)}, u32[]{:S(2)}) %collective-permute-start.7) | collective-permute-done | bytes 2097184 | tf_op jit(solution)/shard_map/ppermute | solution.py:29
  141.9 13.0 %all-to-all-start.2 = ((bf16[128,18,128]{2,1,0:T(8,128)(2,1)}), bf16[128,18,128]{2,1,0:T(8,128)(2,1)S(1)}, u32[]{:S(2)}, u32[]{:S(2)}) async-start(bf16[128,18,128]{2,1,0:T(8,128)(2,1)} %copy-done.5), calls=%async_computation.2 | async-start | bytes 1572864 | tf_op jit(solution)/shard_map/all_to_all | solution.py:256
  154.9 2.3 slice.75
  157.2 2.4 collective-permute-start.10
  159.6 2.3 slice.74
  162.0 2.8 %collective-permute-start.9 = (bf16[4096,128]{1,0:T(8,128)(2,1)}, bf16[4096,128]{1,0:T(8,128)(2,1)}, u32[]{:S(2)}, u32[]{:S(2)}) collective-permute-start(bf16[4096,128]{1,0:T(8,128)(2,1)} %slice.74), channel_id=1, source_target_pairs={{0,64},{64,128},{128,192},{192,0},{1,65},{65,129},{129,193},{193,1... | collective-permute-start | bytes 3145736 | tf_op jit(solution)/shard_map/ppermute | solution.py:29
  164.8 15.4 %all-to-all-done.2.came = bf16[128,18,128]{2,1,0:T(8,128)(2,1)S(1)} async-done(((bf16[128,18,128]{2,1,0:T(8,128)(2,1)}), bf16[128,18,128]{2,1,0:T(8,128)(2,1)S(1)}, u32[]{:S(2)}, u32[]{:S(2)}) %all-to-all-start.2) | async-done | bytes 589856 | tf_op jit(solution)/shard_map/all_to_all | solution.py:256
  180.1 1.0 copy-done.3
  181.1 1.1 copy-done.4
  183.2 5.7 %collective-permute-done.9.far_gate = bf16[4096,128]{1,0:T(8,128)(2,1)} collective-permute-done((bf16[4096,128]{1,0:T(8,128)(2,1)}, bf16[4096,128]{1,0:T(8,128)(2,1)}, u32[]{:S(2)}, u32[]{:S(2)}) %collective-permute-start.9) | collective-permute-done | bytes 1048608 | tf_op jit(solution)/shard_map/ppermute | solution.py:29
  188.8 2.2 copy-done
  191.0 6.1 %shard_map.138 = bf16[128,18,128]{2,1,0:T(8,128)(2,1)S(1)} custom-call(s32[1]{0:T(128)} %bitcast.place, bf16[96,4096]{1,0:T(8,128)(2,1)S(1)} %shard_map.137.normed, bf16[8192,128]{1,0:T(8,128)(2,1)S(1)} %pad_maximum_fusion.own, bf16[8192,128]{1,0:T(8,128)(2,1)} %collective-permute-done.7.left_in, bf16[8192,128]{1,0:T(8,128)(2,1)} %collective-permute-done.8.right_in, ...), custom_call_target="tpu_custom_call" | custom-call | tf_op jit(solution)/shard_map/pallas_call | solution.py:265
  197.2 40.6 %all_to_all.20.back = bf16[128,18,128]{2,1,0:T(8,128)(2,1)S(1)} all-to-all(bf16[128,18,128]{2,1,0:T(8,128)(2,1)S(1)} %shard_map.138), channel_id=1, replica_groups=mesh['yh'=2,'x'=4,'z'=8,'yl'=4,'core'=2] {'yh','z','yl','core'}, dimensions={0} | all-to-all | bytes 1179648 | tf_op jit(solution)/shard_map/all_to_all | solution.py:273
  237.8 1.8 shard_map.139
  (53 shorter events, 3.5 us)
Async XLA Ops:
  9.4 35.7 %collective-permute-start = (bf16[400,128]{1,0:T(8,128)(2,1)S(1)}, bf16[400,128]{1,0:T(8,128)(2,1)S(1)}, u32[]{:S(2)}, u32[]{:S(2)}) collective-permute-start(bf16[400,128]{1,0:T(8,128)(2,1)S(1)} %fusion.16), channel_id=1, source_target_pairs={{0,64},{64,128},{128,192},{192,0},{1,65},{65,129},{129,193},{193,1... | collective-permute-start | bytes 307208 | tf_op jit(solution)/shard_map/ppermute | solution.py:29
  13.4 31.7 %collective-permute-start.1 = (bf16[400,128]{1,0:T(8,128)(2,1)S(1)}, bf16[400,128]{1,0:T(8,128)(2,1)S(1)}, u32[]{:S(2)}, u32[]{:S(2)}) collective-permute-start(bf16[400,128]{1,0:T(8,128)(2,1)S(1)} %fusion.16), channel_id=1, source_target_pairs={{0,128},{64,192},{128,0},{192,64},{1,129},{65,193},{129,1},{193,65... | collective-permute-start | bytes 307208 | tf_op jit(solution)/shard_map/ppermute | solution.py:29
  17.7 27.4 %collective-permute-start.2 = (bf16[400,128]{1,0:T(8,128)(2,1)S(1)}, bf16[400,128]{1,0:T(8,128)(2,1)S(1)}, u32[]{:S(2)}, u32[]{:S(2)}) collective-permute-start(bf16[400,128]{1,0:T(8,128)(2,1)S(1)} %fusion.16), channel_id=1, source_target_pairs={{0,192},{64,0},{128,64},{192,128},{1,193},{65,1},{129,65},{193,129... | collective-permute-start | bytes 307208 | tf_op jit(solution)/shard_map/ppermute | solution.py:29
  20.8 25.6 %collective-permute-start.3 = (bf16[1206,128]{1,0:T(8,128)(2,1)S(1)}, bf16[1206,128]{1,0:T(8,128)(2,1)}, u32[]{:S(2)}, u32[]{:S(2)}) collective-permute-start(bf16[1206,128]{1,0:T(8,128)(2,1)S(1)} %pad_maximum_fusion.2), channel_id=1, source_target_pairs={{0,256},{256,0},{1,257},{257,1},{2,258},{258,2},{3,259},{259,3},{4... | collective-permute-start | bytes 926216 | tf_op jit(solution)/shard_map/ppermute | solution.py:24
  31.7 61.8 %all-to-all-start = ((bf16[8,64,1024]{2,1,0:T(8,128)(2,1)}), bf16[8,64,1024]{2,1,0:T(8,128)(2,1)}, u32[]{:S(2)}, u32[]{:S(2)}) async-start(bf16[8,64,1024]{2,1,0:T(8,128)(2,1)} %copy.36), calls=%async_computation | async-start | bytes 2097152 | tf_op jit(solution)/shard_map/all_to_all | solution.py:218
  41.7 147.1 %all-gather.2.cloned.1.call-start = ((), (), s32[]{:S(2)}) async-start(), calls=%async_computation.4 | async-start | bytes 5242880 | tf_op jit(solution)/shard_map/all_gather | solution.py:214
  49.6 1.1 copy-start.10
  50.7 9.4 %copy-start.9 = (bf16[4096,128]{1,0:T(8,128)(2,1)S(1)}, bf16[4096,128]{1,0:T(8,128)(2,1)}, u32[]{:S(2)}) copy-start(bf16[4096,128]{1,0:T(8,128)(2,1)} %get-tuple-element.42) | copy-start | bytes 3145732
  52.3 8.1 %collective-permute-start.4 = (bf16[384,128]{1,0:T(8,128)(2,1)S(1)}, bf16[384,128]{1,0:T(8,128)(2,1)S(1)}, u32[]{:S(2)}, u32[]{:S(2)}) collective-permute-start(bf16[384,128]{1,0:T(8,128)(2,1)S(1)} %get-tuple-element.45), channel_id=1, source_target_pairs={{0,192},{64,0},{128,64},{192,128},{1,193},{65,1},{129,65},{193,129... | collective-permute-start | bytes 294920 | tf_op jit(solution)/shard_map/ppermute | solution.py:29
  54.2 9.5 %collective-permute-start.5 = (bf16[384,128]{1,0:T(8,128)(2,1)S(1)}, bf16[384,128]{1,0:T(8,128)(2,1)S(1)}, u32[]{:S(2)}, u32[]{:S(2)}) collective-permute-start(bf16[384,128]{1,0:T(8,128)(2,1)S(1)} %get-tuple-element.47), channel_id=1, source_target_pairs={{0,128},{64,192},{128,0},{192,64},{1,129},{65,193},{129,1},{193,65... | collective-permute-start | bytes 294920 | tf_op jit(solution)/shard_map/ppermute | solution.py:29
  58.2 10.0 %collective-permute-start.6 = (bf16[384,128]{1,0:T(8,128)(2,1)S(1)}, bf16[384,128]{1,0:T(8,128)(2,1)S(1)}, u32[]{:S(2)}, u32[]{:S(2)}) collective-permute-start(bf16[384,128]{1,0:T(8,128)(2,1)S(1)} %get-tuple-element.46), channel_id=1, source_target_pairs={{0,64},{64,128},{128,192},{192,0},{1,65},{65,129},{129,193},{193,1... | collective-permute-start | bytes 294920 | tf_op jit(solution)/shard_map/ppermute | solution.py:29
  60.1 43.3 %copy-start.11 = (s32[384,2]{0,1:T(2,128)S(1)}, s32[384,2]{0,1:T(2,128)}, u32[]{:S(2)}) copy-start(s32[384,2]{0,1:T(2,128)} %param.25) | copy-start | bytes 9220
  60.3 47.3 %copy-start.12 = (f32[64]{0:T(128)S(1)}, f32[64]{0:T(128)}, u32[]{:S(2)}) copy-start(f32[64]{0:T(128)} %param.22) | copy-start | bytes 772
  60.3 58.3 %copy-start.1 = (s32[1536,1]{1,0:T(8,128)S(1)}, s32[1536,1]{1,0:T(8,128)}, u32[]{:S(2)}) copy-start(s32[1536,1]{1,0:T(8,128)} %constant.81.clone.rows) | copy-start | bytes 18436
  60.3 58.2 %copy-start.6 = (bf16[384,64]{0,1:T(8,128)(2,1)S(1)}, bf16[384,64]{0,1:T(8,128)(2,1)}, u32[]{:S(2)}) copy-start(bf16[384,64]{0,1:T(8,128)(2,1)} %param.16) | copy-start | bytes 147460
  68.3 73.7 %collective-permute-start.7 = (bf16[8192,128]{1,0:T(8,128)(2,1)S(1)}, bf16[8192,128]{1,0:T(8,128)(2,1)}, u32[]{:S(2)}, u32[]{:S(2)}) collective-permute-start(bf16[8192,128]{1,0:T(8,128)(2,1)S(1)} %pad_maximum_fusion.own), channel_id=1, source_target_pairs={{0,64},{64,128},{128,192},{192,0},{1,65},{65,129},{129,193},{193,1... | collective-permute-start | bytes 6291464 | tf_op jit(solution)/shard_map/ppermute | solution.py:29
  70.2 71.7 %collective-permute-start.8 = (bf16[8192,128]{1,0:T(8,128)(2,1)S(1)}, bf16[8192,128]{1,0:T(8,128)(2,1)}, u32[]{:S(2)}, u32[]{:S(2)}) collective-permute-start(bf16[8192,128]{1,0:T(8,128)(2,1)S(1)} %pad_maximum_fusion.own), channel_id=1, source_target_pairs={{0,192},{64,0},{128,64},{192,128},{1,193},{65,1},{129,65},{193,129... | collective-permute-start | bytes 6291464 | tf_op jit(solution)/shard_map/ppermute | solution.py:29
  96.6 22.0 %all-to-all-start.1 = ((bf16[8,64,384]{2,1,0:T(8,128)(2,1)}), bf16[8,64,384]{2,1,0:T(8,128)(2,1)S(1)}, u32[]{:S(2)}, u32[]{:S(2)}) async-start(bf16[8,64,384]{2,1,0:T(8,128)(2,1)} %bitcast.39), calls=%async_computation.1 | async-start | bytes 786432 | tf_op jit(solution)/shard_map/all_to_all | solution.py:242
  105.3 75.8 %copy-start.7 = (f32[4096]{0:T(1024)S(1)}, f32[4096]{0:T(1024)}, u32[]{:S(2)}) copy-start(f32[4096]{0:T(1024)} %param.24) | copy-start | bytes 49156
  119.8 1.0 copy-start.5
  141.9 38.2 %all-to-all-start.2 = ((bf16[128,18,128]{2,1,0:T(8,128)(2,1)}), bf16[128,18,128]{2,1,0:T(8,128)(2,1)S(1)}, u32[]{:S(2)}, u32[]{:S(2)}) async-start(bf16[128,18,128]{2,1,0:T(8,128)(2,1)} %copy-done.5), calls=%async_computation.2 | async-start | bytes 1572864 | tf_op jit(solution)/shard_map/all_to_all | solution.py:256
  157.2 26.0 %collective-permute-start.10 = (bf16[4096,128]{1,0:T(8,128)(2,1)}, bf16[4096,128]{1,0:T(8,128)(2,1)}, u32[]{:S(2)}, u32[]{:S(2)}) collective-permute-start(bf16[4096,128]{1,0:T(8,128)(2,1)} %slice.75), channel_id=1, source_target_pairs={{0,192},{64,0},{128,64},{192,128},{1,193},{65,1},{129,65},{193,129... | collective-permute-start | bytes 3145736 | tf_op jit(solution)/shard_map/ppermute | solution.py:29
  162.0 26.9 %collective-permute-start.9 = (bf16[4096,128]{1,0:T(8,128)(2,1)}, bf16[4096,128]{1,0:T(8,128)(2,1)}, u32[]{:S(2)}, u32[]{:S(2)}) collective-permute-start(bf16[4096,128]{1,0:T(8,128)(2,1)} %slice.74), channel_id=1, source_target_pairs={{0,64},{64,128},{128,192},{192,0},{1,65},{65,129},{129,193},{193,1... | collective-permute-start | bytes 3145736 | tf_op jit(solution)/shard_map/ppermute | solution.py:29
  180.1 1.0 copy-start.3
  181.1 1.1 copy-start.4
  188.8 2.2 copy-start
  191.0 46.8 %copy-start.2 = (s32[1536,1]{1,0:T(8,128)S(1)}, s32[1536,1]{1,0:T(8,128)}, u32[]{:S(2)}) copy-start(s32[1536,1]{1,0:T(8,128)} %constant.81.clone.rows) | copy-start | bytes 18436
  191.0 46.8 %copy-start.8 = (s32[384,2]{0,1:T(2,128)S(1)}, s32[384,2]{0,1:T(2,128)}, u32[]{:S(2)}) copy-start(s32[384,2]{0,1:T(2,128)} %param.26) | copy-start | bytes 9220
Sparse Core Ops, SparseCore 0:
  44.6 76.0 all-gather.1

commit v7 on v6

--- a/solution.py
+++ b/solution.py
@@ -31,6 +31,11 @@
 
 def tie(*values):
     return lax.optimization_barrier(values)
+
+
+def spread(v, axis):
+    n = lax.axis_size(axis)
+    return lax.all_to_all(jnp.broadcast_to(v[None], (n,) + v.shape), axis, 0, 0, tiled=True)
 
 
 def slots_of(expert_ids, capacity, experts):
@@ -94,22 +99,21 @@
     normed[...] = (rows * lax.rsqrt(mean_square + NORM_EPSILON) * gain[...]).astype(bf16)
 
 
-def expert_kernel(experts, half, padded, place, normed, own, left_in, right_in, far_gate, far_up, downs, out, wide):
+def expert_kernel(
+    experts, half, padded, place, normed, gates, own_up, left_up, right_up, far_low, far_high, downs, out, wide
+):
     nx = downs.shape[0]
-    inner = normed.shape[1]
     rows = normed[...]
-    for k, (gates, ups) in enumerate(
-        (
-            (own.at[:inner], own.at[inner:]),
-            (left_in.at[:inner], left_in.at[inner:]),
-            (right_in.at[:inner], right_in.at[inner:]),
-            (far_gate, far_up),
-        )
-    ):
-        gate = jnp.dot(rows, gates[...], preferred_element_type=f32)
-        up = jnp.dot(rows, ups[...], preferred_element_type=f32)
+    cut = far_low.shape[0]
+    for k, ups in enumerate(((own_up,), (left_up,), (right_up,), (far_low, far_high))):
+        origin = (place[0] + (0, nx - 1, 1, 2)[k]) % nx
+        gate = jnp.dot(rows, gates[origin], preferred_element_type=f32)
+        if len(ups) == 1:
+            up = jnp.dot(rows, ups[0][...], preferred_element_type=f32)
+        else:
+            up = jnp.dot(rows[:, :cut], ups[0][...], preferred_element_type=f32)
+            up = up + jnp.dot(rows[:, cut:], ups[1][...], preferred_element_type=f32)
         act = (gate / (1.0 + jnp.exp(-gate)) * up).astype(bf16)
-        origin = (place[0] + (0, nx - 1, 1, 2)[k]) % nx
         product = jnp.dot(act, downs[origin], preferred_element_type=f32)
         wide[...] = product if k == 0 else wide[...] + product
     lanes = out.shape[2]
@@ -210,11 +214,13 @@
     )
     packed, own = tie(jnp.concatenate([queries, slot_rows]), own)
     other = swap(own, "yh")
-    gathered = jnp.stack([packed] + [shift(packed, "x", k) for k in range(1, nx)])
     down_all = lax.all_gather(w_down[0], "x")
+    gathered = spread(packed, "x")
     gathered, wide_in = tie(gathered, w_in[0])
-    own_in = jnp.concatenate([wide_in[:, 0], wide_in[:, 1]], axis=0)
-    turned = out_weight.T.reshape(feats, nz, near * head).transpose(1, 0, 2)
+    turned = out_weight.T
+    own_up = wide_in[:, 1]
+    gate_all = lax.all_gather(wide_in[:, 0], "x")
+    turned = turned.reshape(feats, nz, near * head).transpose(1, 0, 2)
     near_weight = lax.all_to_all(turned, "z", 0, 0, tiled=True).reshape(nz * feats, near * head)
     all_queries = gathered[:, :tokens].reshape(nx * tokens, head)
     all_slots = gathered[:, tokens : tokens + tokens // head].reshape(nx * tokens).astype(jnp.int32)
@@ -230,15 +236,17 @@
     values = jnp.concatenate([own[half:], other[half:]], axis=0)
     mixed = attention(all_queries, keys, values, local_frame, frame_rows)
     back = mixed.reshape(nx, tokens, head)
-    attended = sum(
-        (shift(back[k], "x", -k) if k else back[k]).astype(f32) for k in range(nx)
-    ).astype(bf16)
-    attended, own_in = tie(attended, own_in)
-    left_in, right_in = shift(own_in, "x", 1), shift(own_in, "x", -1)
+    attended = lax.dynamic_index_in_dim(back, x, 0, keepdims=False).astype(f32)
+    for k in range(1, nx):
+        piece = lax.dynamic_index_in_dim(back, (x + k) % nx, 0, keepdims=False)
+        attended = attended + shift(piece, "x", k).astype(f32)
+    attended, own_up = tie(attended.astype(bf16), own_up)
+    left_up, right_up = shift(own_up, "x", 1), shift(own_up, "x", -1)
     heads = lax.all_gather(attended, NEAR, axis=1, tiled=True)
     partial = lax.dot_general(
         near_weight, heads, (((1,), (1,)), ((), ())), preferred_element_type=f32
     ).astype(bf16)
+    partial, down_all = tie(partial, down_all)
     parts = lax.all_to_all(partial.reshape(nz, feats, tokens), "z", 0, 0, tiled=True)
     capacity = 6 * tokens // experts
     half, padded = capacity // 2, -(-(capacity // 2) // 8) * 8
@@ -250,9 +258,9 @@
         jax.ShapeDtypeStruct((feats, tokens), bf16),
         jax.ShapeDtypeStruct((nh * experts, half, lanes), bf16),
     )(parts, hidden_in.T, attn_gate[:, None], slots, table)
-    sent, left_in, right_in = tie(sent, left_in, right_in)
-    width = w_in.shape[1]
-    far_gate, far_up = shift(left_in[:width], "x", 1), shift(right_in[width:], "x", -1)
+    sent, left_up, right_up = tie(sent, left_up, right_up)
+    cut = w_in.shape[1] // 2
+    far_low, far_high = shift(left_up[:cut], "x", 1), shift(right_up[cut:], "x", -1)
     came = lax.all_to_all(sent, BOTH, 0, 0, tiled=True)
     rows = 2 * nh * padded
     (normed,) = local_kernel(
@@ -264,12 +272,12 @@
     in_vmem = pl.BlockSpec(memory_space=pltpu.VMEM)
     dealt = pl.pallas_call(
         functools.partial(expert_kernel, experts, half, padded),
-        in_specs=[pl.BlockSpec(memory_space=pltpu.SMEM)] + [in_vmem] * 7,
+        in_specs=[pl.BlockSpec(memory_space=pltpu.SMEM)] + [in_vmem] * 8,
         out_specs=in_vmem,
         out_shape=jax.ShapeDtypeStruct(came.shape, bf16),
         scratch_shapes=[pltpu.VMEM((rows, experts * feats), f32)],
         compiler_params=pltpu.CompilerParams(vmem_limit_bytes=40 * 1024 * 1024),
-    )(x[None], normed, own_in, left_in, right_in, far_gate, far_up, down_all)
+    )(x[None], normed, gate_all, own_up, left_up, right_up, far_low, far_high, down_all)
     back_sums = lax.all_to_all(dealt, BOTH, 0, 0, tiled=True)
     (out,) = local_kernel(
         functools.partial(combine_kernel, experts, half, padded),

time: 248 us -> 214 us (0.86)
  waiting for transfers between devices: 62 us -> 42.8 us
  starting transfers between devices: 68.3 us -> 59.9 us
  blocking collectives: 59.3 us -> 54.8 us
  local copies, waits for them, and re-layouts: 24.1 us -> 20.7 us
    ppermute x10 -> x7, waiting for transfers between devices: 35.2 us -> 8.46 us  [shift(): return lax.ppermute(v, axis, [(i, (i + by) % n) for i in range(n)])]
    ppermute x10 -> x7, starting transfers between devices: 31 us -> 20.8 us  [shift(): return lax.ppermute(v, axis, [(i, (i + by) % n) for i in range(n)])]
    all_to_all x1, blocking collectives: 40.6 us -> 35.4 us  [per_device(): back_sums = lax.all_to_all(dealt, BOTH, 0, 0, tiled=True)]
    all_to_all x0 -> x1, starting transfers between devices: none -> 4.84 us  [spread(): lax.all_to_all(jnp.broadcast_to(v[None], (n,) + v.shape), axis, 0, 0, til...]
    all_to_all x0 -> x1, waiting for transfers between devices: none -> 4.45 us  [spread(): lax.all_to_all(jnp.broadcast_to(v[None], (n,) + v.shape), axis, 0, 0, til...]
    all_to_all x1, starting transfers between devices: 13 us -> 8.9 us  [per_device(): came = lax.all_to_all(sent, BOTH, 0, 0, tiled=True)]
    all_to_all x1, waiting for transfers between devices: 10.8 us -> 14.1 us  [per_device(): lax.all_to_all(partial.reshape(nz, feats, tokens), 'z', 0, 0, tiled=True)]
    unnamed x29 -> x19, local copies, waits for them, and re-layouts: 9.8 us -> 8.31 us
  transfers between devices with their start and end apart: 15 -> 14, of which waited for: 7 -> 6; matrix products, arithmetic and copies ran while one was open for 10% -> 13% of each run, Pallas kernels for 1% -> 1%
where the time goes in v7:
time: 214 us; the launch traced here: 212 us
  starting transfers between devices  59.9 us (28%)
  blocking collectives  54.8 us (26%)
  waiting for transfers between devices  42.8 us (20%)
  local copies, waits for them, and re-layouts  20.7 us (10%)
  between operations  13.7 us (6%)
  Pallas kernels  9.63 us (5%)
  matrix products  5.81 us (3%)
  other arithmetic  4.52 us (2%)
    all_to_all x1, blocking collectives, per_device(): back_sums = lax.all_to_all(dealt, BOTH, 0, 0, tiled=True)  35.4 us
    ppermute x7, starting transfers between devices, shift(): return lax.ppermute(v, axis, [(i, (i + by) % n) for i in range(n)])  20.8 us
    all_gather x1, blocking collectives, per_device(): heads = lax.all_gather(attended, NEAR, axis=1, tiled=True)  19.4 us
    all_to_all x1, waiting for transfers between devices, per_device(): came = lax.all_to_all(sent, BOTH, 0, 0, tiled=True)  15 us
    all_to_all x1, waiting for transfers between devices, per_device(): lax.all_to_all(partial.reshape(nz, feats, tokens), 'z', 0, 0, tiled=True)  14.1 us
    all_to_all x1, starting transfers between devices, per_device(): lax.all_to_all(turned, 'z', 0, 0, tiled=True)  9.95 us
    all_to_all x1, starting transfers between devices, per_device(): came = lax.all_to_all(sent, BOTH, 0, 0, tiled=True)  8.9 us
    ppermute x7, waiting for transfers between devices, shift(): return lax.ppermute(v, axis, [(i, (i + by) % n) for i in range(n)])  8.46 us
  transfers between devices with their start and end apart: 14, of which 6 were waited for; matrix products, arithmetic and copies ran while one was open for 13% of the time, Pallas kernels for 1%

profile of v7, /device:TPU:1, one launch (start us, length us, event | category | flops | bytes accessed | tf_op | source)
XLA Modules:
  0.0 211.8 jit_solution(2426845259462676823)
XLA Ops:
  6.5 0.7 all-gather.4.cloned.1.call-update
  7.3 1.0 constant_dynamic-slice_fusion
  8.4 0.8 select_reduce_fusion
  9.2 0.9 fusion.19
  10.1 0.8 pad_maximum_fusion
  10.9 0.8 broadcast_in_dim.61
  11.7 4.8 %all-to-all-start = ((bf16[4,400,128]{2,1,0:T(8,128)(2,1)}), bf16[4,400,128]{2,1,0:T(8,128)(2,1)S(1)}, u32[]{:S(2)}, u32[]{:S(2)}) async-start(bf16[4,400,128]{2,1,0:T(8,128)(2,1)} %broadcast_in_dim.61), calls=%async_computation | async-start | bytes 819200 | tf_op jit(solution)/shard_map/all_to_all | solution.py:38
  16.5 1.9 copy.43
  18.4 4.5 %all-to-all-done = bf16[4,400,128]{2,1,0:T(8,128)(2,1)S(1)} async-done(((bf16[4,400,128]{2,1,0:T(8,128)(2,1)}), bf16[4,400,128]{2,1,0:T(8,128)(2,1)S(1)}, u32[]{:S(2)}, u32[]{:S(2)}) %all-to-all-start) | async-done | bytes 409632 | tf_op jit(solution)/shard_map/all_to_all | solution.py:38
  22.8 1.2 fusion.31
  24.1 8.2 %collective-permute-start = (bf16[1206,128]{1,0:T(8,128)(2,1)}, bf16[1206,128]{1,0:T(8,128)(2,1)S(1)}, u32[]{:S(2)}, u32[]{:S(2)}) collective-permute-start(bf16[1206,128]{1,0:T(8,128)(2,1)} %pad_maximum_fusion), channel_id=1, source_target_pairs={{0,256},{256,0},{1,257},{257,1},{2,258},{258,2},{3,259},{259,3},{4... | collective-permute-start | bytes 926216 | tf_op jit(solution)/shard_map/ppermute | solution.py:24
  32.2 1.9 copy.41
  34.2 1.6 copy.36
  35.7 9.9 %all-to-all-start.1 = ((bf16[8,64,1024]{2,1,0:T(8,128)(2,1)}), bf16[8,64,1024]{2,1,0:T(8,128)(2,1)S(1)}, u32[]{:S(2)}, u32[]{:S(2)}) async-start(bf16[8,64,1024]{2,1,0:T(8,128)(2,1)} %copy.36), calls=%async_computation.1 | async-start | bytes 2097152 | tf_op jit(solution)/shard_map/all_to_all | solution.py:224
  45.7 1.7 fusion.32
  47.5 2.2 %fusion.34 = (f32[1536]{0:T(1024)S(1)}, f32[1536,1206]{0,1:T(8,128)S(1)}) fusion(bf16[1536,128]{1,0:T(8,128)(2,1)S(1)} %bitcast.47, bf16[603,128]{1,0:T(8,128)(2,1)S(1)} %get-tuple-element.55, bf16[603,128]{1,0:T(8,128)(2,1)} %get-tuple-element.53, s32[1536]{0:T(1024)S(1)} %get-tuple-element.44, s32[1206]{0:T(1024)S(1)} %add_select_fusion), kind=kOutput, calls=%fused_computation.62 | convolution fusion | flops 482244096 | bytes 8128728 | tf_op jit(solution)/shard_map/dot_general | solution.py:168
  49.7 1.1 fusion.1
  50.8 1.5 fusion.4
  52.4 0.7 dynamic-slice_bitcast_fusion.2
  53.1 2.8 %collective-permute-start.3 = (bf16[384,128]{1,0:T(8,128)(2,1)}, bf16[384,128]{1,0:T(8,128)(2,1)S(1)}, u32[]{:S(2)}, u32[]{:S(2)}) collective-permute-start(bf16[384,128]{1,0:T(8,128)(2,1)} %get-tuple-element.50), channel_id=1, source_target_pairs={{0,192},{64,0},{128,64},{192,128},{1,193},{65,1},{129,65},{193,129... | collective-permute-start | bytes 294920 | tf_op jit(solution)/shard_map/ppermute | solution.py:29
  55.9 3.1 %collective-permute-start.2 = (bf16[384,128]{1,0:T(8,128)(2,1)}, bf16[384,128]{1,0:T(8,128)(2,1)S(1)}, u32[]{:S(2)}, u32[]{:S(2)}) collective-permute-start(bf16[384,128]{1,0:T(8,128)(2,1)} %get-tuple-element.51), channel_id=1, source_target_pairs={{0,128},{64,192},{128,0},{192,64},{1,129},{65,193},{129,1},{193,65... | collective-permute-start | bytes 294920 | tf_op jit(solution)/shard_map/ppermute | solution.py:29
  59.0 1.9 collective-permute-start.1
  60.9 0.2 collective-permute-done.3
  61.1 4.2 %collective-permute-done.2 = bf16[384,128]{1,0:T(8,128)(2,1)S(1)} collective-permute-done((bf16[384,128]{1,0:T(8,128)(2,1)}, bf16[384,128]{1,0:T(8,128)(2,1)S(1)}, u32[]{:S(2)}, u32[]{:S(2)}) %collective-permute-start.2) | collective-permute-done | bytes 98336 | tf_op jit(solution)/shard_map/ppermute | solution.py:29
  65.3 4.0 %collective-permute-done.1 = bf16[384,128]{1,0:T(8,128)(2,1)} collective-permute-done((bf16[384,128]{1,0:T(8,128)(2,1)}, bf16[384,128]{1,0:T(8,128)(2,1)}, u32[]{:S(2)}, u32[]{:S(2)}) %collective-permute-start.1) | collective-permute-done | bytes 98336 | tf_op jit(solution)/shard_map/ppermute | solution.py:29
  69.4 0.9 fusion.18
  70.3 1.9 collective-permute-start.4
  72.3 4.6 %collective-permute-start.5 = (bf16[4096,128]{1,0:T(8,128)(2,1)S(1)}, bf16[4096,128]{1,0:T(8,128)(2,1)}, u32[]{:S(2)}, u32[]{:S(2)}) collective-permute-start(bf16[4096,128]{1,0:T(8,128)(2,1)S(1)} %get-tuple-element.37.own_up), channel_id=1, source_target_pairs={{0,192},{64,0},{128,64},{192,128},{1,193},{65,1},{129,65},{193,129... | collective-permute-start | bytes 3145736 | tf_op jit(solution)/shard_map/ppermute | solution.py:29
  76.8 19.4 %all_gather.9 = bf16[384,1024]{1,0:T(8,128)(2,1)} all-gather(bf16[384,128]{1,0:T(8,128)(2,1)S(1)} %fusion.18), channel_id=1, replica_groups=mesh['yh'=2,'x'=4,'z'=8,'yl'=4,'core'=2] {'yl','core'}, dimensions={1}, use_global_device_ids=true | all-gather | bytes 884736 | tf_op jit(solution)/shard_map/all_gather | solution.py:245
  96.2 1.7 fusion.6
  98.0 0.9 copy.37
  98.9 7.3 %all-to-all-start.2 = ((bf16[8,64,384]{2,1,0:T(8,128)(2,1)}), bf16[8,64,384]{2,1,0:T(8,128)(2,1)S(1)}, u32[]{:S(2)}, u32[]{:S(2)}) async-start(bf16[8,64,384]{2,1,0:T(8,128)(2,1)} %bitcast.14), calls=%async_computation.2 | async-start | bytes 786432 | tf_op jit(solution)/shard_map/all_to_all | solution.py:250
  106.6 0.4 fusion.8
  107.0 0.2 convert_element_type.70
  107.3 14.1 %all-to-all-done.2.parts = bf16[8,64,384]{2,1,0:T(8,128)(2,1)S(1)} async-done(((bf16[8,64,384]{2,1,0:T(8,128)(2,1)}), bf16[8,64,384]{2,1,0:T(8,128)(2,1)S(1)}, u32[]{:S(2)}, u32[]{:S(2)}) %all-to-all-start.2) | async-done | bytes 393248 | tf_op jit(solution)/shard_map/all_to_all | solution.py:250
  121.4 2.1 shard_map.136
  123.5 8.9 %all-to-all-start.3 = ((bf16[128,18,128]{2,1,0:T(8,128)(2,1)}), bf16[128,18,128]{2,1,0:T(8,128)(2,1)S(1)}, u32[]{:S(2)}, u32[]{:S(2)}) async-start(bf16[128,18,128]{2,1,0:T(8,128)(2,1)} %get-tuple-element.38), calls=%async_computation.3 | async-start | bytes 1572864 | tf_op jit(solution)/shard_map/all_to_all | solution.py:264
  132.4 1.9 slice.54
  134.3 1.9 collective-permute-start.6
  136.2 1.9 slice.55
  138.1 4.6 %collective-permute-start.7 = (bf16[2048,128]{1,0:T(8,128)(2,1)}, bf16[2048,128]{1,0:T(8,128)(2,1)}, u32[]{:S(2)}, u32[]{:S(2)}) collective-permute-start(bf16[2048,128]{1,0:T(8,128)(2,1)} %slice.55), channel_id=1, source_target_pairs={{0,192},{64,0},{128,64},{192,128},{1,193},{65,1},{129,65},{193,129... | collective-permute-start | bytes 1572872 | tf_op jit(solution)/shard_map/ppermute | solution.py:29
  142.6 15.0 %all-to-all-done.3.came = bf16[128,18,128]{2,1,0:T(8,128)(2,1)S(1)} async-done(((bf16[128,18,128]{2,1,0:T(8,128)(2,1)}), bf16[128,18,128]{2,1,0:T(8,128)(2,1)S(1)}, u32[]{:S(2)}, u32[]{:S(2)}) %all-to-all-start.3) | async-done | bytes 589856 | tf_op jit(solution)/shard_map/all_to_all | solution.py:264
  157.6 0.6 shard_map.137.normed
  158.3 2.2 %copy-done = bf16[4,128,4096]{2,1,0:T(8,128)(2,1)S(1)} copy-done((bf16[4,128,4096]{2,1,0:T(8,128)(2,1)S(1)}, bf16[4,128,4096]{2,1,0:T(8,128)(2,1)}, u32[]{:S(2)}) %copy-start) | copy-done | bytes 4194328
  160.4 2.2 %copy-done.1 = bf16[16384,1,128]{2,0,1:T(8,128)(2,1)S(1)} copy-done((bf16[16384,1,128]{2,0,1:T(8,128)(2,1)S(1)}, bf16[16384,1,128]{2,0,1:T(8,128)(2,1)}, u32[]{:S(2)}) %copy-start.1) | copy-done | bytes 4194328
  162.6 5.1 %shard_map.138 = bf16[128,18,128]{2,1,0:T(8,128)(2,1)S(1)} custom-call(s32[1]{0:T(128)} %bitcast.place, bf16[96,4096]{1,0:T(8,128)(2,1)S(1)} %shard_map.137.normed, bf16[4,4096,128]{2,1,0:T(8,128)(2,1)S(1)} %bitcast.39, bf16[4096,128]{1,0:T(8,128)(2,1)S(1)} %get-tuple-element.37.own_up, bf16[4096,128]{1,0:T(8,128)(2,1)} %collective-permute-done.4.left_up, ...), custom_call_target="tpu_custom_call" | custom-call | tf_op jit(solution)/shard_map/pallas_call | solution.py:273
  167.8 35.4 %all_to_all.25.back = bf16[128,18,128]{2,1,0:T(8,128)(2,1)S(1)} all-to-all(bf16[128,18,128]{2,1,0:T(8,128)(2,1)S(1)} %shard_map.138), channel_id=1, replica_groups=mesh['yh'=2,'x'=4,'z'=8,'yl'=4,'core'=2] {'yh','z','yl','core'}, dimensions={0} | all-to-all | bytes 1179648 | tf_op jit(solution)/shard_map/all_to_all | solution.py:281
  203.1 1.8 shard_map.139
  (41 shorter events, 0.8 us)
Async XLA Ops:
  6.5 91.5 %all-gather.4.cloned.1.call-start = ((), (), s32[]{:S(2)}) async-start(), calls=%async_computation.5 | async-start | bytes 5242880 | tf_op jit(solution)/shard_map/all_gather | solution.py:217
  11.7 11.2 %all-to-all-start = ((bf16[4,400,128]{2,1,0:T(8,128)(2,1)}), bf16[4,400,128]{2,1,0:T(8,128)(2,1)S(1)}, u32[]{:S(2)}, u32[]{:S(2)}) async-start(bf16[4,400,128]{2,1,0:T(8,128)(2,1)} %broadcast_in_dim.61), calls=%async_computation | async-start | bytes 819200 | tf_op jit(solution)/shard_map/all_to_all | solution.py:38
  16.5 141.7 %all-gather.6.cloned.1.call-start = ((), (), s32[]{:S(2)}) async-start(), calls=%async_computation.6 | async-start | bytes 5242880 | tf_op jit(solution)/shard_map/all_gather | solution.py:222
  24.1 23.4 %collective-permute-start = (bf16[1206,128]{1,0:T(8,128)(2,1)}, bf16[1206,128]{1,0:T(8,128)(2,1)S(1)}, u32[]{:S(2)}, u32[]{:S(2)}) collective-permute-start(bf16[1206,128]{1,0:T(8,128)(2,1)} %pad_maximum_fusion), channel_id=1, source_target_pairs={{0,256},{256,0},{1,257},{257,1},{2,258},{258,2},{3,259},{259,3},{4... | collective-permute-start | bytes 926216 | tf_op jit(solution)/shard_map/ppermute | solution.py:24
  35.7 60.5 %all-to-all-start.1 = ((bf16[8,64,1024]{2,1,0:T(8,128)(2,1)}), bf16[8,64,1024]{2,1,0:T(8,128)(2,1)S(1)}, u32[]{:S(2)}, u32[]{:S(2)}) async-start(bf16[8,64,1024]{2,1,0:T(8,128)(2,1)} %copy.36), calls=%async_computation.1 | async-start | bytes 2097152 | tf_op jit(solution)/shard_map/all_to_all | solution.py:224
  50.8 55.5 %copy-start.7 = (f32[64]{0:T(128)S(1)}, f32[64]{0:T(128)}, u32[]{:S(2)}) copy-start(f32[64]{0:T(128)} %param.22) | copy-start | bytes 772
  50.8 55.6 %copy-start.6 = (s32[384,2]{0,1:T(2,128)S(1)}, s32[384,2]{0,1:T(2,128)}, u32[]{:S(2)}) copy-start(s32[384,2]{0,1:T(2,128)} %param.25) | copy-start | bytes 9220
  52.3 69.1 %copy-start.2 = (s32[1536,1]{1,0:T(8,128)S(1)}, s32[1536,1]{1,0:T(8,128)}, u32[]{:S(2)}) copy-start(s32[1536,1]{1,0:T(8,128)} %constant.110.clone.rows) | copy-start | bytes 18436
  52.3 69.1 %copy-start.3 = (bf16[384,64]{0,1:T(8,128)(2,1)S(1)}, bf16[384,64]{0,1:T(8,128)(2,1)}, u32[]{:S(2)}) copy-start(bf16[384,64]{0,1:T(8,128)(2,1)} %param.16) | copy-start | bytes 147460
  52.3 105.3 %copy-start.4 = (f32[4096]{0:T(1024)S(1)}, f32[4096]{0:T(1024)}, u32[]{:S(2)}) copy-start(f32[4096]{0:T(1024)} %param.24) | copy-start | bytes 49156
  53.1 8.0 %collective-permute-start.3 = (bf16[384,128]{1,0:T(8,128)(2,1)}, bf16[384,128]{1,0:T(8,128)(2,1)S(1)}, u32[]{:S(2)}, u32[]{:S(2)}) collective-permute-start(bf16[384,128]{1,0:T(8,128)(2,1)} %get-tuple-element.50), channel_id=1, source_target_pairs={{0,192},{64,0},{128,64},{192,128},{1,193},{65,1},{129,65},{193,129... | collective-permute-start | bytes 294920 | tf_op jit(solution)/shard_map/ppermute | solution.py:29
  55.9 9.4 %collective-permute-start.2 = (bf16[384,128]{1,0:T(8,128)(2,1)}, bf16[384,128]{1,0:T(8,128)(2,1)S(1)}, u32[]{:S(2)}, u32[]{:S(2)}) collective-permute-start(bf16[384,128]{1,0:T(8,128)(2,1)} %get-tuple-element.51), channel_id=1, source_target_pairs={{0,128},{64,192},{128,0},{192,64},{1,129},{65,193},{129,1},{193,65... | collective-permute-start | bytes 294920 | tf_op jit(solution)/shard_map/ppermute | solution.py:29
  59.0 10.4 %collective-permute-start.1 = (bf16[384,128]{1,0:T(8,128)(2,1)}, bf16[384,128]{1,0:T(8,128)(2,1)}, u32[]{:S(2)}, u32[]{:S(2)}) collective-permute-start(bf16[384,128]{1,0:T(8,128)(2,1)} %get-tuple-element.49), channel_id=1, source_target_pairs={{0,64},{64,128},{128,192},{192,0},{1,65},{65,129},{129,193},{193,1... | collective-permute-start | bytes 294920 | tf_op jit(solution)/shard_map/ppermute | solution.py:29
  70.3 53.2 %collective-permute-start.4 = (bf16[4096,128]{1,0:T(8,128)(2,1)S(1)}, bf16[4096,128]{1,0:T(8,128)(2,1)}, u32[]{:S(2)}, u32[]{:S(2)}) collective-permute-start(bf16[4096,128]{1,0:T(8,128)(2,1)S(1)} %get-tuple-element.37.own_up), channel_id=1, source_target_pairs={{0,64},{64,128},{128,192},{192,0},{1,65},{65,129},{129,193},{193,1... | collective-permute-start | bytes 3145736 | tf_op jit(solution)/shard_map/ppermute | solution.py:29
  72.3 51.2 %collective-permute-start.5 = (bf16[4096,128]{1,0:T(8,128)(2,1)S(1)}, bf16[4096,128]{1,0:T(8,128)(2,1)}, u32[]{:S(2)}, u32[]{:S(2)}) collective-permute-start(bf16[4096,128]{1,0:T(8,128)(2,1)S(1)} %get-tuple-element.37.own_up), channel_id=1, source_target_pairs={{0,192},{64,0},{128,64},{192,128},{1,193},{65,1},{129,65},{193,129... | collective-permute-start | bytes 3145736 | tf_op jit(solution)/shard_map/ppermute | solution.py:29
  98.9 22.4 %all-to-all-start.2 = ((bf16[8,64,384]{2,1,0:T(8,128)(2,1)}), bf16[8,64,384]{2,1,0:T(8,128)(2,1)S(1)}, u32[]{:S(2)}, u32[]{:S(2)}) async-start(bf16[8,64,384]{2,1,0:T(8,128)(2,1)} %bitcast.14), calls=%async_computation.2 | async-start | bytes 786432 | tf_op jit(solution)/shard_map/all_to_all | solution.py:250
  123.5 34.1 %all-to-all-start.3 = ((bf16[128,18,128]{2,1,0:T(8,128)(2,1)}), bf16[128,18,128]{2,1,0:T(8,128)(2,1)S(1)}, u32[]{:S(2)}, u32[]{:S(2)}) async-start(bf16[128,18,128]{2,1,0:T(8,128)(2,1)} %get-tuple-element.38), calls=%async_computation.3 | async-start | bytes 1572864 | tf_op jit(solution)/shard_map/all_to_all | solution.py:264
  134.3 23.9 %collective-permute-start.6 = (bf16[2048,128]{1,0:T(8,128)(2,1)}, bf16[2048,128]{1,0:T(8,128)(2,1)}, u32[]{:S(2)}, u32[]{:S(2)}) collective-permute-start(bf16[2048,128]{1,0:T(8,128)(2,1)} %slice.54), channel_id=1, source_target_pairs={{0,64},{64,128},{128,192},{192,0},{1,65},{65,129},{129,193},{193,1... | collective-permute-start | bytes 1572872 | tf_op jit(solution)/shard_map/ppermute | solution.py:29
  138.1 20.2 %collective-permute-start.7 = (bf16[2048,128]{1,0:T(8,128)(2,1)}, bf16[2048,128]{1,0:T(8,128)(2,1)}, u32[]{:S(2)}, u32[]{:S(2)}) collective-permute-start(bf16[2048,128]{1,0:T(8,128)(2,1)} %slice.55), channel_id=1, source_target_pairs={{0,192},{64,0},{128,64},{192,128},{1,193},{65,1},{129,65},{193,129... | collective-permute-start | bytes 1572872 | tf_op jit(solution)/shard_map/ppermute | solution.py:29
  158.2 2.2 %copy-start = (bf16[4,128,4096]{2,1,0:T(8,128)(2,1)S(1)}, bf16[4,128,4096]{2,1,0:T(8,128)(2,1)}, u32[]{:S(2)}) copy-start(bf16[4,128,4096]{2,1,0:T(8,128)(2,1)} %all-gather.4.cloned.1.call-done.downs) | copy-start | bytes 12582916
  160.4 2.2 %copy-start.1 = (bf16[16384,1,128]{2,0,1:T(8,128)(2,1)S(1)}, bf16[16384,1,128]{2,0,1:T(8,128)(2,1)}, u32[]{:S(2)}) copy-start(bf16[16384,1,128]{2,0,1:T(8,128)(2,1)} %all-gather.6.cloned.1.call-done) | copy-start | bytes 12582916
  162.6 40.5 %copy-start.5 = (s32[384,2]{0,1:T(2,128)S(1)}, s32[384,2]{0,1:T(2,128)}, u32[]{:S(2)}) copy-start(s32[384,2]{0,1:T(2,128)} %param.26) | copy-start | bytes 9220
Sparse Core Ops, SparseCore 0:
  9.5 63.2 all-gather.3
  74.9 58.4 all-gather.5

commit v8 on v7

--- a/solution.py
+++ b/solution.py
@@ -100,21 +100,51 @@
 
 
 def expert_kernel(
-    experts, half, padded, place, normed, gates, own_up, left_up, right_up, far_low, far_high, downs, out, wide
+    experts,
+    half,
+    padded,
+    place,
+    normed,
+    own_up,
+    left_up,
+    right_up,
+    far_low,
+    far_high,
+    gates_there,
+    downs_there,
+    out,
+    wide,
+    gates,
+    downs,
+    gate_sems,
+    down_sems,
 ):
     nx = downs.shape[0]
+    origins = [(place[0] + turn) % nx for turn in (0, nx - 1, 1, 2)]
+    gate_copies = [
+        pltpu.make_async_copy(gates_there.at[origin], gates.at[k], gate_sems.at[k])
+        for k, origin in enumerate(origins)
+    ]
+    down_copies = [
+        pltpu.make_async_copy(downs_there.at[origin], downs.at[k], down_sems.at[k])
+        for k, origin in enumerate(origins)
+    ]
+    for gate_copy, down_copy in zip(gate_copies, down_copies):
+        gate_copy.start()
+        down_copy.start()
     rows = normed[...]
     cut = far_low.shape[0]
     for k, ups in enumerate(((own_up,), (left_up,), (right_up,), (far_low, far_high))):
-        origin = (place[0] + (0, nx - 1, 1, 2)[k]) % nx
-        gate = jnp.dot(rows, gates[origin], preferred_element_type=f32)
+        gate_copies[k].wait()
+        gate = jnp.dot(rows, gates[k], preferred_element_type=f32)
         if len(ups) == 1:
             up = jnp.dot(rows, ups[0][...], preferred_element_type=f32)
         else:
             up = jnp.dot(rows[:, :cut], ups[0][...], preferred_element_type=f32)
             up = up + jnp.dot(rows[:, cut:], ups[1][...], preferred_element_type=f32)
         act = (gate / (1.0 + jnp.exp(-gate)) * up).astype(bf16)
-        product = jnp.dot(act, downs[origin], preferred_element_type=f32)
+        down_copies[k].wait()
+        product = jnp.dot(act, downs[k], preferred_element_type=f32)
         wide[...] = product if k == 0 else wide[...] + product
     lanes = out.shape[2]
     left = lax.broadcasted_iota(jnp.int32, (half, lanes), 1) < lanes // 2
@@ -216,7 +246,7 @@
     other = swap(own, "yh")
     down_all = lax.all_gather(w_down[0], "x")
     gathered = spread(packed, "x")
-    gathered, wide_in = tie(gathered, w_in[0])
+    wide_in = w_in[0]
     turned = out_weight.T
     own_up = wide_in[:, 1]
     gate_all = lax.all_gather(wide_in[:, 0], "x")
@@ -236,12 +266,14 @@
     values = jnp.concatenate([own[half:], other[half:]], axis=0)
     mixed = attention(all_queries, keys, values, local_frame, frame_rows)
     back = mixed.reshape(nx, tokens, head)
-    attended = lax.dynamic_index_in_dim(back, x, 0, keepdims=False).astype(f32)
-    for k in range(1, nx):
-        piece = lax.dynamic_index_in_dim(back, (x + k) % nx, 0, keepdims=False)
-        attended = attended + shift(piece, "x", k).astype(f32)
-    attended, own_up = tie(attended.astype(bf16), own_up)
+    pieces = [
+        shift(lax.dynamic_index_in_dim(back, (x + k) % nx, 0, keepdims=False), "x", k) for k in range(1, nx)
+    ]
+    pieces[0], own_up = tie(pieces[0], own_up)
     left_up, right_up = shift(own_up, "x", 1), shift(own_up, "x", -1)
+    attended = sum(
+        piece.astype(f32) for piece in [lax.dynamic_index_in_dim(back, x, 0, keepdims=False)] + pieces
+    ).astype(bf16)
     heads = lax.all_gather(attended, NEAR, axis=1, tiled=True)
     partial = lax.dot_general(
         near_weight, heads, (((1,), (1,)), ((), ())), preferred_element_type=f32
@@ -272,12 +304,18 @@
     in_vmem = pl.BlockSpec(memory_space=pltpu.VMEM)
     dealt = pl.pallas_call(
         functools.partial(expert_kernel, experts, half, padded),
-        in_specs=[pl.BlockSpec(memory_space=pltpu.SMEM)] + [in_vmem] * 8,
+        in_specs=[pl.BlockSpec(memory_space=pltpu.SMEM)] + [in_vmem] * 6 + [pl.BlockSpec(memory_space=pl.ANY)] * 2,
         out_specs=in_vmem,
         out_shape=jax.ShapeDtypeStruct(came.shape, bf16),
-        scratch_shapes=[pltpu.VMEM((rows, experts * feats), f32)],
+        scratch_shapes=[
+            pltpu.VMEM((rows, experts * feats), f32),
+            pltpu.VMEM(gate_all.shape, bf16),
+            pltpu.VMEM(down_all.shape, bf16),
+            pltpu.SemaphoreType.DMA((nx,)),
+            pltpu.SemaphoreType.DMA((nx,)),
+        ],
         compiler_params=pltpu.CompilerParams(vmem_limit_bytes=40 * 1024 * 1024),
-    )(x[None], normed, gate_all, own_up, left_up, right_up, far_low, far_high, down_all)
+    )(x[None], normed, own_up, left_up, right_up, far_low, far_high, gate_all, down_all)
     back_sums = lax.all_to_all(dealt, BOTH, 0, 0, tiled=True)
     (out,) = local_kernel(
         functools.partial(combine_kernel, experts, half, padded),

time: 214 us -> 210 us (0.981)
  waiting for transfers between devices: 42.8 us -> 32.6 us
  starting transfers between devices: 59.9 us -> 64.9 us
  blocking collectives: 54.8 us -> 58.2 us
  other arithmetic: 4.52 us -> 2.33 us
    ppermute x7, waiting for transfers between devices: 8.46 us -> 1.62 us  [shift(): return lax.ppermute(v, axis, [(i, (i + by) % n) for i in range(n)])]
    all_to_all x1, waiting for transfers between devices: 4.45 us -> 0.01 us  [spread(): lax.all_to_all(jnp.broadcast_to(v[None], (n,) + v.shape), axis, 0, 0, til...]
    all_to_all x1, blocking collectives: 35.4 us -> 39.5 us  [per_device(): back_sums = lax.all_to_all(dealt, BOTH, 0, 0, tiled=True)]
    ppermute x7, starting transfers between devices: 20.8 us -> 23.7 us  [shift(): return lax.ppermute(v, axis, [(i, (i + by) % n) for i in range(n)])]
    all_to_all x1, starting transfers between devices: 7.29 us -> 9.95 us  [per_device(): lax.all_to_all(partial.reshape(nz, feats, tokens), 'z', 0, 0, tiled=True)]
    unnamed x19 -> x29, local copies, waits for them, and re-layouts: 8.31 us -> 7.67 us
  transfers between devices with their start and end apart: 14 -> 14, of which waited for: 6 -> 4; matrix products, arithmetic and copies ran while one was open for 13% -> 11% of each run, Pallas kernels for 1% -> 1%
where the time goes in v8:
time: 210 us; the launch traced here: 209 us
  starting transfers between devices  64.9 us (31%)
  blocking collectives  58.2 us (28%)
  waiting for transfers between devices  32.6 us (16%)
  local copies, waits for them, and re-layouts  20 us (10%)
  between operations  13.8 us (7%)
  Pallas kernels  10.9 us (5%)
  matrix products  5.82 us (3%)
  other arithmetic  2.33 us (1%)
    all_to_all x1, blocking collectives, per_device(): back_sums = lax.all_to_all(dealt, BOTH, 0, 0, tiled=True)  39.5 us
    ppermute x7, starting transfers between devices, shift(): return lax.ppermute(v, axis, [(i, (i + by) % n) for i in range(n)])  23.7 us
    all_gather x1, blocking collectives, per_device(): heads = lax.all_gather(attended, NEAR, axis=1, tiled=True)  18.7 us
    all_to_all x1, waiting for transfers between devices, per_device(): came = lax.all_to_all(sent, BOTH, 0, 0, tiled=True)  15 us
    all_to_all x1, waiting for transfers between devices, per_device(): lax.all_to_all(partial.reshape(nz, feats, tokens), 'z', 0, 0, tiled=True)  14.1 us
    all_to_all x1, starting transfers between devices, per_device(): lax.all_to_all(turned, 'z', 0, 0, tiled=True)  10 us
    all_to_all x1, starting transfers between devices, per_device(): lax.all_to_all(partial.reshape(nz, feats, tokens), 'z', 0, 0, tiled=True)  9.95 us
    all_to_all x1, starting transfers between devices, per_device(): came = lax.all_to_all(sent, BOTH, 0, 0, tiled=True)  8.86 us
  transfers between devices with their start and end apart: 14, of which 4 were waited for; matrix products, arithmetic and copies ran while one was open for 11% of the time, Pallas kernels for 1%

profile of v8, /device:TPU:1, one launch (start us, length us, event | category | flops | bytes accessed | tf_op | source)
XLA Modules:
  0.0 208.6 jit_solution(17172546093324394125)
XLA Ops:
  6.6 0.7 all-gather.4.cloned.1.call-update
  7.3 1.9 copy.43
  9.2 1.2 fusion.31
  10.5 1.0 constant_dynamic-slice_fusion
  11.7 0.8 broadcast_in_dim.61
  12.5 4.8 %all-to-all-start = ((bf16[4,400,128]{2,1,0:T(8,128)(2,1)}), bf16[4,400,128]{2,1,0:T(8,128)(2,1)S(1)}, u32[]{:S(2)}, u32[]{:S(2)}) async-start(bf16[4,400,128]{2,1,0:T(8,128)(2,1)} %broadcast_in_dim.61), calls=%async_computation | async-start | bytes 819200 | tf_op jit(solution)/shard_map/all_to_all | solution.py:38
  17.4 7.4 %collective-permute-start = (bf16[1206,128]{1,0:T(8,128)(2,1)S(1)}, bf16[1206,128]{1,0:T(8,128)(2,1)}, u32[]{:S(2)}, u32[]{:S(2)}) collective-permute-start(bf16[1206,128]{1,0:T(8,128)(2,1)S(1)} %pad_maximum_fusion), channel_id=1, source_target_pairs={{0,256},{256,0},{1,257},{257,1},{2,258},{258,2},{3,259},{259,3},{4... | collective-permute-start | bytes 926216 | tf_op jit(solution)/shard_map/ppermute | solution.py:24
  24.9 0.6 copy.41
  25.5 1.6 copy.36
  27.1 0.7 fusion.32
  27.7 10.0 %all-to-all-start.1 = ((bf16[8,64,1024]{2,1,0:T(8,128)(2,1)}), bf16[8,64,1024]{2,1,0:T(8,128)(2,1)S(1)}, u32[]{:S(2)}, u32[]{:S(2)}) async-start(bf16[8,64,1024]{2,1,0:T(8,128)(2,1)} %copy.36), calls=%async_computation.1 | async-start | bytes 2097152 | tf_op jit(solution)/shard_map/all_to_all | solution.py:254
  37.9 1.0 fusion.33
  38.9 2.2 %fusion.34 = (f32[1536]{0:T(1024)S(1)}, f32[1536,1206]{0,1:T(8,128)S(1)}) fusion(bf16[1536,128]{1,0:T(8,128)(2,1)S(1)} %bitcast.47, bf16[603,128]{1,0:T(8,128)(2,1)S(1)} %get-tuple-element.51, bf16[603,128]{1,0:T(8,128)(2,1)} %get-tuple-element.49, s32[1536]{0:T(1024)S(1)} %get-tuple-element.40, s32[1206]{0:T(1024)S(1)} %add_select_fusion), kind=kOutput, calls=%fused_computation.62 | convolution fusion | flops 482244096 | bytes 8128728 | tf_op jit(solution)/shard_map/dot_general | solution.py:198
  41.1 1.1 fusion.1
  42.2 1.5 fusion.4
  43.8 0.8 dynamic-slice_bitcast_fusion.2
  44.5 3.4 %collective-permute-start.1 = (bf16[384,128]{1,0:T(8,128)(2,1)}, bf16[384,128]{1,0:T(8,128)(2,1)}, u32[]{:S(2)}, u32[]{:S(2)}) collective-permute-start(bf16[384,128]{1,0:T(8,128)(2,1)} %get-tuple-element.45), channel_id=1, source_target_pairs={{0,64},{64,128},{128,192},{192,0},{1,65},{65,129},{129,193},{193,1... | collective-permute-start | bytes 294920 | tf_op jit(solution)/shard_map/ppermute | solution.py:29
  47.9 4.3 %collective-permute-start.2 = (bf16[384,128]{1,0:T(8,128)(2,1)}, bf16[384,128]{1,0:T(8,128)(2,1)S(1)}, u32[]{:S(2)}, u32[]{:S(2)}) collective-permute-start(bf16[384,128]{1,0:T(8,128)(2,1)} %get-tuple-element.47), channel_id=1, source_target_pairs={{0,128},{64,192},{128,0},{192,64},{1,129},{65,193},{129,1},{193,65... | collective-permute-start | bytes 294920 | tf_op jit(solution)/shard_map/ppermute | solution.py:29
  52.2 3.1 %collective-permute-start.3 = (bf16[384,128]{1,0:T(8,128)(2,1)}, bf16[384,128]{1,0:T(8,128)(2,1)}, u32[]{:S(2)}, u32[]{:S(2)}) collective-permute-start(bf16[384,128]{1,0:T(8,128)(2,1)} %get-tuple-element.46), channel_id=1, source_target_pairs={{0,192},{64,0},{128,64},{192,128},{1,193},{65,1},{129,65},{193,129... | collective-permute-start | bytes 294920 | tf_op jit(solution)/shard_map/ppermute | solution.py:29
  55.3 2.2 %collective-permute-start.4 = (bf16[4096,128]{1,0:T(8,128)(2,1)S(1)}, bf16[4096,128]{1,0:T(8,128)(2,1)}, u32[]{:S(2)}, u32[]{:S(2)}) collective-permute-start(bf16[4096,128]{1,0:T(8,128)(2,1)S(1)} %get-tuple-element.33.own_up), channel_id=1, source_target_pairs={{0,64},{64,128},{128,192},{192,0},{1,65},{65,129},{129,193},{193,1... | collective-permute-start | bytes 3145736 | tf_op jit(solution)/shard_map/ppermute | solution.py:29
  57.5 4.3 %collective-permute-start.5 = (bf16[4096,128]{1,0:T(8,128)(2,1)S(1)}, bf16[4096,128]{1,0:T(8,128)(2,1)}, u32[]{:S(2)}, u32[]{:S(2)}) collective-permute-start(bf16[4096,128]{1,0:T(8,128)(2,1)S(1)} %get-tuple-element.33.own_up), channel_id=1, source_target_pairs={{0,192},{64,0},{128,64},{192,128},{1,193},{65,1},{129,65},{193,129... | collective-permute-start | bytes 3145736 | tf_op jit(solution)/shard_map/ppermute | solution.py:29
  61.8 0.6 copy-done.8
  62.5 1.1 fusion.18
  63.5 18.7 %all_gather.9 = bf16[384,1024]{1,0:T(8,128)(2,1)} all-gather(bf16[384,128]{1,0:T(8,128)(2,1)S(1)} %fusion.18), channel_id=1, replica_groups=mesh['yh'=2,'x'=4,'z'=8,'yl'=4,'core'=2] {'yl','core'}, dimensions={1}, use_global_device_ids=true | all-gather | bytes 884736 | tf_op jit(solution)/shard_map/all_gather | solution.py:277
  82.3 1.7 fusion.6
  84.1 0.9 copy.37
  85.0 9.9 %all-to-all-start.2 = ((bf16[8,64,384]{2,1,0:T(8,128)(2,1)}), bf16[8,64,384]{2,1,0:T(8,128)(2,1)S(1)}, u32[]{:S(2)}, u32[]{:S(2)}) async-start(bf16[8,64,384]{2,1,0:T(8,128)(2,1)} %bitcast.14), calls=%async_computation.2 | async-start | bytes 786432 | tf_op jit(solution)/shard_map/all_to_all | solution.py:282
  94.9 0.1 copy.38
  95.1 0.1 eq.40
  95.2 0.4 fusion.8
  95.6 0.2 convert_element_type.70
  95.9 0.1 copy.40.gate
  96.0 14.1 %all-to-all-done.2.parts = bf16[8,64,384]{2,1,0:T(8,128)(2,1)S(1)} async-done(((bf16[8,64,384]{2,1,0:T(8,128)(2,1)}), bf16[8,64,384]{2,1,0:T(8,128)(2,1)S(1)}, u32[]{:S(2)}, u32[]{:S(2)}) %all-to-all-start.2) | async-done | bytes 393248 | tf_op jit(solution)/shard_map/all_to_all | solution.py:282
  110.1 2.1 shard_map.136
  112.2 8.9 %all-to-all-start.3 = ((bf16[128,18,128]{2,1,0:T(8,128)(2,1)}), bf16[128,18,128]{2,1,0:T(8,128)(2,1)S(1)}, u32[]{:S(2)}, u32[]{:S(2)}) async-start(bf16[128,18,128]{2,1,0:T(8,128)(2,1)} %get-tuple-element.34), calls=%async_computation.3 | async-start | bytes 1572864 | tf_op jit(solution)/shard_map/all_to_all | solution.py:296
  121.0 1.9 slice.53
  122.9 1.9 collective-permute-start.6
  124.8 1.9 slice.54
  126.7 4.6 %collective-permute-start.7 = (bf16[2048,128]{1,0:T(8,128)(2,1)}, bf16[2048,128]{1,0:T(8,128)(2,1)}, u32[]{:S(2)}, u32[]{:S(2)}) collective-permute-start(bf16[2048,128]{1,0:T(8,128)(2,1)} %slice.54), channel_id=1, source_target_pairs={{0,192},{64,0},{128,64},{192,128},{1,193},{65,1},{129,65},{193,129... | collective-permute-start | bytes 1572872 | tf_op jit(solution)/shard_map/ppermute | solution.py:29
  131.3 15.0 %all-to-all-done.3.came = bf16[128,18,128]{2,1,0:T(8,128)(2,1)S(1)} async-done(((bf16[128,18,128]{2,1,0:T(8,128)(2,1)}), bf16[128,18,128]{2,1,0:T(8,128)(2,1)S(1)}, u32[]{:S(2)}, u32[]{:S(2)}) %all-to-all-start.3) | async-done | bytes 589856 | tf_op jit(solution)/shard_map/all_to_all | solution.py:296
  146.3 0.6 shard_map.137.normed
  146.8 1.2 all-gather.6.cloned.1.call-done
  148.0 1.6 collective-permute-done.6.far_low
  149.6 2.2 %copy-done = bf16[4,128,4096]{2,1,0:T(8,128)(2,1)S(1)} copy-done((bf16[4,128,4096]{2,1,0:T(8,128)(2,1)S(1)}, bf16[4,128,4096]{2,1,0:T(8,128)(2,1)}, u32[]{:S(2)}) %copy-start) | copy-done | bytes 4194328
  151.8 2.2 %copy-done.1 = bf16[16384,1,128]{2,0,1:T(8,128)(2,1)S(1)} copy-done((bf16[16384,1,128]{2,0,1:T(8,128)(2,1)S(1)}, bf16[16384,1,128]{2,0,1:T(8,128)(2,1)}, u32[]{:S(2)}) %copy-start.1) | copy-done | bytes 4194328
  154.0 6.4 %shard_map.138 = bf16[128,18,128]{2,1,0:T(8,128)(2,1)S(1)} custom-call(s32[1]{0:T(128)} %bitcast.place, bf16[96,4096]{1,0:T(8,128)(2,1)S(1)} %shard_map.137.normed, bf16[4096,128]{1,0:T(8,128)(2,1)S(1)} %get-tuple-element.33.own_up, bf16[4096,128]{1,0:T(8,128)(2,1)} %collective-permute-done.4.left_up, bf16[4096,128]{1,0:T(8,128)(2,1)} %collective-permute-done.5.right_up, ...), custom_call_target="tpu_custom_call" | custom-call | tf_op jit(solution)/shard_map/pallas_call | solution.py:305
  160.4 39.5 %all_to_all.25.back = bf16[128,18,128]{2,1,0:T(8,128)(2,1)S(1)} all-to-all(bf16[128,18,128]{2,1,0:T(8,128)(2,1)S(1)} %shard_map.138), channel_id=1, replica_groups=mesh['yh'=2,'x'=4,'z'=8,'yl'=4,'core'=2] {'yh','z','yl','core'}, dimensions={0} | all-to-all | bytes 1179648 | tf_op jit(solution)/shard_map/all_to_all | solution.py:319
  199.9 1.8 shard_map.139
  (51 shorter events, 0.6 us)
Async XLA Ops:
  6.5 3.9 %copy-start.10 = (s32[384]{0:T(512)S(1)}, s32[384]{0:T(512)}, u32[]{:S(2)}) copy-start(s32[384]{0:T(512)} %param.20) | copy-start | bytes 4612
  6.5 3.9 %copy-start.12 = (s32[24]{0:T(128)S(1)}, s32[24]{0:T(128)}, u32[]{:S(2)}) copy-start(s32[24]{0:T(128)} %param.21) | copy-start | bytes 292
  6.5 5.1 %copy-start.7 = (bf16[384,128]{1,0:T(8,128)(2,1)S(1)}, bf16[384,128]{1,0:T(8,128)(2,1)}, u32[]{:S(2)}) copy-start(bf16[384,128]{1,0:T(8,128)(2,1)} %param.17) | copy-start | bytes 294916
  6.5 18.3 %copy-start.6 = (bf16[8192,64]{0,1:T(8,128)(2,1)S(1)}, bf16[8192,64]{0,1:T(8,128)(2,1)}, u32[]{:S(2)}) copy-start(bf16[8192,64]{0,1:T(8,128)(2,1)} %param.23) | copy-start | bytes 3145732
  6.5 77.5 %all-gather.4.cloned.1.call-start = ((), (), s32[]{:S(2)}) async-start(), calls=%async_computation.5 | async-start | bytes 5242880 | tf_op jit(solution)/shard_map/all_gather | solution.py:247
  7.3 140.8 %all-gather.6.cloned.1.call-start = ((), (), s32[]{:S(2)}) async-start(), calls=%async_computation.6 | async-start | bytes 5242880 | tf_op jit(solution)/shard_map/all_gather | solution.py:252
  12.5 15.2 %all-to-all-start = ((bf16[4,400,128]{2,1,0:T(8,128)(2,1)}), bf16[4,400,128]{2,1,0:T(8,128)(2,1)S(1)}, u32[]{:S(2)}, u32[]{:S(2)}) async-start(bf16[4,400,128]{2,1,0:T(8,128)(2,1)} %broadcast_in_dim.61), calls=%async_computation | async-start | bytes 819200 | tf_op jit(solution)/shard_map/all_to_all | solution.py:38
  17.4 20.5 %collective-permute-start = (bf16[1206,128]{1,0:T(8,128)(2,1)S(1)}, bf16[1206,128]{1,0:T(8,128)(2,1)}, u32[]{:S(2)}, u32[]{:S(2)}) collective-permute-start(bf16[1206,128]{1,0:T(8,128)(2,1)S(1)} %pad_maximum_fusion), channel_id=1, source_target_pairs={{0,256},{256,0},{1,257},{257,1},{2,258},{258,2},{3,259},{259,3},{4... | collective-permute-start | bytes 926216 | tf_op jit(solution)/shard_map/ppermute | solution.py:24
  27.7 54.5 %all-to-all-start.1 = ((bf16[8,64,1024]{2,1,0:T(8,128)(2,1)}), bf16[8,64,1024]{2,1,0:T(8,128)(2,1)S(1)}, u32[]{:S(2)}, u32[]{:S(2)}) async-start(bf16[8,64,1024]{2,1,0:T(8,128)(2,1)} %copy.36), calls=%async_computation.1 | async-start | bytes 2097152 | tf_op jit(solution)/shard_map/all_to_all | solution.py:254
  42.2 52.7 %copy-start.9 = (s32[384,2]{0,1:T(2,128)S(1)}, s32[384,2]{0,1:T(2,128)}, u32[]{:S(2)}) copy-start(s32[384,2]{0,1:T(2,128)} %param.25) | copy-start | bytes 9220
  43.7 52.2 %copy-start.11 = (f32[64]{0:T(128)S(1)}, f32[64]{0:T(128)}, u32[]{:S(2)}) copy-start(f32[64]{0:T(128)} %param.22) | copy-start | bytes 772
  43.7 66.3 %copy-start.2 = (s32[1536,1]{1,0:T(8,128)S(1)}, s32[1536,1]{1,0:T(8,128)}, u32[]{:S(2)}) copy-start(s32[1536,1]{1,0:T(8,128)} %constant.110.clone.rows) | copy-start | bytes 18436
  43.7 66.3 %copy-start.3 = (bf16[384,64]{0,1:T(8,128)(2,1)S(1)}, bf16[384,64]{0,1:T(8,128)(2,1)}, u32[]{:S(2)}) copy-start(bf16[384,64]{0,1:T(8,128)(2,1)} %param.16) | copy-start | bytes 147460
  43.8 102.5 %copy-start.4 = (f32[4096]{0:T(1024)S(1)}, f32[4096]{0:T(1024)}, u32[]{:S(2)}) copy-start(f32[4096]{0:T(1024)} %param.24) | copy-start | bytes 49156
  44.5 10.8 %collective-permute-start.1 = (bf16[384,128]{1,0:T(8,128)(2,1)}, bf16[384,128]{1,0:T(8,128)(2,1)}, u32[]{:S(2)}, u32[]{:S(2)}) collective-permute-start(bf16[384,128]{1,0:T(8,128)(2,1)} %get-tuple-element.45), channel_id=1, source_target_pairs={{0,64},{64,128},{128,192},{192,0},{1,65},{65,129},{129,193},{193,1... | collective-permute-start | bytes 294920 | tf_op jit(solution)/shard_map/ppermute | solution.py:29
  47.9 13.9 %collective-permute-start.2 = (bf16[384,128]{1,0:T(8,128)(2,1)}, bf16[384,128]{1,0:T(8,128)(2,1)S(1)}, u32[]{:S(2)}, u32[]{:S(2)}) collective-permute-start(bf16[384,128]{1,0:T(8,128)(2,1)} %get-tuple-element.47), channel_id=1, source_target_pairs={{0,128},{64,192},{128,0},{192,64},{1,129},{65,193},{129,1},{193,65... | collective-permute-start | bytes 294920 | tf_op jit(solution)/shard_map/ppermute | solution.py:29
  52.2 10.3 %collective-permute-start.3 = (bf16[384,128]{1,0:T(8,128)(2,1)}, bf16[384,128]{1,0:T(8,128)(2,1)}, u32[]{:S(2)}, u32[]{:S(2)}) collective-permute-start(bf16[384,128]{1,0:T(8,128)(2,1)} %get-tuple-element.46), channel_id=1, source_target_pairs={{0,192},{64,0},{128,64},{192,128},{1,193},{65,1},{129,65},{193,129... | collective-permute-start | bytes 294920 | tf_op jit(solution)/shard_map/ppermute | solution.py:29
  55.3 56.9 %collective-permute-start.4 = (bf16[4096,128]{1,0:T(8,128)(2,1)S(1)}, bf16[4096,128]{1,0:T(8,128)(2,1)}, u32[]{:S(2)}, u32[]{:S(2)}) collective-permute-start(bf16[4096,128]{1,0:T(8,128)(2,1)S(1)} %get-tuple-element.33.own_up), channel_id=1, source_target_pairs={{0,64},{64,128},{128,192},{192,0},{1,65},{65,129},{129,193},{193,1... | collective-permute-start | bytes 3145736 | tf_op jit(solution)/shard_map/ppermute | solution.py:29
  57.5 54.7 %collective-permute-start.5 = (bf16[4096,128]{1,0:T(8,128)(2,1)S(1)}, bf16[4096,128]{1,0:T(8,128)(2,1)}, u32[]{:S(2)}, u32[]{:S(2)}) collective-permute-start(bf16[4096,128]{1,0:T(8,128)(2,1)S(1)} %get-tuple-element.33.own_up), channel_id=1, source_target_pairs={{0,192},{64,0},{128,64},{192,128},{1,193},{65,1},{129,65},{193,129... | collective-permute-start | bytes 3145736 | tf_op jit(solution)/shard_map/ppermute | solution.py:29
  61.8 0.7 copy-start.8
  85.0 25.1 %all-to-all-start.2 = ((bf16[8,64,384]{2,1,0:T(8,128)(2,1)}), bf16[8,64,384]{2,1,0:T(8,128)(2,1)S(1)}, u32[]{:S(2)}, u32[]{:S(2)}) async-start(bf16[8,64,384]{2,1,0:T(8,128)(2,1)} %bitcast.14), calls=%async_computation.2 | async-start | bytes 786432 | tf_op jit(solution)/shard_map/all_to_all | solution.py:282
  112.2 34.1 %all-to-all-start.3 = ((bf16[128,18,128]{2,1,0:T(8,128)(2,1)}), bf16[128,18,128]{2,1,0:T(8,128)(2,1)S(1)}, u32[]{:S(2)}, u32[]{:S(2)}) async-start(bf16[128,18,128]{2,1,0:T(8,128)(2,1)} %get-tuple-element.34), calls=%async_computation.3 | async-start | bytes 1572864 | tf_op jit(solution)/shard_map/all_to_all | solution.py:296
  122.9 26.7 %collective-permute-start.6 = (bf16[2048,128]{1,0:T(8,128)(2,1)}, bf16[2048,128]{1,0:T(8,128)(2,1)}, u32[]{:S(2)}, u32[]{:S(2)}) collective-permute-start(bf16[2048,128]{1,0:T(8,128)(2,1)} %slice.53), channel_id=1, source_target_pairs={{0,64},{64,128},{128,192},{192,0},{1,65},{65,129},{129,193},{193,1... | collective-permute-start | bytes 1572872 | tf_op jit(solution)/shard_map/ppermute | solution.py:29
  126.7 22.9 %collective-permute-start.7 = (bf16[2048,128]{1,0:T(8,128)(2,1)}, bf16[2048,128]{1,0:T(8,128)(2,1)}, u32[]{:S(2)}, u32[]{:S(2)}) collective-permute-start(bf16[2048,128]{1,0:T(8,128)(2,1)} %slice.54), channel_id=1, source_target_pairs={{0,192},{64,0},{128,64},{192,128},{1,193},{65,1},{129,65},{193,129... | collective-permute-start | bytes 1572872 | tf_op jit(solution)/shard_map/ppermute | solution.py:29
  149.6 2.2 %copy-start = (bf16[4,128,4096]{2,1,0:T(8,128)(2,1)S(1)}, bf16[4,128,4096]{2,1,0:T(8,128)(2,1)}, u32[]{:S(2)}) copy-start(bf16[4,128,4096]{2,1,0:T(8,128)(2,1)} %all-gather.4.cloned.1.call-done.downs_there) | copy-start | bytes 12582916
  151.8 2.2 %copy-start.1 = (bf16[16384,1,128]{2,0,1:T(8,128)(2,1)S(1)}, bf16[16384,1,128]{2,0,1:T(8,128)(2,1)}, u32[]{:S(2)}) copy-start(bf16[16384,1,128]{2,0,1:T(8,128)(2,1)} %all-gather.6.cloned.1.call-done) | copy-start | bytes 12582916
  154.0 45.9 %copy-start.5 = (s32[384,2]{0,1:T(2,128)S(1)}, s32[384,2]{0,1:T(2,128)}, u32[]{:S(2)}) copy-start(s32[384,2]{0,1:T(2,128)} %param.26) | copy-start | bytes 9220
Sparse Core Ops, SparseCore 0:
  9.5 73.3 all-gather.3
  85.0 62.9 all-gather.5

commit v9 on v8

--- a/solution.py
+++ b/solution.py
@@ -314,7 +314,7 @@
             pltpu.SemaphoreType.DMA((nx,)),
             pltpu.SemaphoreType.DMA((nx,)),
         ],
-        compiler_params=pltpu.CompilerParams(vmem_limit_bytes=40 * 1024 * 1024),
+        compiler_params=pltpu.CompilerParams(vmem_limit_bytes=48 * 1024 * 1024),
     )(x[None], normed, own_up, left_up, right_up, far_low, far_high, gate_all, down_all)
     back_sums = lax.all_to_all(dealt, BOTH, 0, 0, tiled=True)
     (out,) = local_kernel(

time: 210 us -> 206 us (0.981)
  local copies, waits for them, and re-layouts: 20 us -> 15.7 us
    unnamed x29 -> x25, local copies, waits for them, and re-layouts: 7.67 us -> 3.29 us
where the time goes in v9:
time: 206 us; the launch traced here: 205 us
  starting transfers between devices  64.9 us (32%)
  blocking collectives  58.2 us (28%)
  waiting for transfers between devices  32.5 us (16%)
  local copies, waits for them, and re-layouts  15.7 us (8%)
  between operations  13.8 us (7%)
  Pallas kernels  11.5 us (6%)
  matrix products  5.82 us (3%)
  other arithmetic  2.33 us (1%)
    all_to_all x1, blocking collectives, per_device(): back_sums = lax.all_to_all(dealt, BOTH, 0, 0, tiled=True)  39.5 us
    ppermute x7, starting transfers between devices, shift(): return lax.ppermute(v, axis, [(i, (i + by) % n) for i in range(n)])  23.7 us
    all_gather x1, blocking collectives, per_device(): heads = lax.all_gather(attended, NEAR, axis=1, tiled=True)  18.7 us
    all_to_all x1, waiting for transfers between devices, per_device(): came = lax.all_to_all(sent, BOTH, 0, 0, tiled=True)  15 us
    all_to_all x1, waiting for transfers between devices, per_device(): lax.all_to_all(partial.reshape(nz, feats, tokens), 'z', 0, 0, tiled=True)  14.1 us
    all_to_all x1, starting transfers between devices, per_device(): lax.all_to_all(turned, 'z', 0, 0, tiled=True)  10 us
    all_to_all x1, starting transfers between devices, per_device(): lax.all_to_all(partial.reshape(nz, feats, tokens), 'z', 0, 0, tiled=True)  9.95 us
    all_to_all x1, starting transfers between devices, per_device(): came = lax.all_to_all(sent, BOTH, 0, 0, tiled=True)  8.86 us
  transfers between devices with their start and end apart: 14, of which 4 were waited for; matrix products, arithmetic and copies ran while one was open for 11% of the time, Pallas kernels for 1%

profile of v9, /device:TPU:1, one launch (start us, length us, event | category | flops | bytes accessed | tf_op | source)
XLA Modules:
  0.0 204.8 jit_solution(1761163726669657107)
XLA Ops:
  6.6 0.7 all-gather.4.cloned.1.call-update
  7.3 1.9 copy.43
  9.2 1.2 fusion.31
  10.4 0.1 select_reduce_fusion
  10.5 1.0 constant_dynamic-slice_fusion
  11.7 0.8 broadcast_in_dim.61
  12.5 4.8 %all-to-all-start = ((bf16[4,400,128]{2,1,0:T(8,128)(2,1)}), bf16[4,400,128]{2,1,0:T(8,128)(2,1)S(1)}, u32[]{:S(2)}, u32[]{:S(2)}) async-start(bf16[4,400,128]{2,1,0:T(8,128)(2,1)} %broadcast_in_dim.61), calls=%async_computation | async-start | bytes 819200 | tf_op jit(solution)/shard_map/all_to_all | solution.py:38
  17.4 7.4 %collective-permute-start = (bf16[1206,128]{1,0:T(8,128)(2,1)S(1)}, bf16[1206,128]{1,0:T(8,128)(2,1)}, u32[]{:S(2)}, u32[]{:S(2)}) collective-permute-start(bf16[1206,128]{1,0:T(8,128)(2,1)S(1)} %pad_maximum_fusion), channel_id=1, source_target_pairs={{0,256},{256,0},{1,257},{257,1},{2,258},{258,2},{3,259},{259,3},{4... | collective-permute-start | bytes 926216 | tf_op jit(solution)/shard_map/ppermute | solution.py:24
  24.9 0.6 copy.41
  25.5 1.6 copy.36
  27.1 0.7 fusion.32
  27.8 10.0 %all-to-all-start.1 = ((bf16[8,64,1024]{2,1,0:T(8,128)(2,1)}), bf16[8,64,1024]{2,1,0:T(8,128)(2,1)S(1)}, u32[]{:S(2)}, u32[]{:S(2)}) async-start(bf16[8,64,1024]{2,1,0:T(8,128)(2,1)} %copy.36), calls=%async_computation.1 | async-start | bytes 2097152 | tf_op jit(solution)/shard_map/all_to_all | solution.py:254
  37.9 1.0 fusion.33
  39.0 2.2 %fusion.34 = (f32[1536]{0:T(1024)S(1)}, f32[1536,1206]{0,1:T(8,128)S(1)}) fusion(bf16[1536,128]{1,0:T(8,128)(2,1)S(1)} %bitcast.47, bf16[603,128]{1,0:T(8,128)(2,1)S(1)} %get-tuple-element.51, bf16[603,128]{1,0:T(8,128)(2,1)} %get-tuple-element.49, s32[1536]{0:T(1024)S(1)} %get-tuple-element.40, s32[1206]{0:T(1024)S(1)} %add_select_fusion), kind=kOutput, calls=%fused_computation.62 | convolution fusion | flops 482244096 | bytes 8128728 | tf_op jit(solution)/shard_map/dot_general | solution.py:198
  41.2 1.1 fusion.1
  42.2 1.5 fusion.4
  43.8 0.7 dynamic-slice_bitcast_fusion.2
  44.6 3.4 %collective-permute-start.1 = (bf16[384,128]{1,0:T(8,128)(2,1)}, bf16[384,128]{1,0:T(8,128)(2,1)}, u32[]{:S(2)}, u32[]{:S(2)}) collective-permute-start(bf16[384,128]{1,0:T(8,128)(2,1)} %get-tuple-element.45), channel_id=1, source_target_pairs={{0,64},{64,128},{128,192},{192,0},{1,65},{65,129},{129,193},{193,1... | collective-permute-start | bytes 294920 | tf_op jit(solution)/shard_map/ppermute | solution.py:29
  47.9 4.3 %collective-permute-start.2 = (bf16[384,128]{1,0:T(8,128)(2,1)}, bf16[384,128]{1,0:T(8,128)(2,1)S(1)}, u32[]{:S(2)}, u32[]{:S(2)}) collective-permute-start(bf16[384,128]{1,0:T(8,128)(2,1)} %get-tuple-element.47), channel_id=1, source_target_pairs={{0,128},{64,192},{128,0},{192,64},{1,129},{65,193},{129,1},{193,65... | collective-permute-start | bytes 294920 | tf_op jit(solution)/shard_map/ppermute | solution.py:29
  52.2 3.1 %collective-permute-start.3 = (bf16[384,128]{1,0:T(8,128)(2,1)}, bf16[384,128]{1,0:T(8,128)(2,1)}, u32[]{:S(2)}, u32[]{:S(2)}) collective-permute-start(bf16[384,128]{1,0:T(8,128)(2,1)} %get-tuple-element.46), channel_id=1, source_target_pairs={{0,192},{64,0},{128,64},{192,128},{1,193},{65,1},{129,65},{193,129... | collective-permute-start | bytes 294920 | tf_op jit(solution)/shard_map/ppermute | solution.py:29
  55.3 2.2 %collective-permute-start.4 = (bf16[4096,128]{1,0:T(8,128)(2,1)S(1)}, bf16[4096,128]{1,0:T(8,128)(2,1)}, u32[]{:S(2)}, u32[]{:S(2)}) collective-permute-start(bf16[4096,128]{1,0:T(8,128)(2,1)S(1)} %get-tuple-element.33.own_up), channel_id=1, source_target_pairs={{0,64},{64,128},{128,192},{192,0},{1,65},{65,129},{129,193},{193,1... | collective-permute-start | bytes 3145736 | tf_op jit(solution)/shard_map/ppermute | solution.py:29
  57.5 4.3 %collective-permute-start.5 = (bf16[4096,128]{1,0:T(8,128)(2,1)S(1)}, bf16[4096,128]{1,0:T(8,128)(2,1)}, u32[]{:S(2)}, u32[]{:S(2)}) collective-permute-start(bf16[4096,128]{1,0:T(8,128)(2,1)S(1)} %get-tuple-element.33.own_up), channel_id=1, source_target_pairs={{0,192},{64,0},{128,64},{192,128},{1,193},{65,1},{129,65},{193,129... | collective-permute-start | bytes 3145736 | tf_op jit(solution)/shard_map/ppermute | solution.py:29
  61.9 0.6 copy-done.6
  62.5 1.1 fusion.18
  63.6 18.7 %all_gather.9 = bf16[384,1024]{1,0:T(8,128)(2,1)} all-gather(bf16[384,128]{1,0:T(8,128)(2,1)S(1)} %fusion.18), channel_id=1, replica_groups=mesh['yh'=2,'x'=4,'z'=8,'yl'=4,'core'=2] {'yl','core'}, dimensions={1}, use_global_device_ids=true | all-gather | bytes 884736 | tf_op jit(solution)/shard_map/all_gather | solution.py:277
  82.3 1.7 fusion.6
  84.1 0.9 copy.37
  85.0 9.9 %all-to-all-start.2 = ((bf16[8,64,384]{2,1,0:T(8,128)(2,1)}), bf16[8,64,384]{2,1,0:T(8,128)(2,1)S(1)}, u32[]{:S(2)}, u32[]{:S(2)}) async-start(bf16[8,64,384]{2,1,0:T(8,128)(2,1)} %bitcast.14), calls=%async_computation.2 | async-start | bytes 786432 | tf_op jit(solution)/shard_map/all_to_all | solution.py:282
  94.9 0.1 copy.38
  95.1 0.1 eq.40
  95.2 0.4 fusion.8
  95.6 0.2 convert_element_type.70
  95.8 0.1 copy.39
  95.9 0.1 copy.40.gate
  96.0 14.1 %all-to-all-done.2.parts = bf16[8,64,384]{2,1,0:T(8,128)(2,1)S(1)} async-done(((bf16[8,64,384]{2,1,0:T(8,128)(2,1)}), bf16[8,64,384]{2,1,0:T(8,128)(2,1)S(1)}, u32[]{:S(2)}, u32[]{:S(2)}) %all-to-all-start.2) | async-done | bytes 393248 | tf_op jit(solution)/shard_map/all_to_all | solution.py:282
  110.1 2.1 %shard_map.136 = (bf16[64,384]{1,0:T(8,128)(2,1)S(1)}, bf16[128,18,128]{2,1,0:T(8,128)(2,1)}) custom-call(bf16[8,64,384]{2,1,0:T(8,128)(2,1)S(1)} %all-to-all-done.2.parts, bf16[64,384]{1,0:T(8,128)(2,1)S(1)} %bitcast.39, f32[64,1]{1,0:T(8,128)S(1)} %copy.40.gate, s32[2,384]{1,0:T(2,128)S(1)} %add_bitcast_fusion.slots, s32[1536,1]{1,0:T(8,128)S(1)} %copy-done), custom_call_target="tpu_custom_call" | custom-call | tf_op jit(solution)/shard_map/pallas_call | solution.py:288
  112.2 8.9 %all-to-all-start.3 = ((bf16[128,18,128]{2,1,0:T(8,128)(2,1)}), bf16[128,18,128]{2,1,0:T(8,128)(2,1)S(1)}, u32[]{:S(2)}, u32[]{:S(2)}) async-start(bf16[128,18,128]{2,1,0:T(8,128)(2,1)} %get-tuple-element.34), calls=%async_computation.3 | async-start | bytes 1572864 | tf_op jit(solution)/shard_map/all_to_all | solution.py:296
  121.1 1.9 slice.53
  123.0 1.9 collective-permute-start.6
  124.9 1.9 slice.54
  126.8 4.6 %collective-permute-start.7 = (bf16[2048,128]{1,0:T(8,128)(2,1)}, bf16[2048,128]{1,0:T(8,128)(2,1)}, u32[]{:S(2)}, u32[]{:S(2)}) collective-permute-start(bf16[2048,128]{1,0:T(8,128)(2,1)} %slice.54), channel_id=1, source_target_pairs={{0,192},{64,0},{128,64},{192,128},{1,193},{65,1},{129,65},{193,129... | collective-permute-start | bytes 1572872 | tf_op jit(solution)/shard_map/ppermute | solution.py:29
  131.3 15.0 %all-to-all-done.3.came = bf16[128,18,128]{2,1,0:T(8,128)(2,1)S(1)} async-done(((bf16[128,18,128]{2,1,0:T(8,128)(2,1)}), bf16[128,18,128]{2,1,0:T(8,128)(2,1)S(1)}, u32[]{:S(2)}, u32[]{:S(2)}) %all-to-all-start.3) | async-done | bytes 589856 | tf_op jit(solution)/shard_map/all_to_all | solution.py:296
  146.3 0.6 shard_map.137.normed
  146.9 1.1 all-gather.6.cloned.1.call-done
  148.0 1.7 collective-permute-done.6.far_low
  149.6 7.0 %shard_map.138 = bf16[128,18,128]{2,1,0:T(8,128)(2,1)S(1)} custom-call(s32[1]{0:T(128)} %bitcast.place, bf16[96,4096]{1,0:T(8,128)(2,1)S(1)} %shard_map.137.normed, bf16[4096,128]{1,0:T(8,128)(2,1)S(1)} %get-tuple-element.33.own_up, bf16[4096,128]{1,0:T(8,128)(2,1)} %collective-permute-done.4.left_up, bf16[4096,128]{1,0:T(8,128)(2,1)} %collective-permute-done.5.right_up, ...), custom_call_target="tpu_custom_call" | custom-call | tf_op jit(solution)/shard_map/pallas_call | solution.py:305
  156.7 39.5 %all_to_all.25.back = bf16[128,18,128]{2,1,0:T(8,128)(2,1)S(1)} all-to-all(bf16[128,18,128]{2,1,0:T(8,128)(2,1)S(1)} %shard_map.138), channel_id=1, replica_groups=mesh['yh'=2,'x'=4,'z'=8,'yl'=4,'core'=2] {'yh','z','yl','core'}, dimensions={0} | all-to-all | bytes 1179648 | tf_op jit(solution)/shard_map/all_to_all | solution.py:319
  196.1 1.8 shard_map.139
  (47 shorter events, 0.4 us)
Async XLA Ops:
  6.5 3.9 %copy-start.8 = (s32[384]{0:T(512)S(1)}, s32[384]{0:T(512)}, u32[]{:S(2)}) copy-start(s32[384]{0:T(512)} %param.20) | copy-start | bytes 4612
  6.5 3.9 %copy-start.10 = (s32[24]{0:T(128)S(1)}, s32[24]{0:T(128)}, u32[]{:S(2)}) copy-start(s32[24]{0:T(128)} %param.21) | copy-start | bytes 292
  6.5 5.1 %copy-start.5 = (bf16[384,128]{1,0:T(8,128)(2,1)S(1)}, bf16[384,128]{1,0:T(8,128)(2,1)}, u32[]{:S(2)}) copy-start(bf16[384,128]{1,0:T(8,128)(2,1)} %param.17) | copy-start | bytes 294916
  6.5 18.3 %copy-start.4 = (bf16[8192,64]{0,1:T(8,128)(2,1)S(1)}, bf16[8192,64]{0,1:T(8,128)(2,1)}, u32[]{:S(2)}) copy-start(bf16[8192,64]{0,1:T(8,128)(2,1)} %param.23) | copy-start | bytes 3145732
  6.5 77.5 %all-gather.4.cloned.1.call-start = ((), (), s32[]{:S(2)}) async-start(), calls=%async_computation.5 | async-start | bytes 5242880 | tf_op jit(solution)/shard_map/all_gather | solution.py:247
  7.3 140.7 %all-gather.6.cloned.1.call-start = ((), (), s32[]{:S(2)}) async-start(), calls=%async_computation.6 | async-start | bytes 5242880 | tf_op jit(solution)/shard_map/all_gather | solution.py:252
  12.5 15.2 %all-to-all-start = ((bf16[4,400,128]{2,1,0:T(8,128)(2,1)}), bf16[4,400,128]{2,1,0:T(8,128)(2,1)S(1)}, u32[]{:S(2)}, u32[]{:S(2)}) async-start(bf16[4,400,128]{2,1,0:T(8,128)(2,1)} %broadcast_in_dim.61), calls=%async_computation | async-start | bytes 819200 | tf_op jit(solution)/shard_map/all_to_all | solution.py:38
  17.4 20.5 %collective-permute-start = (bf16[1206,128]{1,0:T(8,128)(2,1)S(1)}, bf16[1206,128]{1,0:T(8,128)(2,1)}, u32[]{:S(2)}, u32[]{:S(2)}) collective-permute-start(bf16[1206,128]{1,0:T(8,128)(2,1)S(1)} %pad_maximum_fusion), channel_id=1, source_target_pairs={{0,256},{256,0},{1,257},{257,1},{2,258},{258,2},{3,259},{259,3},{4... | collective-permute-start | bytes 926216 | tf_op jit(solution)/shard_map/ppermute | solution.py:24
  27.8 54.5 %all-to-all-start.1 = ((bf16[8,64,1024]{2,1,0:T(8,128)(2,1)}), bf16[8,64,1024]{2,1,0:T(8,128)(2,1)S(1)}, u32[]{:S(2)}, u32[]{:S(2)}) async-start(bf16[8,64,1024]{2,1,0:T(8,128)(2,1)} %copy.36), calls=%async_computation.1 | async-start | bytes 2097152 | tf_op jit(solution)/shard_map/all_to_all | solution.py:254
  42.2 52.7 %copy-start.7 = (s32[384,2]{0,1:T(2,128)S(1)}, s32[384,2]{0,1:T(2,128)}, u32[]{:S(2)}) copy-start(s32[384,2]{0,1:T(2,128)} %param.25) | copy-start | bytes 9220
  43.8 52.1 %copy-start.9 = (f32[64]{0:T(128)S(1)}, f32[64]{0:T(128)}, u32[]{:S(2)}) copy-start(f32[64]{0:T(128)} %param.22) | copy-start | bytes 772
  43.8 66.3 %copy-start = (s32[1536,1]{1,0:T(8,128)S(1)}, s32[1536,1]{1,0:T(8,128)}, u32[]{:S(2)}) copy-start(s32[1536,1]{1,0:T(8,128)} %constant.110.clone.rows) | copy-start | bytes 18436
  43.8 66.3 %copy-start.1 = (bf16[384,64]{0,1:T(8,128)(2,1)S(1)}, bf16[384,64]{0,1:T(8,128)(2,1)}, u32[]{:S(2)}) copy-start(bf16[384,64]{0,1:T(8,128)(2,1)} %param.16) | copy-start | bytes 147460
  43.8 102.5 %copy-start.2 = (f32[4096]{0:T(1024)S(1)}, f32[4096]{0:T(1024)}, u32[]{:S(2)}) copy-start(f32[4096]{0:T(1024)} %param.24) | copy-start | bytes 49156
  44.6 10.8 %collective-permute-start.1 = (bf16[384,128]{1,0:T(8,128)(2,1)}, bf16[384,128]{1,0:T(8,128)(2,1)}, u32[]{:S(2)}, u32[]{:S(2)}) collective-permute-start(bf16[384,128]{1,0:T(8,128)(2,1)} %get-tuple-element.45), channel_id=1, source_target_pairs={{0,64},{64,128},{128,192},{192,0},{1,65},{65,129},{129,193},{193,1... | collective-permute-start | bytes 294920 | tf_op jit(solution)/shard_map/ppermute | solution.py:29
  47.9 13.9 %collective-permute-start.2 = (bf16[384,128]{1,0:T(8,128)(2,1)}, bf16[384,128]{1,0:T(8,128)(2,1)S(1)}, u32[]{:S(2)}, u32[]{:S(2)}) collective-permute-start(bf16[384,128]{1,0:T(8,128)(2,1)} %get-tuple-element.47), channel_id=1, source_target_pairs={{0,128},{64,192},{128,0},{192,64},{1,129},{65,193},{129,1},{193,65... | collective-permute-start | bytes 294920 | tf_op jit(solution)/shard_map/ppermute | solution.py:29
  52.2 10.3 %collective-permute-start.3 = (bf16[384,128]{1,0:T(8,128)(2,1)}, bf16[384,128]{1,0:T(8,128)(2,1)}, u32[]{:S(2)}, u32[]{:S(2)}) collective-permute-start(bf16[384,128]{1,0:T(8,128)(2,1)} %get-tuple-element.46), channel_id=1, source_target_pairs={{0,192},{64,0},{128,64},{192,128},{1,193},{65,1},{129,65},{193,129... | collective-permute-start | bytes 294920 | tf_op jit(solution)/shard_map/ppermute | solution.py:29
  55.3 56.9 %collective-permute-start.4 = (bf16[4096,128]{1,0:T(8,128)(2,1)S(1)}, bf16[4096,128]{1,0:T(8,128)(2,1)}, u32[]{:S(2)}, u32[]{:S(2)}) collective-permute-start(bf16[4096,128]{1,0:T(8,128)(2,1)S(1)} %get-tuple-element.33.own_up), channel_id=1, source_target_pairs={{0,64},{64,128},{128,192},{192,0},{1,65},{65,129},{129,193},{193,1... | collective-permute-start | bytes 3145736 | tf_op jit(solution)/shard_map/ppermute | solution.py:29
  57.5 54.7 %collective-permute-start.5 = (bf16[4096,128]{1,0:T(8,128)(2,1)S(1)}, bf16[4096,128]{1,0:T(8,128)(2,1)}, u32[]{:S(2)}, u32[]{:S(2)}) collective-permute-start(bf16[4096,128]{1,0:T(8,128)(2,1)S(1)} %get-tuple-element.33.own_up), channel_id=1, source_target_pairs={{0,192},{64,0},{128,64},{192,128},{1,193},{65,1},{129,65},{193,129... | collective-permute-start | bytes 3145736 | tf_op jit(solution)/shard_map/ppermute | solution.py:29
  61.8 0.7 copy-start.6
  85.0 25.1 %all-to-all-start.2 = ((bf16[8,64,384]{2,1,0:T(8,128)(2,1)}), bf16[8,64,384]{2,1,0:T(8,128)(2,1)S(1)}, u32[]{:S(2)}, u32[]{:S(2)}) async-start(bf16[8,64,384]{2,1,0:T(8,128)(2,1)} %bitcast.14), calls=%async_computation.2 | async-start | bytes 786432 | tf_op jit(solution)/shard_map/all_to_all | solution.py:282
  112.2 34.1 %all-to-all-start.3 = ((bf16[128,18,128]{2,1,0:T(8,128)(2,1)}), bf16[128,18,128]{2,1,0:T(8,128)(2,1)S(1)}, u32[]{:S(2)}, u32[]{:S(2)}) async-start(bf16[128,18,128]{2,1,0:T(8,128)(2,1)} %get-tuple-element.34), calls=%async_computation.3 | async-start | bytes 1572864 | tf_op jit(solution)/shard_map/all_to_all | solution.py:296
  123.0 26.7 %collective-permute-start.6 = (bf16[2048,128]{1,0:T(8,128)(2,1)}, bf16[2048,128]{1,0:T(8,128)(2,1)}, u32[]{:S(2)}, u32[]{:S(2)}) collective-permute-start(bf16[2048,128]{1,0:T(8,128)(2,1)} %slice.53), channel_id=1, source_target_pairs={{0,64},{64,128},{128,192},{192,0},{1,65},{65,129},{129,193},{193,1... | collective-permute-start | bytes 1572872 | tf_op jit(solution)/shard_map/ppermute | solution.py:29
  126.8 22.9 %collective-permute-start.7 = (bf16[2048,128]{1,0:T(8,128)(2,1)}, bf16[2048,128]{1,0:T(8,128)(2,1)}, u32[]{:S(2)}, u32[]{:S(2)}) collective-permute-start(bf16[2048,128]{1,0:T(8,128)(2,1)} %slice.54), channel_id=1, source_target_pairs={{0,192},{64,0},{128,64},{192,128},{1,193},{65,1},{129,65},{193,129... | collective-permute-start | bytes 1572872 | tf_op jit(solution)/shard_map/ppermute | solution.py:29
  149.6 46.5 %copy-start.3 = (s32[384,2]{0,1:T(2,128)S(1)}, s32[384,2]{0,1:T(2,128)}, u32[]{:S(2)}) copy-start(s32[384,2]{0,1:T(2,128)} %param.26) | copy-start | bytes 9220
Sparse Core Ops, SparseCore 0:
  9.5 73.3 all-gather.3
  85.0 62.9 all-gather.5
